TPU v7x, 512 devices: a whole 4x8x8 slice. The times are simulated.
512 devices in a mesh: section: 64 (over z_lo, y, core), tp: 8 (over x, z_hi).
Axes of the slice: x: 4, y: 8, z: 8 (z_hi: 2, z_lo: 4; z = z_hi * 4 + z_lo), core: 2. Of those that a mesh axis runs over, the one named last changes fastest.
Arguments:
- tokens: bfloat16 [2048, 6144], P('section', 'tp'), may hold values from -6 to 6
- norm_gain: float32 [6144], P('tp'), may hold values from 0.25 to 1.75
- router_weight: float32 [6144, 8], P('tp'), may hold values from -0.009765625 to 0.009765625
- routes: int32 [2048, 2], P('section'), may hold values from 0 to 7, all different within a row; in each aligned block of 32 rows (0 to 31, 32 to 63, ...) at most 12 rows name the same one
- w_gate: bfloat16 [6144, 65536], P(None, ('section', 'tp')), may hold values from -0.078125 to 0.078125
- w_up: bfloat16 [6144, 65536], P(None, ('section', 'tp')), may hold values from -0.078125 to 0.078125
- w_down: bfloat16 [65536, 6144], P('section', 'tp'), may hold values from -0.09375 to 0.09375
Outputs:
- mixed: bfloat16 [2048, 6144], P('section', 'tp')
Inputs may be any that keep to these rules, and one draw needn't show every extreme that they name: `routes`: in each aligned block of 32 rows (the rows of one index of section) the two ids of a row differ, and no expert is named by more than 12 rows; some expert is named by exactly 12 rows in some block.
All inputs are finite; a program needn't handle non-finite values.
Results may differ from a plain program's by a relative error of at most 0.015.
Values may be sent and summed in bfloat16 or wider, within the bound.
No kernel may reach another device: no remote copies, remote signals or barrier semaphores. Data moves between devices by JAX's collectives and lax.ppermute only.
A program may use at most 128 MiB of HBM per device.

v0:
```python
import jax
import jax.numpy as jnp
from jax import lax
from jax.sharding import PartitionSpec as P

D = 6144
TOP = 2
CAP = 12


epsilon = 1e-05


def placement_matrix(block_routes, experts, capacity):
    flat_ids = block_routes.reshape(-1)
    onehot = (flat_ids[:, None] == jnp.arange(experts, dtype=jnp.int32)[None, :]).astype(jnp.int32)
    ranking = jnp.sum((jnp.cumsum(onehot, 0) - onehot) * onehot, 1)
    position = flat_ids * capacity + ranking
    return position[None, :] == jnp.arange(experts * capacity, dtype=jnp.int32)[:, None]


def route_probs(logits, routes, experts):
    onehot = (routes[:, :, None] == jnp.arange(experts, dtype=jnp.int32)[None, None, :]).astype(
        jnp.float32
    )
    chosen = jnp.sum(onehot * logits[:, None, :], -1)
    first = jax.nn.sigmoid(chosen[:, 0] - chosen[:, 1])
    second = jax.nn.sigmoid(chosen[:, 1] - chosen[:, 0])
    return jnp.stack([first, second], 1)


def pack_rows(selector, normed, sections, experts):
    doubled = jnp.repeat(normed, TOP, axis=0)
    buffer = jnp.dot(
        selector.astype(jnp.bfloat16), doubled, preferred_element_type=jnp.float32
    ).astype(jnp.bfloat16)
    slices = sections // experts
    width = normed.shape[1]
    spread = jnp.broadcast_to(buffer.reshape(experts, 1, CAP, width), (experts, slices, CAP, width))
    return spread.reshape(sections, CAP, width)


def shards(tokens, norm_gain, router_weight, routes, w_gate, w_up, w_down):
    sections = lax.axis_size("section")
    experts = router_weight.shape[1]
    values = tokens.astype(jnp.float32)
    selector = placement_matrix(routes, experts, CAP)
    scaled = values * norm_gain[None, :]
    square_part = jnp.sum(values * values, -1)
    router_part = jnp.dot(scaled, router_weight, precision=lax.Precision.HIGHEST)
    square_sum, router_sum = lax.psum((square_part, router_part), "tp")
    inverse = lax.rsqrt(square_sum / D + epsilon)
    normed = (scaled * inverse[:, None]).astype(jnp.bfloat16)
    logits = router_sum * inverse[:, None]
    outgoing = pack_rows(selector, normed, sections, experts)
    arrived = lax.all_to_all(outgoing, "section", split_axis=0, concat_axis=0, tiled=True)
    expert_rows = arrived.reshape(sections * CAP, arrived.shape[2])
    piece = lax.all_gather(expert_rows, "tp", axis=1, tiled=True)
    gate = jnp.dot(piece, w_gate, preferred_element_type=jnp.float32)
    upward = jnp.dot(piece, w_up, preferred_element_type=jnp.float32)
    probs = route_probs(logits, routes, experts)
    hidden = (jax.nn.silu(gate) * upward).astype(jnp.bfloat16)
    partial_out = jnp.dot(
        lax.all_gather(hidden, "tp", axis=1, tiled=True), w_down, preferred_element_type=jnp.float32
    )
    width = partial_out.shape[1]
    returned = lax.all_to_all(
        partial_out.reshape(sections, CAP, width).astype(jnp.bfloat16),
        "section",
        split_axis=0,
        concat_axis=0,
        tiled=True,
    ).astype(jnp.float32)
    expert_out = (
        returned.reshape(experts, sections // experts, CAP, width)
        .sum(1)
        .reshape(experts * CAP, width)
    )
    weights = (
        (selector.astype(jnp.float32).T * probs.reshape(-1)[:, None])
        .reshape(tokens.shape[0], TOP, experts * CAP)
        .sum(1)
    )
    combined = jnp.dot(weights, expert_out, precision=lax.Precision.HIGHEST)
    return (values + combined).astype(jnp.bfloat16)


def solution(mesh):
    placed = (
        P("section", "tp"),
        P("tp"),
        P("tp", None),
        P("section", None),
        P(None, ("section", "tp")),
        P(None, ("section", "tp")),
        P("section", "tp"),
    )
    return jax.shard_map(
        shards, mesh=mesh, in_specs=placed, out_specs=P("section", "tp"), check_vma=False
    )
```

profile of v0, /device:TPU:6, one launch (start us, length us, event | category | flops | bytes accessed | tf_op | source)
XLA Modules:
  0.0 426.0 jit_solution(7852494220117642602)
XLA Ops:
  6.5 0.9 copy.28
  7.4 0.1 eq.49
  7.6 0.1 reduce_window_sum.11
  7.7 0.2 select_reduce_fusion.1
  7.9 0.9 fusion.5
  8.8 1.0 fusion.3
  9.8 32.2 %all-reduce = (f32[32,8]{0,1:T(8,128)S(1)}, f32[32]{0:T(128)S(1)}) all-reduce(f32[32,8]{0,1:T(8,128)S(1)} %fusion.3, f32[32]{0:T(128)S(1)} %fusion.5), channel_id=1, replica_groups=mesh['section'=64,'tp'=8] {'tp'}, use_global_device_ids=true, to_apply=%region_2.3 | all-reduce | flops 288 | bytes 2304 | tf_op jit(solution)/shard_map/psum | solution.py:51
  42.0 0.9 fusion.4
  43.0 0.2 convolution_convert_fusion.1
  43.2 0.1 broadcast_in_dim.8
  43.3 49.7 %all_to_all.10 = bf16[64,12,768]{2,1,0:T(8,128)(2,1)S(1)} all-to-all(bf16[64,12,768]{2,1,0:T(8,128)(2,1)S(1)} %bitcast.14), channel_id=1, replica_groups=mesh['section'=64,'tp'=8] {'section'}, dimensions={0} | all-to-all | bytes 2359296 | tf_op jit(solution)/shard_map/all_to_all | solution.py:56
  93.0 1.1 reshape.54
  94.2 189.3 %all-gather.3.cloned.1.call-done = bf16[768,6144]{1,0:T(8,128)(2,1)} async-done(((bf16[768,768]{1,0:T(8,128)(2,1)}), bf16[768,6144]{1,0:T(8,128)(2,1)}) %all-gather.3.cloned.1.call-update) | async-done | bytes 9437200 | tf_op jit(solution)/shard_map/all_gather | solution.py:58
  283.5 6.1 %fusion.9 = f32[768,128]{1,0:T(8,128)S(1)} fusion(bf16[768,6144]{1,0:T(8,128)(2,1)} %all-gather.3.cloned.1.call-done, bf16[6144,128]{1,0:T(8,128)(2,1)} %param.11), kind=kOutput, calls=%fused_computation.30 | convolution fusion | flops 1207959552 | bytes 11403264 | tf_op jit(solution)/shard_map/dot_general | solution.py:59
  289.6 0.8 copy-done.2
  290.4 3.3 fusion
  293.7 71.8 %all-gather.5.cloned.1.call-done = bf16[768,1024]{1,0:T(8,128)(2,1)} async-done(((bf16[768,128]{1,0:T(8,128)(2,1)}), bf16[768,1024]{1,0:T(8,128)(2,1)}) %all-gather.5.cloned.1.call-update) | async-done | bytes 1572880 | tf_op jit(solution)/shard_map/all_gather | solution.py:64
  365.5 2.8 convolution_convert_fusion
  368.3 1.3 convert_element_type.36
  369.6 8.6 %all-to-all-start.1 = ((bf16[64,12,768]{2,1,0:T(8,128)(2,1)}), bf16[64,12,768]{2,1,0:T(8,128)(2,1)S(1)}, u32[]{:S(2)}, u32[]{:S(2)}) async-start(bf16[64,12,768]{2,1,0:T(8,128)(2,1)} %convert_element_type.36), calls=%async_computation.1 | async-start | bytes 3145728 | tf_op jit(solution)/shard_map/all_to_all | solution.py:67
  378.1 0.1 reduce_sum.48
  378.5 38.6 %all-to-all-done.1 = bf16[64,12,768]{2,1,0:T(8,128)(2,1)S(1)} async-done(((bf16[64,12,768]{2,1,0:T(8,128)(2,1)}), bf16[64,12,768]{2,1,0:T(8,128)(2,1)S(1)}, u32[]{:S(2)}, u32[]{:S(2)}) %all-to-all-start.1) | async-done | bytes 1179680 | tf_op jit(solution)/shard_map/all_to_all | solution.py:67
  417.1 0.3 convert_reduce_fusion
  417.4 1.7 fusion.1
  (25 shorter events, 0.6 us)
Async XLA Ops:
  6.5 358.9 %copy-start = (bf16[1024,768]{1,0:T(8,128)(2,1)S(1)}, bf16[1024,768]{1,0:T(8,128)(2,1)}, u32[]{:S(2)}) copy-start(bf16[1024,768]{1,0:T(8,128)(2,1)} %param.13) | copy-start | bytes 4718596
  6.5 277.0 %all-gather.3.cloned.1.call-start = ((), (), s32[]{:S(2)}) async-start(), calls=%async_computation.2 | async-start | bytes 10616832 | tf_op jit(solution)/shard_map/all_gather | solution.py:58
  94.2 195.4 %copy-start.3 = (bf16[6144,128]{1,0:T(8,128)(2,1)S(1)}, bf16[6144,128]{1,0:T(8,128)(2,1)}, u32[]{:S(2)}) copy-start(bf16[6144,128]{1,0:T(8,128)(2,1)} %param.12) | copy-start | bytes 4718596
  94.2 271.3 %all-gather.5.cloned.1.call-start = ((), (), s32[]{:S(2)}) async-start(), calls=%async_computation.3 | async-start | bytes 1769472 | tf_op jit(solution)/shard_map/all_gather | solution.py:64
  283.5 6.9 %copy-start.2 = (bf16[768,6144]{1,0:T(8,128)(2,1)S(1)}, bf16[768,6144]{1,0:T(8,128)(2,1)}, u32[]{:S(2)}) copy-start(bf16[768,6144]{1,0:T(8,128)(2,1)} %all-gather.3.cloned.1.call-done) | copy-start | bytes 28311556
  369.6 8.7 %copy-start.1 = (s32[32,2]{0,1:T(2,128)S(1)}, s32[32,2]{0,1:T(2,128)}, u32[]{:S(2)}) copy-start(s32[32,2]{0,1:T(2,128)} %param.10) | copy-start | bytes 772
  369.6 47.5 %all-to-all-start.1 = ((bf16[64,12,768]{2,1,0:T(8,128)(2,1)}), bf16[64,12,768]{2,1,0:T(8,128)(2,1)S(1)}, u32[]{:S(2)}, u32[]{:S(2)}) async-start(bf16[64,12,768]{2,1,0:T(8,128)(2,1)} %convert_element_type.36), calls=%async_computation.1 | async-start | bytes 3145728 | tf_op jit(solution)/shard_map/all_to_all | solution.py:67
Sparse Core Ops, SparseCore 0:
  94.3 189.1 all-gather.2
  293.8 71.5 all-gather.4
where the time goes:
time: 429 us; the launch traced here: 426 us
  waiting for transfers between devices  300 us (70%)
  blocking collectives  81.9 us (19%)
  matrix products  15 us (3%)
  between operations  13.6 us (3%)
  starting transfers between devices  8.6 us (2%)
  local copies, waits for them, and re-layouts  4.69 us (1%)
    all_gather x1, waiting for transfers between devices, shards(): piece = lax.all_gather(expert_rows, 'tp', axis=1, tiled=True)  189 us
    all_gather x1, waiting for transfers between devices, shards(): lax.all_gather(hidden, 'tp', axis=1, tiled=True)  71.8 us
    all_to_all x1, blocking collectives, shards(): lax.all_to_all(outgoing, 'section', split_axis=0, concat_axis=0, tiled=True)  49.7 us
    all_to_all x1, waiting for transfers between devices, shards(): lax.all_to_all(partial_out.reshape(sections, CAP, width).astype(jnp.bfloa...  38.6 us
    psum x1, blocking collectives, shards(): square_sum, router_sum = lax.psum((square_part, router_part), 'tp')  32.2 us
  transfers between devices with their start and end apart: 3, of which 3 were waited for; matrix products, arithmetic and copies ran while one was open for 0% of the time, Pallas kernels for 0%

commit v1 on v0

v1 whole, which is shorter than its diff:
```python
import jax
import jax.numpy as jnp
from jax import lax
from jax.sharding import Mesh, PartitionSpec as P

D = 6144
TOP = 2
CAP = 12
HALVES = 2

epsilon = 1e-05

NAMES = ("zlo", "yh", "yl", "core", "x", "zhi")
SIZES = (4, 2, 4, 2, 4, 2)
HOMES = ("zlo", "yh", "yl")
DISPATCH = ("zlo", "yh", "yl", "zhi")


def shift(value, axis, by):
    size = lax.axis_size(axis)
    return lax.ppermute(value, axis, [(i, (i + by) % size) for i in range(size)])


def slot_ids(block_routes, experts):
    flat_ids = block_routes.reshape(-1)
    onehot = (flat_ids[:, None] == jnp.arange(experts, dtype=jnp.int32)[None, :]).astype(jnp.int32)
    ranking = jnp.sum((jnp.cumsum(onehot, 0) - onehot) * onehot, 1)
    return flat_ids * CAP + ranking


def route_probs(logits, routes, experts):
    onehot = (routes[:, :, None] == jnp.arange(experts, dtype=jnp.int32)[None, None, :]).astype(
        jnp.float32
    )
    chosen = jnp.sum(onehot * logits[:, None, :], -1)
    first = jax.nn.sigmoid(chosen[:, 0] - chosen[:, 1])
    second = jax.nn.sigmoid(chosen[:, 1] - chosen[:, 0])
    return jnp.stack([first, second], 1)


def split_sum(values):
    high = values.astype(jnp.bfloat16)
    low = (values - high.astype(jnp.float32)).astype(jnp.bfloat16)
    return high, low


def shards(tokens, norm_gain, router_weight, routes, w_gate, w_up, w_down):
    experts = router_weight.shape[1]
    count, width = tokens.shape
    units = w_gate.shape[1]
    half = width // HALVES
    nx, nz = lax.axis_size("x"), lax.axis_size("zhi")
    x, zhi = lax.axis_index("x"), lax.axis_index("zhi")
    homes = lax.axis_size("zlo") * lax.axis_size("yh") * lax.axis_size("yl")
    rows_n = homes * CAP

    wcat = jnp.concatenate([w_gate, w_up], 1).reshape(nx, nz * width, 2 * units)

    def piece(k):
        return lax.dynamic_index_in_dim(wcat, (x + k) % nx, 0, keepdims=False)

    steps = (2, 1, 3)
    w_x = {k: shift(piece(k), "x", k) for k in steps}
    w_x[0] = piece(0)
    w_c = {k: shift(w_x[k], "core", 1) for k in (0, 1, 3, 2)}

    wd = w_down.reshape(nx, nz, units, width)
    wd_ord = jnp.concatenate(
        [
            lax.dynamic_index_in_dim(
                lax.dynamic_index_in_dim(wd, (x + nx - k) % nx, 0, keepdims=False),
                (zhi + dz) % nz, 0, keepdims=False,
            )
            for dz in range(nz)
            for k in range(nx)
        ],
        0,
    )
    wd_all = jnp.concatenate([wd_ord, shift(wd_ord, "core", 1)], 0)

    gain_other = shift(norm_gain, "zhi", 1)
    gains = jnp.where(
        zhi == 0,
        jnp.concatenate([norm_gain, gain_other]),
        jnp.concatenate([gain_other, norm_gain]),
    )

    position = slot_ids(routes, experts).reshape(count, TOP)
    slots = jnp.arange(experts * CAP, dtype=jnp.int32)
    picks = (position[:, :, None] == slots[None, None, :]).astype(jnp.float32)
    chosen = picks.sum(1)
    sel = chosen.T.reshape(experts, 1, CAP, 1, count)
    eye = jnp.eye(HALVES, dtype=jnp.float32).reshape(1, HALVES, 1, HALVES, 1)
    sel2 = (sel * eye).reshape(experts * HALVES * CAP, HALVES * count).astype(jnp.bfloat16)
    tok2 = jnp.concatenate([tokens[:, :half], tokens[:, half:]], 0)
    packed = jnp.dot(sel2, tok2, preferred_element_type=jnp.float32).astype(jnp.bfloat16)
    fan = lax.axis_size("yl") * nz
    outgoing = jnp.broadcast_to(
        packed.reshape(experts, 1, HALVES * CAP, half), (experts, fan, HALVES * CAP, half)
    ).reshape(experts * fan, HALVES * CAP, half)
    arrived = lax.all_to_all(outgoing, DISPATCH, 0, 0, tiled=True)
    raw = (
        arrived.reshape(homes, nz, HALVES, CAP, half)
        .transpose(0, 3, 1, 2, 4)
        .reshape(rows_n, nz * width)
        .astype(jnp.float32)
    )
    scaled_rows = (raw * gains[None, :]).astype(jnp.bfloat16)
    squares = jnp.sum(raw * raw, 1)
    sq_hi, sq_lo = split_sum(squares)
    cols = 2 * units
    tail = jnp.concatenate([sq_hi, sq_lo]).reshape(-1, cols)
    tail_n = tail.shape[0]
    tail = jnp.pad(tail, ((0, 16 - tail_n), (0, 0)))

    def partial(k):
        own = jnp.dot(scaled_rows, w_x[k], preferred_element_type=jnp.float32)
        other = jnp.dot(scaled_rows, w_c[k], preferred_element_type=jnp.float32)
        return jnp.concatenate([own.astype(jnp.bfloat16), other.astype(jnp.bfloat16), tail], 0)

    got = [shift(partial(k), "x", -k) for k in steps] + [partial(0)]
    total = sum(g.astype(jnp.float32) for g in got)
    tail_sum = total[2 * rows_n : 2 * rows_n + tail_n].reshape(2, rows_n)
    inverse = lax.rsqrt((tail_sum[0] + tail_sum[1]) / D + epsilon)
    both = total[: 2 * rows_n].reshape(2, rows_n, cols) * inverse[None, :, None]
    hidden = (jax.nn.silu(both[..., :units]) * both[..., units:]).astype(jnp.bfloat16)

    hid_other = shift(hidden, "zhi", 1)
    gathered = []
    for h in (hidden, hid_other):
        gathered += [h] + [shift(h, "x", k) for k in (1, 2, 3)]
    wide = jnp.concatenate([g[0] for g in gathered] + [g[1] for g in gathered], 1)
    part = jnp.dot(wide, wd_all, preferred_element_type=jnp.float32).astype(jnp.bfloat16)
    back = (
        part.reshape(homes, CAP, HALVES, half)
        .transpose(0, 2, 1, 3)
        .reshape(homes, HALVES * CAP, half)
    )
    returned = lax.all_to_all(back, HOMES, 0, 0, tiled=True).reshape(homes * HALVES * CAP, half)

    values = tokens.astype(jnp.float32)
    scaled = values * norm_gain[None, :]
    router_part = jnp.concatenate(
        [
            jnp.dot(scaled, router_weight, precision=lax.Precision.HIGHEST),
            jnp.sum(values * values, -1, keepdims=True),
        ],
        1,
    )
    summed = router_part + shift(router_part, "zhi", 1)
    for by in (1, 2):
        pairs = [(i, i ^ by) for i in range(nx)]
        summed = summed + lax.ppermute(summed, "x", pairs)
    logits = summed[:, :experts] * lax.rsqrt(summed[:, experts:] / D + epsilon)
    probs = route_probs(logits, routes, experts)
    weights = (picks * probs[:, :, None]).sum(1)
    spread = jnp.broadcast_to(
        weights.reshape(1, count, experts, 1, 1, CAP)
        * jnp.eye(HALVES, dtype=jnp.float32).reshape(HALVES, 1, 1, 1, HALVES, 1),
        (HALVES, count, experts, homes // experts, HALVES, CAP),
    ).reshape(HALVES * count, homes * HALVES * CAP)
    w_hi, w_lo = split_sum(spread)
    mixed = jnp.dot(w_hi, returned, preferred_element_type=jnp.float32) + jnp.dot(
        w_lo, returned, preferred_element_type=jnp.float32
    )
    combined = jnp.concatenate([mixed[:count], mixed[count:]], 1)
    return (values + combined).astype(jnp.bfloat16)


def solution(mesh):
    fine = Mesh(mesh.devices.reshape(SIZES), NAMES)
    section, tp = NAMES[:4], NAMES[4:]
    placed = (
        P(section, tp),
        P(tp),
        P(tp, None),
        P(section, None),
        P(None, section + tp),
        P(None, section + tp),
        P(section, tp),
    )
    return jax.shard_map(
        shards, mesh=fine, in_specs=placed, out_specs=P(section, tp), check_vma=False
    )
```

time: 429 us -> 239 us (0.56)
  waiting for transfers between devices: 300 us -> 62.9 us
  starting transfers between devices: 8.6 us -> 103 us
  blocking collectives: 81.9 us -> 0 us
  local copies, waits for them, and re-layouts: 4.69 us -> 39.9 us
  between operations: 13.6 us -> 0.87 us
  other arithmetic: 2.56 us -> 11.6 us
    all_gather x2 -> x0, waiting for transfers between devices: 261 us -> none  [the longest x1 189 us: shards(): piece = lax.all_gather(expert_rows, 'tp', axis=1, tiled=True)]
    ppermute x0 -> x22, starting transfers between devices: none -> 77.1 us  [the longest x20 70.3 us: shift(): lax.ppermute(value, axis, [(i, (i + by) % size) for i in range(size)])]
    all_to_all x1 -> x0, blocking collectives: 49.7 us -> none  [shards(): lax.all_to_all(outgoing, 'section', split_axis=0, concat_axis=0, tiled=True)]
    ppermute x0 -> x22, waiting for transfers between devices: none -> 45.9 us  [the longest x20 40.9 us: shift(): lax.ppermute(value, axis, [(i, (i + by) % size) for i in range(size)])]
    psum x1 -> x0, blocking collectives: 32.2 us -> none  [shards(): square_sum, router_sum = lax.psum((square_part, router_part), 'tp')]
    all_to_all x1 -> x2, waiting for transfers between devices: 38.6 us -> 17 us  [the longest x1 17 us: shards(): lax.all_to_all(back, HOMES, 0, 0, tiled=True)]
    all_to_all x1 -> x2, starting transfers between devices: 8.55 us -> 25.6 us  [the longest x1 13.7 us: shards(): arrived = lax.all_to_all(outgoing, DISPATCH, 0, 0, tiled=True)]
    convert_element_type x1 -> x10, local copies, waits for them, and re-layouts: 1.3 us -> 16.6 us  [the longest x4 12.5 us: shards(): raw = arrived.reshape(homes, nz, HALVES, CAP, half).transpose(0, 3, 1, 2,...]
  transfers between devices with their start and end apart: 3 -> 24, of which waited for: 3 -> 10; matrix products, arithmetic and copies ran while one was open for 0% -> 26% of each run, Pallas kernels for 0% -> 0%
where the time goes in v1:
time: 239 us; the launch traced here: 237 us
  starting transfers between devices  103 us (43%)
  waiting for transfers between devices  62.9 us (26%)
  local copies, waits for them, and re-layouts  39.9 us (17%)
  matrix products  18.8 us (8%)
  other arithmetic  11.6 us (5%)
    ppermute x20, starting transfers between devices, shift(): lax.ppermute(value, axis, [(i, (i + by) % size) for i in range(size)])  70.3 us
    ppermute x20, waiting for transfers between devices, shift(): lax.ppermute(value, axis, [(i, (i + by) % size) for i in range(size)])  40.9 us
    all_to_all x1, waiting for transfers between devices, shards(): lax.all_to_all(back, HOMES, 0, 0, tiled=True)  17 us
    all_to_all x1, starting transfers between devices, shards(): arrived = lax.all_to_all(outgoing, DISPATCH, 0, 0, tiled=True)  13.7 us
    unnamed x50, local copies, waits for them, and re-layouts  13.7 us
    convert_element_type x4, local copies, waits for them, and re-layouts, shards(): raw = arrived.reshape(homes, nz, HALVES, CAP, half).transpose(0, 3, 1, 2,...  12.5 us
    all_to_all x1, starting transfers between devices, shards(): lax.all_to_all(back, HOMES, 0, 0, tiled=True)  11.8 us
    dot_general x4, matrix products, partial(): own = jnp.dot(scaled_rows, w_x[k], preferred_element_type=jnp.float32)  7.43 us
  transfers between devices with their start and end apart: 24, of which 10 were waited for; matrix products, arithmetic and copies ran while one was open for 26% of the time, Pallas kernels for 0%

profile of v1, /device:TPU:6, one launch (start us, length us, event | category | flops | bytes accessed | tf_op | source)
XLA Modules:
  0.0 236.8 jit_solution(18084999506875144901)
XLA Ops:
  0.0 11.1 %collective-permute-start.3 = (f32[768]{0:T(1024)}, f32[768]{0:T(1024)S(1)}, u32[]{:S(2)}, u32[]{:S(2)}) collective-permute-start(f32[768]{0:T(1024)} %param.8), channel_id=1, source_target_pairs={{0,1},{1,0},{2,3},{3,2},{4,5},{5,4},{6,7},{7,6},{8,9},{9,8},{10,11... | collective-permute-start | bytes 9224 | tf_op jit(solution)/shard_map/ppermute | solution.py:21
  29.6 4.1 %collective-permute-start.2 = (f32[32,9]{0,1:T(8,128)S(1)}, f32[32,9]{0,1:T(8,128)S(1)}, u32[]{:S(2)}, u32[]{:S(2)}) collective-permute-start(f32[32,9]{0,1:T(8,128)S(1)} %add.208), channel_id=1, source_target_pairs={{0,4},{2,6},{4,0},{6,2},{1,5},{3,7},{5,1},{7,3},{8,12},{10,14},{12... | collective-permute-start | bytes 3464 | tf_op jit(solution)/shard_map/ppermute | solution.py:153
  38.6 13.7 %all-to-all-start = ((bf16[64,24,384]{2,1,0:T(8,128)(2,1)}), bf16[64,24,384]{2,1,0:T(8,128)(2,1)}, u32[]{:S(2)}, u32[]{:S(2)}) async-start(bf16[64,24,384]{2,1,0:T(8,128)(2,1)} %bitcast.4), calls=%async_computation | async-start | bytes 2359296 | tf_op jit(solution)/shard_map/all_to_all | solution.py:101
  59.8 3.4 %collective-permute-start.4 = (bf16[1536,256]{1,0:T(8,128)(2,1)}, bf16[1536,256]{1,0:T(8,128)(2,1)}, u32[]{:S(2)}, u32[]{:S(2)}) collective-permute-start(bf16[1536,256]{1,0:T(8,128)(2,1)} %get-tuple-element.12), channel_id=1, source_target_pairs={{0,4},{2,6},{4,0},{6,2},{1,5},{3,7},{5,1},{7,3},{8,12},{10,14},{12... | collective-permute-start | bytes 2359304 | tf_op jit(solution)/shard_map/ppermute | solution.py:21
  63.2 4.0 %collective-permute-start.7 = (bf16[1536,256]{1,0:T(8,128)(2,1)}, bf16[1536,256]{1,0:T(8,128)(2,1)}, u32[]{:S(2)}, u32[]{:S(2)}) collective-permute-start(bf16[1536,256]{1,0:T(8,128)(2,1)} %get-tuple-element.11), channel_id=1, source_target_pairs={{0,2},{2,4},{4,6},{6,0},{1,3},{3,5},{5,7},{7,1},{8,10},{10,12},{12... | collective-permute-start | bytes 2359304 | tf_op jit(solution)/shard_map/ppermute | solution.py:21
  76.1 8.0 %collective-permute-done.4 = bf16[1536,256]{1,0:T(8,128)(2,1)} collective-permute-done((bf16[1536,256]{1,0:T(8,128)(2,1)}, bf16[1536,256]{1,0:T(8,128)(2,1)}, u32[]{:S(2)}, u32[]{:S(2)}) %collective-permute-start.4) | collective-permute-done | bytes 786464 | tf_op jit(solution)/shard_map/ppermute | solution.py:21
  85.9 12.3 %collective-permute-done.7 = bf16[1536,256]{1,0:T(8,128)(2,1)} collective-permute-done((bf16[1536,256]{1,0:T(8,128)(2,1)}, bf16[1536,256]{1,0:T(8,128)(2,1)}, u32[]{:S(2)}, u32[]{:S(2)}) %collective-permute-start.7) | collective-permute-done | bytes 786464 | tf_op jit(solution)/shard_map/ppermute | solution.py:21
  111.5 3.2 %fusion = (bf16[32,12,2,2,384]{4,2,0,1,3:T(2,128)(2,1)}, f32[32,12]{0,1:T(8,128)S(1)}) fusion(f32[32,2,2,12,384]{4,1,0,3,2:T(2,128)S(1)} %reshape.170, f32[2,2,384]{2,0,1:T(2,128)S(1)} %copy.72), kind=kLoop, calls=%fused_computation.5 | loop fusion | flops 2358912 | bytes 3546624 | tf_op jit(solution)/shard_map/convert_element_type | solution.py:108
  114.7 3.3 %copy.70 = f32[32,12,2,2,384]{4,3,2,1,0:T(2,128)} copy(f32[32,12,2,2,384]{4,2,0,1,3:T(2,128)S(1)} %bitcast.144) | data formatting | bytes 4718592 | tf_op jit(solution)/shard_map/convert_element_type | solution.py:106
  118.0 3.2 %reshape.168 = f32[384,1536]{1,0:T(8,128)S(1)} reshape(f32[32,12,2,2,384]{4,3,2,1,0:T(2,128)} %copy.70) | data formatting | bytes 4718592 | tf_op jit(solution)/shard_map/convert_element_type | solution.py:106
  133.4 4.5 %collective-permute-start.12 = (bf16[784,256]{1,0:T(8,128)(2,1)}, bf16[784,256]{1,0:T(8,128)(2,1)}, u32[]{:S(2)}, u32[]{:S(2)}) collective-permute-start(bf16[784,256]{1,0:T(8,128)(2,1)} %get-tuple-element.25), channel_id=1, source_target_pairs={{0,2},{2,4},{4,6},{6,0},{1,3},{3,5},{5,7},{7,1},{8,10},{10,12},{12... | collective-permute-start | bytes 1204232 | tf_op jit(solution)/shard_map/ppermute | solution.py:21
  140.2 4.8 %collective-permute-start.6 = (bf16[784,256]{1,0:T(8,128)(2,1)}, bf16[784,256]{1,0:T(8,128)(2,1)}, u32[]{:S(2)}, u32[]{:S(2)}) collective-permute-start(bf16[784,256]{1,0:T(8,128)(2,1)} %get-tuple-element.23), channel_id=1, source_target_pairs={{0,4},{2,6},{4,0},{6,2},{1,5},{3,7},{5,1},{7,3},{8,12},{10,14},{12... | collective-permute-start | bytes 1204232 | tf_op jit(solution)/shard_map/ppermute | solution.py:21
  151.8 9.1 %collective-permute-done.9 = bf16[784,256]{1,0:T(8,128)(2,1)} collective-permute-done((bf16[784,256]{1,0:T(8,128)(2,1)}, bf16[784,256]{1,0:T(8,128)(2,1)}, u32[]{:S(2)}, u32[]{:S(2)}) %collective-permute-start.9) | collective-permute-done | bytes 401440 | tf_op jit(solution)/shard_map/ppermute | solution.py:21
  164.7 3.1 %collective-permute-start.15 = (bf16[2,384,128]{2,1,0:T(8,128)(2,1)S(1)}, bf16[2,384,128]{2,1,0:T(8,128)(2,1)S(1)}, u32[]{:S(2)}, u32[]{:S(2)}) collective-permute-start(bf16[2,384,128]{2,1,0:T(8,128)(2,1)S(1)} %fusion.6), channel_id=1, source_target_pairs={{0,4},{2,6},{4,0},{6,2},{1,5},{3,7},{5,1},{7,3},{8,12},{10,14},{12... | collective-permute-start | bytes 589832 | tf_op jit(solution)/shard_map/ppermute | solution.py:21
  167.8 3.3 %collective-permute-start.16 = (bf16[2,384,128]{2,1,0:T(8,128)(2,1)S(1)}, bf16[2,384,128]{2,1,0:T(8,128)(2,1)S(1)}, u32[]{:S(2)}, u32[]{:S(2)}) collective-permute-start(bf16[2,384,128]{2,1,0:T(8,128)(2,1)S(1)} %fusion.6), channel_id=1, source_target_pairs={{0,6},{2,0},{4,2},{6,4},{1,7},{3,1},{5,3},{7,5},{8,14},{10,8},{12,... | collective-permute-start | bytes 589832 | tf_op jit(solution)/shard_map/ppermute | solution.py:21
  171.1 7.3 %collective-permute-start.17 = (bf16[2,384,128]{2,1,0:T(8,128)(2,1)S(1)}, bf16[2,384,128]{2,1,0:T(8,128)(2,1)S(1)}, u32[]{:S(2)}, u32[]{:S(2)}) collective-permute-start(bf16[2,384,128]{2,1,0:T(8,128)(2,1)S(1)} %fusion.6), channel_id=1, source_target_pairs={{0,1},{1,0},{2,3},{3,2},{4,5},{5,4},{6,7},{7,6},{8,9},{9,8},{10,11... | collective-permute-start | bytes 589832 | tf_op jit(solution)/shard_map/ppermute | solution.py:21
  178.5 6.0 %collective-permute-done.17 = bf16[2,384,128]{2,1,0:T(8,128)(2,1)S(1)} collective-permute-done((bf16[2,384,128]{2,1,0:T(8,128)(2,1)S(1)}, bf16[2,384,128]{2,1,0:T(8,128)(2,1)S(1)}, u32[]{:S(2)}, u32[]{:S(2)}) %collective-permute-start.17) | collective-permute-done | bytes 196640 | tf_op jit(solution)/shard_map/ppermute | solution.py:21
  184.5 4.0 %collective-permute-start.18 = (bf16[2,384,128]{2,1,0:T(8,128)(2,1)S(1)}, bf16[2,384,128]{2,1,0:T(8,128)(2,1)S(1)}, u32[]{:S(2)}, u32[]{:S(2)}) collective-permute-start(bf16[2,384,128]{2,1,0:T(8,128)(2,1)S(1)} %collective-permute-done.17), channel_id=1, source_target_pairs={{0,2},{2,4},{4,6},{6,0},{1,3},{3,5},{5,7},{7,1},{8,10},{10,12},{12... | collective-permute-start | bytes 589832 | tf_op jit(solution)/shard_map/ppermute | solution.py:21
  188.5 3.4 %collective-permute-start.19 = (bf16[2,384,128]{2,1,0:T(8,128)(2,1)S(1)}, bf16[2,384,128]{2,1,0:T(8,128)(2,1)S(1)}, u32[]{:S(2)}, u32[]{:S(2)}) collective-permute-start(bf16[2,384,128]{2,1,0:T(8,128)(2,1)S(1)} %collective-permute-done.17), channel_id=1, source_target_pairs={{0,4},{2,6},{4,0},{6,2},{1,5},{3,7},{5,1},{7,3},{8,12},{10,14},{12... | collective-permute-start | bytes 589832 | tf_op jit(solution)/shard_map/ppermute | solution.py:21
  191.8 3.3 %collective-permute-start.20 = (bf16[2,384,128]{2,1,0:T(8,128)(2,1)S(1)}, bf16[2,384,128]{2,1,0:T(8,128)(2,1)S(1)}, u32[]{:S(2)}, u32[]{:S(2)}) collective-permute-start(bf16[2,384,128]{2,1,0:T(8,128)(2,1)S(1)} %collective-permute-done.17), channel_id=1, source_target_pairs={{0,6},{2,0},{4,2},{6,4},{1,7},{3,1},{5,3},{7,5},{8,14},{10,8},{12,... | collective-permute-start | bytes 589832 | tf_op jit(solution)/shard_map/ppermute | solution.py:21
  197.6 3.0 %collective-permute-done.20 = bf16[2,384,128]{2,1,0:T(8,128)(2,1)S(1)} collective-permute-done((bf16[2,384,128]{2,1,0:T(8,128)(2,1)S(1)}, bf16[2,384,128]{2,1,0:T(8,128)(2,1)S(1)}, u32[]{:S(2)}, u32[]{:S(2)}) %collective-permute-start.20) | collective-permute-done | bytes 196640 | tf_op jit(solution)/shard_map/ppermute | solution.py:21
  200.9 3.3 %convolution_convert_fusion = bf16[384,768]{1,0:T(8,128)(2,1)S(1)} fusion(bf16[384,2048]{1,0:T(8,128)(2,1)S(1)} %fusion.11, bf16[2048,768]{1,0:T(8,128)(2,1)} %constant_dynamic-update-slice_fusion), kind=kOutput, calls=%fused_computation.4 | convolution fusion | flops 1208254464 | bytes 5308416 | tf_op jit(solution)/shard_map/dot_general | solution.py:133
  205.5 11.8 %all-to-all-start.1 = ((bf16[32,24,384]{2,1,0:T(8,128)(2,1)}), bf16[32,24,384]{2,1,0:T(8,128)(2,1)S(1)}, u32[]{:S(2)}, u32[]{:S(2)}) async-start(bf16[32,24,384]{2,1,0:T(8,128)(2,1)} %copy.75), calls=%async_computation.1 | async-start | bytes 1179648 | tf_op jit(solution)/shard_map/all_to_all | solution.py:139
  218.6 17.0 %all-to-all-done.1 = bf16[32,24,384]{2,1,0:T(8,128)(2,1)S(1)} async-done(((bf16[32,24,384]{2,1,0:T(8,128)(2,1)}), bf16[32,24,384]{2,1,0:T(8,128)(2,1)S(1)}, u32[]{:S(2)}, u32[]{:S(2)}) %all-to-all-start.1) | async-done | bytes 589856 | tf_op jit(solution)/shard_map/all_to_all | solution.py:139
  (157 shorter events, 85.5 us)
Async XLA Ops:
  0.0 74.0 %collective-permute-start.3 = (f32[768]{0:T(1024)}, f32[768]{0:T(1024)S(1)}, u32[]{:S(2)}, u32[]{:S(2)}) collective-permute-start(f32[768]{0:T(1024)} %param.8), channel_id=1, source_target_pairs={{0,1},{1,0},{2,3},{3,2},{4,5},{5,4},{6,7},{7,6},{8,9},{9,8},{10,11... | collective-permute-start | bytes 9224 | tf_op jit(solution)/shard_map/ppermute | solution.py:21
  13.0 11.1 %collective-permute-start = (f32[32,9]{0,1:T(8,128)S(1)}, f32[32,9]{0,1:T(8,128)S(1)}, u32[]{:S(2)}, u32[]{:S(2)}) collective-permute-start(f32[32,9]{0,1:T(8,128)S(1)} %pad_maximum_fusion.1), channel_id=1, source_target_pairs={{0,1},{1,0},{2,3},{3,2},{4,5},{5,4},{6,7},{7,6},{8,9},{9,8},{10,11... | collective-permute-start | bytes 3464 | tf_op jit(solution)/shard_map/ppermute | solution.py:21
  24.1 5.5 %collective-permute-start.1 = (f32[32,9]{0,1:T(8,128)S(1)}, f32[32,9]{0,1:T(8,128)S(1)}, u32[]{:S(2)}, u32[]{:S(2)}) collective-permute-start(f32[32,9]{0,1:T(8,128)S(1)} %fusion.37), channel_id=1, source_target_pairs={{0,2},{2,0},{4,6},{6,4},{1,3},{3,1},{5,7},{7,5},{8,10},{10,8},{12,... | collective-permute-start | bytes 3464 | tf_op jit(solution)/shard_map/ppermute | solution.py:153
  29.6 7.0 %collective-permute-start.2 = (f32[32,9]{0,1:T(8,128)S(1)}, f32[32,9]{0,1:T(8,128)S(1)}, u32[]{:S(2)}, u32[]{:S(2)}) collective-permute-start(f32[32,9]{0,1:T(8,128)S(1)} %add.208), channel_id=1, source_target_pairs={{0,4},{2,6},{4,0},{6,2},{1,5},{3,7},{5,1},{7,3},{8,12},{10,14},{12... | collective-permute-start | bytes 3464 | tf_op jit(solution)/shard_map/ppermute | solution.py:153
  38.6 66.9 %all-to-all-start = ((bf16[64,24,384]{2,1,0:T(8,128)(2,1)}), bf16[64,24,384]{2,1,0:T(8,128)(2,1)}, u32[]{:S(2)}, u32[]{:S(2)}) async-start(bf16[64,24,384]{2,1,0:T(8,128)(2,1)} %bitcast.4), calls=%async_computation | async-start | bytes 2359296 | tf_op jit(solution)/shard_map/all_to_all | solution.py:101
  53.8 49.0 %collective-permute-start.21 = (bf16[1024,768]{1,0:T(8,128)(2,1)}, bf16[1024,768]{1,0:T(8,128)(2,1)}, u32[]{:S(2)}, u32[]{:S(2)}) collective-permute-start(bf16[1024,768]{1,0:T(8,128)(2,1)} %get-tuple-element.15), channel_id=1, source_target_pairs={{0,8},{8,0},{1,9},{9,1},{2,10},{10,2},{3,11},{11,3},{4,12},{12,4},... | collective-permute-start | bytes 4718600 | tf_op jit(solution)/shard_map/ppermute | solution.py:21
  59.8 24.2 %collective-permute-start.4 = (bf16[1536,256]{1,0:T(8,128)(2,1)}, bf16[1536,256]{1,0:T(8,128)(2,1)}, u32[]{:S(2)}, u32[]{:S(2)}) collective-permute-start(bf16[1536,256]{1,0:T(8,128)(2,1)} %get-tuple-element.12), channel_id=1, source_target_pairs={{0,4},{2,6},{4,0},{6,2},{1,5},{3,7},{5,1},{7,3},{8,12},{10,14},{12... | collective-permute-start | bytes 2359304 | tf_op jit(solution)/shard_map/ppermute | solution.py:21
  63.2 35.0 %collective-permute-start.7 = (bf16[1536,256]{1,0:T(8,128)(2,1)}, bf16[1536,256]{1,0:T(8,128)(2,1)}, u32[]{:S(2)}, u32[]{:S(2)}) collective-permute-start(bf16[1536,256]{1,0:T(8,128)(2,1)} %get-tuple-element.11), channel_id=1, source_target_pairs={{0,2},{2,4},{4,6},{6,0},{1,3},{3,5},{5,7},{7,1},{8,10},{10,12},{12... | collective-permute-start | bytes 2359304 | tf_op jit(solution)/shard_map/ppermute | solution.py:21
  67.3 33.2 %collective-permute-start.10 = (bf16[1536,256]{1,0:T(8,128)(2,1)}, bf16[1536,256]{1,0:T(8,128)(2,1)}, u32[]{:S(2)}, u32[]{:S(2)}) collective-permute-start(bf16[1536,256]{1,0:T(8,128)(2,1)} %get-tuple-element.10), channel_id=1, source_target_pairs={{0,6},{2,0},{4,2},{6,4},{1,7},{3,1},{5,3},{7,5},{8,14},{10,8},{12,... | collective-permute-start | bytes 2359304 | tf_op jit(solution)/shard_map/ppermute | solution.py:21
  74.1 76.1 %collective-permute-start.13 = (bf16[1536,256]{1,0:T(8,128)(2,1)S(1)}, bf16[1536,256]{1,0:T(8,128)(2,1)}, u32[]{:S(2)}, u32[]{:S(2)}) collective-permute-start(bf16[1536,256]{1,0:T(8,128)(2,1)S(1)} %copy-done.7), channel_id=1, source_target_pairs={{0,8},{8,0},{1,9},{9,1},{2,10},{10,2},{3,11},{11,3},{4,12},{12,4},... | collective-permute-start | bytes 2359304 | tf_op jit(solution)/shard_map/ppermute | solution.py:21
  84.0 43.4 %collective-permute-start.5 = (bf16[1536,256]{1,0:T(8,128)(2,1)}, bf16[1536,256]{1,0:T(8,128)(2,1)}, u32[]{:S(2)}, u32[]{:S(2)}) collective-permute-start(bf16[1536,256]{1,0:T(8,128)(2,1)} %collective-permute-done.4), channel_id=1, source_target_pairs={{0,8},{8,0},{1,9},{9,1},{2,10},{10,2},{3,11},{11,3},{4,12},{12,4},... | collective-permute-start | bytes 2359304 | tf_op jit(solution)/shard_map/ppermute | solution.py:21
  98.3 30.7 %collective-permute-start.8 = (bf16[1536,256]{1,0:T(8,128)(2,1)}, bf16[1536,256]{1,0:T(8,128)(2,1)}, u32[]{:S(2)}, u32[]{:S(2)}) collective-permute-start(bf16[1536,256]{1,0:T(8,128)(2,1)} %collective-permute-done.7), channel_id=1, source_target_pairs={{0,8},{8,0},{1,9},{9,1},{2,10},{10,2},{3,11},{11,3},{4,12},{12,4},... | collective-permute-start | bytes 2359304 | tf_op jit(solution)/shard_map/ppermute | solution.py:21
  100.4 30.2 %collective-permute-start.11 = (bf16[1536,256]{1,0:T(8,128)(2,1)}, bf16[1536,256]{1,0:T(8,128)(2,1)}, u32[]{:S(2)}, u32[]{:S(2)}) collective-permute-start(bf16[1536,256]{1,0:T(8,128)(2,1)} %collective-permute-done.10), channel_id=1, source_target_pairs={{0,8},{8,0},{1,9},{9,1},{2,10},{10,2},{3,11},{11,3},{4,12},{12,4},... | collective-permute-start | bytes 2359304 | tf_op jit(solution)/shard_map/ppermute | solution.py:21
  133.4 18.4 %collective-permute-start.12 = (bf16[784,256]{1,0:T(8,128)(2,1)}, bf16[784,256]{1,0:T(8,128)(2,1)}, u32[]{:S(2)}, u32[]{:S(2)}) collective-permute-start(bf16[784,256]{1,0:T(8,128)(2,1)} %get-tuple-element.25), channel_id=1, source_target_pairs={{0,2},{2,4},{4,6},{6,0},{1,3},{3,5},{5,7},{7,1},{8,10},{10,12},{12... | collective-permute-start | bytes 1204232 | tf_op jit(solution)/shard_map/ppermute | solution.py:21
  137.9 23.0 %collective-permute-start.9 = (bf16[784,256]{1,0:T(8,128)(2,1)}, bf16[784,256]{1,0:T(8,128)(2,1)}, u32[]{:S(2)}, u32[]{:S(2)}) collective-permute-start(bf16[784,256]{1,0:T(8,128)(2,1)} %get-tuple-element.24), channel_id=1, source_target_pairs={{0,6},{2,0},{4,2},{6,4},{1,7},{3,1},{5,3},{7,5},{8,14},{10,8},{12,... | collective-permute-start | bytes 1204232 | tf_op jit(solution)/shard_map/ppermute | solution.py:21
  140.2 20.7 %collective-permute-start.6 = (bf16[784,256]{1,0:T(8,128)(2,1)}, bf16[784,256]{1,0:T(8,128)(2,1)}, u32[]{:S(2)}, u32[]{:S(2)}) collective-permute-start(bf16[784,256]{1,0:T(8,128)(2,1)} %get-tuple-element.23), channel_id=1, source_target_pairs={{0,4},{2,6},{4,0},{6,2},{1,5},{3,7},{5,1},{7,3},{8,12},{10,14},{12... | collective-permute-start | bytes 1204232 | tf_op jit(solution)/shard_map/ppermute | solution.py:21
  162.7 29.1 %collective-permute-start.14 = (bf16[2,384,128]{2,1,0:T(8,128)(2,1)S(1)}, bf16[2,384,128]{2,1,0:T(8,128)(2,1)S(1)}, u32[]{:S(2)}, u32[]{:S(2)}) collective-permute-start(bf16[2,384,128]{2,1,0:T(8,128)(2,1)S(1)} %fusion.6), channel_id=1, source_target_pairs={{0,2},{2,4},{4,6},{6,0},{1,3},{3,5},{5,7},{7,1},{8,10},{10,12},{12... | collective-permute-start | bytes 589832 | tf_op jit(solution)/shard_map/ppermute | solution.py:21
  164.7 30.5 %collective-permute-start.15 = (bf16[2,384,128]{2,1,0:T(8,128)(2,1)S(1)}, bf16[2,384,128]{2,1,0:T(8,128)(2,1)S(1)}, u32[]{:S(2)}, u32[]{:S(2)}) collective-permute-start(bf16[2,384,128]{2,1,0:T(8,128)(2,1)S(1)} %fusion.6), channel_id=1, source_target_pairs={{0,4},{2,6},{4,0},{6,2},{1,5},{3,7},{5,1},{7,3},{8,12},{10,14},{12... | collective-permute-start | bytes 589832 | tf_op jit(solution)/shard_map/ppermute | solution.py:21
  167.8 27.4 %collective-permute-start.16 = (bf16[2,384,128]{2,1,0:T(8,128)(2,1)S(1)}, bf16[2,384,128]{2,1,0:T(8,128)(2,1)S(1)}, u32[]{:S(2)}, u32[]{:S(2)}) collective-permute-start(bf16[2,384,128]{2,1,0:T(8,128)(2,1)S(1)} %fusion.6), channel_id=1, source_target_pairs={{0,6},{2,0},{4,2},{6,4},{1,7},{3,1},{5,3},{7,5},{8,14},{10,8},{12,... | collective-permute-start | bytes 589832 | tf_op jit(solution)/shard_map/ppermute | solution.py:21
  171.1 13.4 %collective-permute-start.17 = (bf16[2,384,128]{2,1,0:T(8,128)(2,1)S(1)}, bf16[2,384,128]{2,1,0:T(8,128)(2,1)S(1)}, u32[]{:S(2)}, u32[]{:S(2)}) collective-permute-start(bf16[2,384,128]{2,1,0:T(8,128)(2,1)S(1)} %fusion.6), channel_id=1, source_target_pairs={{0,1},{1,0},{2,3},{3,2},{4,5},{5,4},{6,7},{7,6},{8,9},{9,8},{10,11... | collective-permute-start | bytes 589832 | tf_op jit(solution)/shard_map/ppermute | solution.py:21
  184.5 10.8 %collective-permute-start.18 = (bf16[2,384,128]{2,1,0:T(8,128)(2,1)S(1)}, bf16[2,384,128]{2,1,0:T(8,128)(2,1)S(1)}, u32[]{:S(2)}, u32[]{:S(2)}) collective-permute-start(bf16[2,384,128]{2,1,0:T(8,128)(2,1)S(1)} %collective-permute-done.17), channel_id=1, source_target_pairs={{0,2},{2,4},{4,6},{6,0},{1,3},{3,5},{5,7},{7,1},{8,10},{10,12},{12... | collective-permute-start | bytes 589832 | tf_op jit(solution)/shard_map/ppermute | solution.py:21
  188.5 9.1 %collective-permute-start.19 = (bf16[2,384,128]{2,1,0:T(8,128)(2,1)S(1)}, bf16[2,384,128]{2,1,0:T(8,128)(2,1)S(1)}, u32[]{:S(2)}, u32[]{:S(2)}) collective-permute-start(bf16[2,384,128]{2,1,0:T(8,128)(2,1)S(1)} %collective-permute-done.17), channel_id=1, source_target_pairs={{0,4},{2,6},{4,0},{6,2},{1,5},{3,7},{5,1},{7,3},{8,12},{10,14},{12... | collective-permute-start | bytes 589832 | tf_op jit(solution)/shard_map/ppermute | solution.py:21
  191.8 8.8 %collective-permute-start.20 = (bf16[2,384,128]{2,1,0:T(8,128)(2,1)S(1)}, bf16[2,384,128]{2,1,0:T(8,128)(2,1)S(1)}, u32[]{:S(2)}, u32[]{:S(2)}) collective-permute-start(bf16[2,384,128]{2,1,0:T(8,128)(2,1)S(1)} %collective-permute-done.17), channel_id=1, source_target_pairs={{0,6},{2,0},{4,2},{6,4},{1,7},{3,1},{5,3},{7,5},{8,14},{10,8},{12,... | collective-permute-start | bytes 589832 | tf_op jit(solution)/shard_map/ppermute | solution.py:21
  205.5 30.2 %all-to-all-start.1 = ((bf16[32,24,384]{2,1,0:T(8,128)(2,1)}), bf16[32,24,384]{2,1,0:T(8,128)(2,1)S(1)}, u32[]{:S(2)}, u32[]{:S(2)}) async-start(bf16[32,24,384]{2,1,0:T(8,128)(2,1)} %copy.75), calls=%async_computation.1 | async-start | bytes 1179648 | tf_op jit(solution)/shard_map/all_to_all | solution.py:139
  (10 other events, 147.7 us)

commit v2 on v0

v2 whole, which is shorter than its diff:
```python
import functools

import jax
import jax.numpy as jnp
from jax import lax
from jax.experimental import pallas as pl
from jax.experimental.pallas import tpu as pltpu
from jax.sharding import Mesh, PartitionSpec as P

D = 6144
CAP = 12
MAIN = 8
REST = CAP - MAIN
TAIL = 16

epsilon = 1e-05

NAMES = ("zlo", "yh", "yl", "core", "x", "zhi")
SIZES = (4, 2, 4, 2, 4, 2)
HOMES = ("zlo", "yh", "yl")
DISPATCH = ("zhi", "zlo", "yh", "yl")
F32, BF16 = jnp.float32, jnp.bfloat16
VMEM_LIMIT = 48 * 1024 * 1024


def shift(value, axis, by):
    size = lax.axis_size(axis)
    return lax.ppermute(value, axis, [(i, (i + by) % size) for i in range(size)])


def local_kernel(body, out, *args, flops=0, scratch=(), smem=0):
    outs = out if isinstance(out, (list, tuple)) else [out]
    moved = sum(a.size * a.dtype.itemsize for a in args) + sum(
        o.size * o.dtype.itemsize for o in outs
    )
    return pl.pallas_call(
        body,
        out_shape=out,
        in_specs=[
            pl.BlockSpec(memory_space=pltpu.SMEM if i < smem else pltpu.VMEM)
            for i in range(len(args))
        ],
        scratch_shapes=list(scratch),
        out_specs=jax.tree.map(lambda _: pl.BlockSpec(memory_space=pltpu.VMEM), out),
        compiler_params=pltpu.CompilerParams(vmem_limit_bytes=VMEM_LIMIT),
        cost_estimate=pl.CostEstimate(flops=flops, bytes_accessed=moved, transcendentals=0),
    )(*args)


def iota(shape, dim):
    return lax.broadcasted_iota(jnp.int32, shape, dim)


def dot(a, b):
    return jnp.dot(a, b, preferred_element_type=F32)


def rest_pick(homes, half, wide):
    halves, plain = 2 * REST * homes, REST * homes
    shape = (halves, plain) if wide else (plain, halves)
    a, b = iota(shape, 0 if wide else 1), iota(shape, 1 if wide else 0)
    same = (a // (2 * REST) == b // REST) & (a % REST == b % REST)
    return (same & (a % (2 * REST) // REST == half)).astype(F32).astype(BF16)


def pack_kernel(fan, routes_ref, tok_ref, out_ref):
    count, width = tok_ref.shape
    half = width // 2
    first, second = routes_ref[0:1, :], routes_ref[1:2, :]
    experts = out_ref.shape[0] // (fan[0] * fan[1] * MAIN)
    n = experts * MAIN
    row = iota((n, count), 0)
    named = ((first == row // MAIN) | (second == row // MAIN)).astype(F32)
    earlier = (iota((count, count), 0) < iota((count, count), 1)).astype(F32).astype(BF16)
    slot = dot(named.astype(BF16), earlier)
    place = (row % MAIN).astype(F32)
    pick_main = jnp.where(slot == place, named, 0.0).astype(BF16)
    rest_place = (MAIN + row % REST).astype(F32)
    pick_rest = jnp.where(slot == rest_place, named, 0.0).astype(BF16)
    tok = tok_ref[...]
    main = dot(pick_main, tok).astype(BF16)
    rest = dot(pick_rest, tok)
    is_first = iota((n, half), 0) % MAIN < REST
    rest = jnp.where(is_first, rest[:, :half], rest[:, half:]).astype(BF16)
    for e in range(experts):
        block = slice(e * MAIN, (e + 1) * MAIN)
        main_e = jnp.concatenate([main[block]] * fan[1], 0)
        rest_e = jnp.concatenate([rest[block]] * fan[1], 0)
        for z in range(fan[0]):
            at = pl.ds((z * experts + e) * fan[1] * MAIN, fan[1] * MAIN)
            out_ref[at, :width] = main_e
            out_ref[at, width:] = rest_e


def unpack_kernel(homes, in_ref, gain_ref, rows_ref, tail_ref):
    width = gain_ref.shape[1]
    half = width // 2
    n_main, n_rest = homes * MAIN, homes * REST
    squares_main = jnp.zeros((n_main, 1), F32)
    squares_rest = jnp.zeros((n_rest, 1), F32)
    picks = [rest_pick(homes, h, False) for h in range(2)]
    for z in range(2):
        block = pl.ds(z * n_main, n_main)
        gain = gain_ref[z : z + 1, :]
        main = in_ref[block, :width].astype(F32)
        rows_ref[:n_main, z * width : (z + 1) * width] = (main * gain).astype(BF16)
        squares_main += jnp.sum(main * main, 1, keepdims=True)
        halves = in_ref[block, width:]
        for h in range(2):
            rest = dot(picks[h], halves)
            at = slice(z * width + h * half, z * width + (h + 1) * half)
            rows_ref[n_main:, at] = (rest * gain[:, h * half : (h + 1) * half]).astype(BF16)
            squares_rest += jnp.sum(rest * rest, 1, keepdims=True)

    def lanes(column):
        n = column.shape[0]
        return jnp.sum(jnp.where(iota((n, n), 0) == iota((n, n), 1), column, 0.0), 0, keepdims=True)

    a = lanes(squares_main)
    b = lanes(squares_rest)
    b = jnp.concatenate([b, jnp.zeros((1, n_main - n_rest), F32)], 1)
    row = iota((TAIL, n_main), 0)
    a_hi, b_hi = a.astype(BF16).astype(F32), b.astype(BF16).astype(F32)
    tail = jnp.where(row == 0, a_hi, jnp.where(row == 1, a - a_hi, 0.0))
    tail = jnp.where(row == 2, b_hi, jnp.where(row == 3, b - b_hi, tail))
    tail_ref[...] = tail.astype(BF16)


def partial_kernel(rows_ref, own_ref, other_ref, tail_ref, out_ref):
    n = rows_ref.shape[0]
    out_ref[:n, :] = dot(rows_ref[...], own_ref[...]).astype(BF16)
    out_ref[n : 2 * n, :] = dot(rows_ref[...], other_ref[...]).astype(BF16)
    out_ref[2 * n :, :] = tail_ref[...]


def hidden_kernel(n_main, *refs):
    out_ref = refs[-1]
    units = out_ref.shape[1]
    n = out_ref.shape[0] // 2
    tail = sum(r[2 * n :, :].astype(F32) for r in refs[:-1])
    mean_main = tail[0:1, :] + tail[1:2, :]
    mean_rest = (tail[2:3, :] + tail[3:4, :])[:, : n - n_main]

    def column(line):
        m = line.shape[1]
        return jnp.sum(jnp.where(iota((m, m), 0) == iota((m, m), 1), line, 0.0), 1, keepdims=True)

    squares = jnp.concatenate([column(mean_main), column(mean_rest)], 0)
    inverse = lax.rsqrt(squares / D + epsilon)
    for c in range(2):
        at = pl.ds(c * n, n)
        total = sum(r[at, :].astype(F32) for r in refs[:-1])
        gate, upward = total[:, :units] * inverse, total[:, units:] * inverse
        out_ref[at, :] = (jax.nn.silu(gate) * upward).astype(BF16)


def down_kernel(homes, nx, nz, at_ref, own_ref, other_ref, *refs):
    pieces, out_ref, wide_ref = refs[:-2], refs[-2], refs[-1]
    width = own_ref.shape[1]
    half = width // 2
    units = pieces[0].shape[1]
    n = homes * CAP
    n_main = homes * MAIN
    total = None
    for c, w_ref in enumerate((own_ref, other_ref)):
        for dz in range(nz):
            for k in range(nx):
                t = (at_ref[0] + nx - k) % nx * nz + (at_ref[1] + dz) % nz
                cols = pl.ds(pl.multiple_of(t * units, units), units)
                wide_ref[c, :, cols] = pieces[dz * nx + k][c * n : (c + 1) * n, :]
        term = dot(wide_ref[c], w_ref[...])
        total = term if total is None else total + term
    part = total.astype(BF16)
    out_ref[:, :width] = part[:n_main]
    rest = part[n_main:]
    out_ref[:, width:] = (
        dot(rest_pick(homes, 0, True), rest[:, :half])
        + dot(rest_pick(homes, 1, True), rest[:, half:])
    ).astype(BF16)


def route_weights(logits, routes, experts, homes):
    ids = jnp.arange(experts, dtype=jnp.int32)
    named = (routes[:, :, None] == ids[None, None, :]).astype(F32)
    chosen = jnp.sum(named * logits[:, None, :], -1)
    probs = jnp.stack(
        [
            jax.nn.sigmoid(chosen[:, 0] - chosen[:, 1]),
            jax.nn.sigmoid(chosen[:, 1] - chosen[:, 0]),
        ],
        1,
    )
    count = routes.shape[0]
    both = named.sum(1)
    slot = jnp.cumsum(both, 0) - both
    weight = (named * probs[:, :, None]).sum(1)
    place = jnp.arange(MAIN, dtype=F32)
    shape = (count, experts, homes // experts, MAIN)
    main = jnp.where(slot[:, :, None] == place, weight[:, :, None], 0.0)[:, :, None, :]
    rest_slot = MAIN + place % REST
    rest = jnp.where(slot[:, :, None] == rest_slot, weight[:, :, None], 0.0)[:, :, None, :]
    out = [jnp.broadcast_to(main, shape).reshape(count, -1)]
    for h in range(2):
        mine = (place >= REST) == (h == 1)
        out.append(jnp.broadcast_to(jnp.where(mine, rest, 0.0), shape).reshape(count, -1))
    stacked = jnp.concatenate(out, 0)
    high = stacked.astype(BF16)
    low = (stacked - high.astype(F32)).astype(BF16)
    return high, low


def combine_kernel(tok_ref, hi_ref, lo_ref, back_ref, out_ref):
    count, width = tok_ref.shape
    half = width // 2
    main = back_ref[:, :width]
    rest = back_ref[:, width:]
    at = slice(0, count)
    total = tok_ref[...].astype(F32) + dot(hi_ref[at, :], main) + dot(lo_ref[at, :], main)
    for h in range(2):
        at = slice((h + 1) * count, (h + 2) * count)
        cols = slice(h * half, (h + 1) * half)
        extra = dot(hi_ref[at, :], rest) + dot(lo_ref[at, :], rest)
        out_ref[:, cols] = (total[:, cols] + extra).astype(BF16)


def shards(tokens, norm_gain, router_weight, routes, w_gate, w_up, w_down):
    experts = router_weight.shape[1]
    count, width = tokens.shape
    units = w_gate.shape[1]
    half = width // 2
    span = width + half
    nx, nz, ny = lax.axis_size("x"), lax.axis_size("zhi"), lax.axis_size("yl")
    x, zhi = lax.axis_index("x"), lax.axis_index("zhi")
    homes = experts * ny
    n = homes * CAP
    cols = 2 * units

    def piece(k):
        at = ((x + k) % nx) * (nz * width)
        return jnp.concatenate(
            [lax.dynamic_slice_in_dim(w, at, nz * width, 0) for w in (w_gate, w_up)], 1
        )

    outgoing = local_kernel(
        functools.partial(pack_kernel, (nz, ny)),
        jax.ShapeDtypeStruct((nz * homes * MAIN, span), BF16),
        routes.T,
        tokens,
    )
    outgoing, w_gate, w_up, w_down, norm_gain = lax.optimization_barrier(
        (outgoing, w_gate, w_up, w_down, norm_gain)
    )
    arrived = lax.all_to_all(
        outgoing.reshape(nz * homes, MAIN, span), DISPATCH, 0, 0, tiled=True
    ).reshape(nz * homes * MAIN, span)

    w_x = {k: shift(piece(k), "x", k) for k in (1, 3, 2)}
    w_x[0] = piece(0)
    w_c = {k: shift(w_x[k], "core", 1) for k in (0, 1, 3, 2)}

    wd_other = shift(w_down, "core", 1)

    values = tokens.astype(F32)
    router_part = jnp.concatenate(
        [
            jnp.dot(values * norm_gain[None, :], router_weight, precision=lax.Precision.HIGHEST),
            jnp.sum(values * values, -1, keepdims=True),
        ],
        1,
    )
    summed = router_part + shift(router_part, "zhi", 1)
    for by in (1, 2):
        summed = summed + lax.ppermute(summed, "x", [(i, i ^ by) for i in range(nx)])
    logits = summed[:, :experts] * lax.rsqrt(summed[:, experts:] / D + epsilon)
    w_hi, w_lo = route_weights(logits, routes, experts, homes)

    gain_other = shift(norm_gain, "zhi", 1)
    gains = jnp.where(
        zhi == 0,
        jnp.stack([norm_gain, gain_other]),
        jnp.stack([gain_other, norm_gain]),
    )
    rows, tail = local_kernel(
        functools.partial(unpack_kernel, homes),
        [
            jax.ShapeDtypeStruct((n, nz * width), BF16),
            jax.ShapeDtypeStruct((TAIL, homes * MAIN), BF16),
        ],
        arrived,
        gains,
    )

    def partial(k):
        return local_kernel(
            partial_kernel,
            jax.ShapeDtypeStruct((2 * n + TAIL, cols), BF16),
            rows,
            w_x[k],
            w_c[k],
            tail,
            flops=4 * n * nz * width * cols,
        )

    got = [shift(partial(k), "x", -k) for k in (1, 3, 2)] + [partial(0)]
    hidden = local_kernel(
        functools.partial(hidden_kernel, homes * MAIN),
        jax.ShapeDtypeStruct((2 * n, units), BF16),
        *got,
    )

    gathered = []
    for h in (hidden, shift(hidden, "zhi", 1)):
        gathered += [h] + [shift(h, "x", k) for k in (1, 2, 3)]
    back = local_kernel(
        functools.partial(down_kernel, homes, nx, nz),
        jax.ShapeDtypeStruct((homes * MAIN, span), BF16),
        jnp.stack([x, zhi]).astype(jnp.int32),
        w_down,
        wd_other,
        *gathered,
        flops=4 * n * w_down.size,
        scratch=[pltpu.VMEM((2, n, nx * nz * units), BF16)],
        smem=1,
    )
    returned = lax.all_to_all(
        back.reshape(homes, MAIN, span), HOMES, 0, 0, tiled=True
    ).reshape(homes * MAIN, span)
    return local_kernel(
        combine_kernel,
        jax.ShapeDtypeStruct((count, width), BF16),
        tokens,
        w_hi,
        w_lo,
        returned,
    )


def solution(mesh):
    fine = Mesh(mesh.devices.reshape(SIZES), NAMES)
    section, tp = NAMES[:4], NAMES[4:]
    placed = (
        P(section, tp),
        P(tp),
        P(tp, None),
        P(section, None),
        P(None, section + tp),
        P(None, section + tp),
        P(section, tp),
    )
    return jax.shard_map(
        shards, mesh=fine, in_specs=placed, out_specs=P(section, tp), check_vma=False
    )
```

time: 429 us -> 170 us (0.40)
  waiting for transfers between devices: 300 us -> 49.8 us
  starting transfers between devices: 8.6 us -> 97.4 us
  blocking collectives: 81.9 us -> 0 us
  Pallas kernels: 0 us -> 16.4 us
  matrix products: 15 us -> 0.16 us
  between operations: 13.6 us -> 0.64 us
    all_gather x2 -> x0, waiting for transfers between devices: 261 us -> none  [the longest x1 189 us: shards(): piece = lax.all_gather(expert_rows, 'tp', axis=1, tiled=True)]
    ppermute x0 -> x22, starting transfers between devices: none -> 71.2 us  [the longest x20 65.9 us: shift(): lax.ppermute(value, axis, [(i, (i + by) % size) for i in range(size)])]
    all_to_all x1 -> x0, blocking collectives: 49.7 us -> none  [shards(): lax.all_to_all(outgoing, 'section', split_axis=0, concat_axis=0, tiled=True)]
    ppermute x0 -> x22, waiting for transfers between devices: none -> 33.7 us  [the longest x20 30.1 us: shift(): lax.ppermute(value, axis, [(i, (i + by) % size) for i in range(size)])]
    psum x1 -> x0, blocking collectives: 32.2 us -> none  [shards(): square_sum, router_sum = lax.psum((square_part, router_part), 'tp')]
    all_to_all x1 -> x2, waiting for transfers between devices: 38.6 us -> 16.1 us  [the longest x1 16.1 us: shards(): lax.all_to_all(back.reshape(homes, MAIN, span), HOMES, 0, 0, tiled=True)]
    all_to_all x1 -> x2, starting transfers between devices: 8.55 us -> 26.2 us  [the longest x1 16.6 us: shards(): lax.all_to_all(outgoing.reshape(nz * homes, MAIN, span), DISPATCH, 0, 0,...]
    pallas_call x0 -> x9, Pallas kernels: none -> 16.4 us  [local_kernel(): pl.pallas_call(body, out_shape=out, in_specs=[pl.BlockSpec(memory_space=p...]
  transfers between devices with their start and end apart: 3 -> 24, of which waited for: 3 -> 8; matrix products, arithmetic and copies ran while one was open for 0% -> 2% of each run, Pallas kernels for 0% -> 5%
where the time goes in v2:
time: 170 us; the launch traced here: 169 us
  starting transfers between devices  97.4 us (57%)
  waiting for transfers between devices  49.8 us (29%)
  Pallas kernels  16.4 us (10%)
  local copies, waits for them, and re-layouts  3.66 us (2%)
    ppermute x20, starting transfers between devices, shift(): lax.ppermute(value, axis, [(i, (i + by) % size) for i in range(size)])  65.9 us
    ppermute x20, waiting for transfers between devices, shift(): lax.ppermute(value, axis, [(i, (i + by) % size) for i in range(size)])  30.1 us
    all_to_all x1, starting transfers between devices, shards(): lax.all_to_all(outgoing.reshape(nz * homes, MAIN, span), DISPATCH, 0, 0,...  16.6 us
    pallas_call x9, Pallas kernels, local_kernel(): pl.pallas_call(body, out_shape=out, in_specs=[pl.BlockSpec(memory_space=p...  16.4 us
    all_to_all x1, waiting for transfers between devices, shards(): lax.all_to_all(back.reshape(homes, MAIN, span), HOMES, 0, 0, tiled=True)  16.1 us
    all_to_all x1, starting transfers between devices, shards(): lax.all_to_all(back.reshape(homes, MAIN, span), HOMES, 0, 0, tiled=True)  9.64 us
    ppermute x2, starting transfers between devices, shards(): lax.ppermute(summed, 'x', [(i, i ^ by) for i in range(nx)])  5.29 us
    ppermute x2, waiting for transfers between devices, shards(): lax.ppermute(summed, 'x', [(i, i ^ by) for i in range(nx)])  3.65 us
  transfers between devices with their start and end apart: 24, of which 8 were waited for; matrix products, arithmetic and copies ran while one was open for 2% of the time, Pallas kernels for 5%

profile of v2, /device:TPU:6, one launch (start us, length us, event | category | flops | bytes accessed | tf_op | source)
XLA Modules:
  0.0 168.9 jit_solution(2476765164488760109)
XLA Ops:
  2.9 16.6 %all-to-all-start = ((bf16[64,8,1152]{2,1,0:T(8,128)(2,1)}), bf16[64,8,1152]{2,1,0:T(8,128)(2,1)S(1)}, u32[]{:S(2)}, u32[]{:S(2)}) async-start(bf16[64,8,1152]{2,1,0:T(8,128)(2,1)} %bitcast.8), calls=%async_computation | async-start | bytes 2359296 | tf_op jit(solution)/shard_map/all_to_all | solution.py:253
  21.4 3.3 %collective-permute-start.11 = (bf16[1536,256]{1,0:T(8,128)(2,1)S(1)}, bf16[1536,256]{1,0:T(8,128)(2,1)}, u32[]{:S(2)}, u32[]{:S(2)}) collective-permute-start(bf16[1536,256]{1,0:T(8,128)(2,1)S(1)} %pad_maximum_fusion.2), channel_id=1, source_target_pairs={{0,4},{2,6},{4,0},{6,2},{1,5},{3,7},{5,1},{7,3},{8,12},{10,14},{12... | collective-permute-start | bytes 2359304 | tf_op jit(solution)/shard_map/ppermute | solution.py:28
  26.9 5.1 %collective-permute-start.5 = (bf16[1536,256]{1,0:T(8,128)(2,1)S(1)}, bf16[1536,256]{1,0:T(8,128)(2,1)S(1)}, u32[]{:S(2)}, u32[]{:S(2)}) collective-permute-start(bf16[1536,256]{1,0:T(8,128)(2,1)S(1)} %pad_maximum_fusion), channel_id=1, source_target_pairs={{0,2},{2,4},{4,6},{6,0},{1,3},{3,5},{5,7},{7,1},{8,10},{10,12},{12... | collective-permute-start | bytes 2359304 | tf_op jit(solution)/shard_map/ppermute | solution.py:28
  32.0 7.5 %collective-permute-start.4 = (f32[768]{0:T(1024)S(1)}, f32[768]{0:T(1024)S(1)}, u32[]{:S(2)}, u32[]{:S(2)}) collective-permute-start(f32[768]{0:T(1024)S(1)} %copy-done.6), channel_id=1, source_target_pairs={{0,1},{1,0},{2,3},{3,2},{4,5},{5,4},{6,7},{7,6},{8,9},{9,8},{10,11... | collective-permute-start | bytes 9224 | tf_op jit(solution)/shard_map/ppermute | solution.py:28
  41.4 4.0 %collective-permute-done.11.own_ref = bf16[1536,256]{1,0:T(8,128)(2,1)} collective-permute-done((bf16[1536,256]{1,0:T(8,128)(2,1)S(1)}, bf16[1536,256]{1,0:T(8,128)(2,1)}, u32[]{:S(2)}, u32[]{:S(2)}) %collective-permute-start.11) | collective-permute-done | bytes 786464 | tf_op jit(solution)/shard_map/ppermute | solution.py:28
  47.3 13.4 %collective-permute-done.8.own_ref = bf16[1536,256]{1,0:T(8,128)(2,1)} collective-permute-done((bf16[1536,256]{1,0:T(8,128)(2,1)S(1)}, bf16[1536,256]{1,0:T(8,128)(2,1)}, u32[]{:S(2)}, u32[]{:S(2)}) %collective-permute-start.8) | collective-permute-done | bytes 786464 | tf_op jit(solution)/shard_map/ppermute | solution.py:28
  68.0 7.2 %collective-permute-start = (f32[32,9]{0,1:T(8,128)S(1)}, f32[32,9]{0,1:T(8,128)S(1)}, u32[]{:S(2)}, u32[]{:S(2)}) collective-permute-start(f32[32,9]{0,1:T(8,128)S(1)} %pad_maximum_fusion.5), channel_id=1, source_target_pairs={{0,1},{1,0},{2,3},{3,2},{4,5},{5,4},{6,7},{7,6},{8,9},{9,8},{10,11... | collective-permute-start | bytes 3464 | tf_op jit(solution)/shard_map/ppermute | solution.py:28
  77.4 3.3 %collective-permute-start.13 = (bf16[784,256]{1,0:T(8,128)(2,1)S(1)}, bf16[784,256]{1,0:T(8,128)(2,1)S(1)}, u32[]{:S(2)}, u32[]{:S(2)}) collective-permute-start(bf16[784,256]{1,0:T(8,128)(2,1)S(1)} %shard_map.77), channel_id=1, source_target_pairs={{0,4},{2,6},{4,0},{6,2},{1,5},{3,7},{5,1},{7,3},{8,12},{10,14},{12... | collective-permute-start | bytes 1204232 | tf_op jit(solution)/shard_map/ppermute | solution.py:28
  82.9 3.1 %collective-permute-start.10 = (bf16[784,256]{1,0:T(8,128)(2,1)S(1)}, bf16[784,256]{1,0:T(8,128)(2,1)S(1)}, u32[]{:S(2)}, u32[]{:S(2)}) collective-permute-start(bf16[784,256]{1,0:T(8,128)(2,1)S(1)} %shard_map.76), channel_id=1, source_target_pairs={{0,2},{2,4},{4,6},{6,0},{1,3},{3,5},{5,7},{7,1},{8,10},{10,12},{12... | collective-permute-start | bytes 1204232 | tf_op jit(solution)/shard_map/ppermute | solution.py:28
  88.0 2.7 %collective-permute-start.7 = (bf16[784,256]{1,0:T(8,128)(2,1)S(1)}, bf16[784,256]{1,0:T(8,128)(2,1)S(1)}, u32[]{:S(2)}, u32[]{:S(2)}) collective-permute-start(bf16[784,256]{1,0:T(8,128)(2,1)S(1)} %shard_map.75), channel_id=1, source_target_pairs={{0,6},{2,0},{4,2},{6,4},{1,7},{3,1},{5,3},{7,5},{8,14},{10,8},{12,... | collective-permute-start | bytes 1204232 | tf_op jit(solution)/shard_map/ppermute | solution.py:28
  94.7 4.2 %collective-permute-done.10.refs_1_ = bf16[784,256]{1,0:T(8,128)(2,1)S(1)} collective-permute-done((bf16[784,256]{1,0:T(8,128)(2,1)S(1)}, bf16[784,256]{1,0:T(8,128)(2,1)S(1)}, u32[]{:S(2)}, u32[]{:S(2)}) %collective-permute-start.10) | collective-permute-done | bytes 401440 | tf_op jit(solution)/shard_map/ppermute | solution.py:28
  98.9 3.0 %collective-permute-done.7.refs_0_ = bf16[784,256]{1,0:T(8,128)(2,1)S(1)} collective-permute-done((bf16[784,256]{1,0:T(8,128)(2,1)S(1)}, bf16[784,256]{1,0:T(8,128)(2,1)S(1)}, u32[]{:S(2)}, u32[]{:S(2)}) %collective-permute-start.7) | collective-permute-done | bytes 401440 | tf_op jit(solution)/shard_map/ppermute | solution.py:28
  102.3 2.5 %collective-permute-start.18 = (bf16[768,128]{1,0:T(8,128)(2,1)S(1)}, bf16[768,128]{1,0:T(8,128)(2,1)S(1)}, u32[]{:S(2)}, u32[]{:S(2)}) collective-permute-start(bf16[768,128]{1,0:T(8,128)(2,1)S(1)} %shard_map.79.refs_0_), channel_id=1, source_target_pairs={{0,1},{1,0},{2,3},{3,2},{4,5},{5,4},{6,7},{7,6},{8,9},{9,8},{10,11... | collective-permute-start | bytes 589832 | tf_op jit(solution)/shard_map/ppermute | solution.py:28
  107.2 3.3 %collective-permute-start.2 = (f32[32,9]{0,1:T(8,128)S(1)}, f32[32,9]{0,1:T(8,128)S(1)}, u32[]{:S(2)}, u32[]{:S(2)}) collective-permute-start(f32[32,9]{0,1:T(8,128)S(1)} %add.79), channel_id=1, source_target_pairs={{0,4},{2,6},{4,0},{6,2},{1,5},{3,7},{5,1},{7,3},{8,12},{10,14},{12... | collective-permute-start | bytes 3464 | tf_op jit(solution)/shard_map/ppermute | solution.py:273
  110.6 3.7 %collective-permute-done.2 = f32[32,9]{0,1:T(8,128)S(1)} collective-permute-done((f32[32,9]{0,1:T(8,128)S(1)}, f32[32,9]{0,1:T(8,128)S(1)}, u32[]{:S(2)}, u32[]{:S(2)}) %collective-permute-start.2) | collective-permute-done | bytes 1184 | tf_op jit(solution)/shard_map/ppermute | solution.py:273
  114.2 3.3 %collective-permute-start.16 = (bf16[768,128]{1,0:T(8,128)(2,1)S(1)}, bf16[768,128]{1,0:T(8,128)(2,1)S(1)}, u32[]{:S(2)}, u32[]{:S(2)}) collective-permute-start(bf16[768,128]{1,0:T(8,128)(2,1)S(1)} %shard_map.79.refs_0_), channel_id=1, source_target_pairs={{0,4},{2,6},{4,0},{6,2},{1,5},{3,7},{5,1},{7,3},{8,12},{10,14},{12... | collective-permute-start | bytes 589832 | tf_op jit(solution)/shard_map/ppermute | solution.py:28
  119.9 4.7 %collective-permute-start.19 = (bf16[768,128]{1,0:T(8,128)(2,1)S(1)}, bf16[768,128]{1,0:T(8,128)(2,1)S(1)}, u32[]{:S(2)}, u32[]{:S(2)}) collective-permute-start(bf16[768,128]{1,0:T(8,128)(2,1)S(1)} %collective-permute-done.18.refs_4_), channel_id=1, source_target_pairs={{0,2},{2,4},{4,6},{6,0},{1,3},{3,5},{5,7},{7,1},{8,10},{10,12},{12... | collective-permute-start | bytes 589832 | tf_op jit(solution)/shard_map/ppermute | solution.py:28
  124.6 3.1 %collective-permute-start.20 = (bf16[768,128]{1,0:T(8,128)(2,1)S(1)}, bf16[768,128]{1,0:T(8,128)(2,1)S(1)}, u32[]{:S(2)}, u32[]{:S(2)}) collective-permute-start(bf16[768,128]{1,0:T(8,128)(2,1)S(1)} %collective-permute-done.18.refs_4_), channel_id=1, source_target_pairs={{0,4},{2,6},{4,0},{6,2},{1,5},{3,7},{5,1},{7,3},{8,12},{10,14},{12... | collective-permute-start | bytes 589832 | tf_op jit(solution)/shard_map/ppermute | solution.py:28
  127.7 3.3 %collective-permute-start.21 = (bf16[768,128]{1,0:T(8,128)(2,1)S(1)}, bf16[768,128]{1,0:T(8,128)(2,1)S(1)}, u32[]{:S(2)}, u32[]{:S(2)}) collective-permute-start(bf16[768,128]{1,0:T(8,128)(2,1)S(1)} %collective-permute-done.18.refs_4_), channel_id=1, source_target_pairs={{0,6},{2,0},{4,2},{6,4},{1,7},{3,1},{5,3},{7,5},{8,14},{10,8},{12,... | collective-permute-start | bytes 589832 | tf_op jit(solution)/shard_map/ppermute | solution.py:28
  131.1 2.9 %collective-permute-done.20.refs_6_ = bf16[768,128]{1,0:T(8,128)(2,1)S(1)} collective-permute-done((bf16[768,128]{1,0:T(8,128)(2,1)S(1)}, bf16[768,128]{1,0:T(8,128)(2,1)S(1)}, u32[]{:S(2)}, u32[]{:S(2)}) %collective-permute-start.20) | collective-permute-done | bytes 196640 | tf_op jit(solution)/shard_map/ppermute | solution.py:28
  134.0 2.5 %collective-permute-done.21.refs_7_ = bf16[768,128]{1,0:T(8,128)(2,1)S(1)} collective-permute-done((bf16[768,128]{1,0:T(8,128)(2,1)S(1)}, bf16[768,128]{1,0:T(8,128)(2,1)S(1)}, u32[]{:S(2)}, u32[]{:S(2)}) %collective-permute-start.21) | collective-permute-done | bytes 196640 | tf_op jit(solution)/shard_map/ppermute | solution.py:28
  136.5 5.0 %shard_map.80 = bf16[256,1152]{1,0:T(8,128)(2,1)} custom-call(s32[2]{0:T(128)S(1)} %pad_add_fusion.at_ref, bf16[1024,768]{1,0:T(8,128)(2,1)} %own_ref, bf16[1024,768]{1,0:T(8,128)(2,1)} %collective-permute-done.3.other_ref, bf16[768,128]{1,0:T(8,128)(2,1)S(1)} %shard_map.79.refs_0_, bf16[768,128]{1,0:T(8,128)(2,1)S(1)} %collective-permute-done.15.refs_1_, ...), custom_call_target="tpu_custom_call" | custom-call | flops 1207959552 | bytes 5308424 | tf_op jit(solution)/shard_map/pallas_call | solution.py:36
  141.5 9.6 %all-to-all-start.1 = ((bf16[32,8,1152]{2,1,0:T(8,128)(2,1)}), bf16[32,8,1152]{2,1,0:T(8,128)(2,1)S(1)}, u32[]{:S(2)}, u32[]{:S(2)}) async-start(bf16[32,8,1152]{2,1,0:T(8,128)(2,1)} %bitcast.10), calls=%async_computation.1 | async-start | bytes 1179648 | tf_op jit(solution)/shard_map/all_to_all | solution.py:325
  151.9 16.1 %all-to-all-done.1 = bf16[32,8,1152]{2,1,0:T(8,128)(2,1)S(1)} async-done(((bf16[32,8,1152]{2,1,0:T(8,128)(2,1)}), bf16[32,8,1152]{2,1,0:T(8,128)(2,1)S(1)}, u32[]{:S(2)}, u32[]{:S(2)}) %all-to-all-start.1) | async-done | bytes 589856 | tf_op jit(solution)/shard_map/all_to_all | solution.py:325
  (83 shorter events, 34.7 us)
Async XLA Ops:
  2.9 64.7 %all-to-all-start = ((bf16[64,8,1152]{2,1,0:T(8,128)(2,1)}), bf16[64,8,1152]{2,1,0:T(8,128)(2,1)S(1)}, u32[]{:S(2)}, u32[]{:S(2)}) async-start(bf16[64,8,1152]{2,1,0:T(8,128)(2,1)} %bitcast.8), calls=%async_computation | async-start | bytes 2359296 | tf_op jit(solution)/shard_map/all_to_all | solution.py:253
  21.4 24.0 %collective-permute-start.11 = (bf16[1536,256]{1,0:T(8,128)(2,1)S(1)}, bf16[1536,256]{1,0:T(8,128)(2,1)}, u32[]{:S(2)}, u32[]{:S(2)}) collective-permute-start(bf16[1536,256]{1,0:T(8,128)(2,1)S(1)} %pad_maximum_fusion.2), channel_id=1, source_target_pairs={{0,4},{2,6},{4,0},{6,2},{1,5},{3,7},{5,1},{7,3},{8,12},{10,14},{12... | collective-permute-start | bytes 2359304 | tf_op jit(solution)/shard_map/ppermute | solution.py:28
  24.8 35.9 %collective-permute-start.8 = (bf16[1536,256]{1,0:T(8,128)(2,1)S(1)}, bf16[1536,256]{1,0:T(8,128)(2,1)}, u32[]{:S(2)}, u32[]{:S(2)}) collective-permute-start(bf16[1536,256]{1,0:T(8,128)(2,1)S(1)} %pad_maximum_fusion.1), channel_id=1, source_target_pairs={{0,6},{2,0},{4,2},{6,4},{1,7},{3,1},{5,3},{7,5},{8,14},{10,8},{12,... | collective-permute-start | bytes 2359304 | tf_op jit(solution)/shard_map/ppermute | solution.py:28
  26.9 35.8 %collective-permute-start.5 = (bf16[1536,256]{1,0:T(8,128)(2,1)S(1)}, bf16[1536,256]{1,0:T(8,128)(2,1)S(1)}, u32[]{:S(2)}, u32[]{:S(2)}) collective-permute-start(bf16[1536,256]{1,0:T(8,128)(2,1)S(1)} %pad_maximum_fusion), channel_id=1, source_target_pairs={{0,2},{2,4},{4,6},{6,0},{1,3},{3,5},{5,7},{7,1},{8,10},{10,12},{12... | collective-permute-start | bytes 2359304 | tf_op jit(solution)/shard_map/ppermute | solution.py:28
  32.0 33.4 %collective-permute-start.4 = (f32[768]{0:T(1024)S(1)}, f32[768]{0:T(1024)S(1)}, u32[]{:S(2)}, u32[]{:S(2)}) collective-permute-start(f32[768]{0:T(1024)S(1)} %copy-done.6), channel_id=1, source_target_pairs={{0,1},{1,0},{2,3},{3,2},{4,5},{5,4},{6,7},{7,6},{8,9},{9,8},{10,11... | collective-permute-start | bytes 9224 | tf_op jit(solution)/shard_map/ppermute | solution.py:28
  39.5 85.1 %collective-permute-start.3 = (bf16[1024,768]{1,0:T(8,128)(2,1)}, bf16[1024,768]{1,0:T(8,128)(2,1)}, u32[]{:S(2)}, u32[]{:S(2)}) collective-permute-start(bf16[1024,768]{1,0:T(8,128)(2,1)} %own_ref), channel_id=1, source_target_pairs={{0,8},{8,0},{1,9},{9,1},{2,10},{10,2},{3,11},{11,3},{4,12},{12,4},... | collective-permute-start | bytes 4718600 | tf_op jit(solution)/shard_map/ppermute | solution.py:28
  45.4 22.6 %collective-permute-start.12 = (bf16[1536,256]{1,0:T(8,128)(2,1)}, bf16[1536,256]{1,0:T(8,128)(2,1)}, u32[]{:S(2)}, u32[]{:S(2)}) collective-permute-start(bf16[1536,256]{1,0:T(8,128)(2,1)} %collective-permute-done.11.own_ref), channel_id=1, source_target_pairs={{0,8},{8,0},{1,9},{9,1},{2,10},{10,2},{3,11},{11,3},{4,12},{12,4},... | collective-permute-start | bytes 2359304 | tf_op jit(solution)/shard_map/ppermute | solution.py:28
  60.7 16.7 %collective-permute-start.9 = (bf16[1536,256]{1,0:T(8,128)(2,1)}, bf16[1536,256]{1,0:T(8,128)(2,1)}, u32[]{:S(2)}, u32[]{:S(2)}) collective-permute-start(bf16[1536,256]{1,0:T(8,128)(2,1)} %collective-permute-done.8.own_ref), channel_id=1, source_target_pairs={{0,8},{8,0},{1,9},{9,1},{2,10},{10,2},{3,11},{11,3},{4,12},{12,4},... | collective-permute-start | bytes 2359304 | tf_op jit(solution)/shard_map/ppermute | solution.py:28
  62.7 20.2 %collective-permute-start.6 = (bf16[1536,256]{1,0:T(8,128)(2,1)S(1)}, bf16[1536,256]{1,0:T(8,128)(2,1)}, u32[]{:S(2)}, u32[]{:S(2)}) collective-permute-start(bf16[1536,256]{1,0:T(8,128)(2,1)S(1)} %collective-permute-done.5.own_ref), channel_id=1, source_target_pairs={{0,8},{8,0},{1,9},{9,1},{2,10},{10,2},{3,11},{11,3},{4,12},{12,4},... | collective-permute-start | bytes 2359304 | tf_op jit(solution)/shard_map/ppermute | solution.py:28
  65.4 25.4 %collective-permute-start.14 = (bf16[1536,256]{1,0:T(8,128)(2,1)S(1)}, bf16[1536,256]{1,0:T(8,128)(2,1)}, u32[]{:S(2)}, u32[]{:S(2)}) collective-permute-start(bf16[1536,256]{1,0:T(8,128)(2,1)S(1)} %pad_maximum_fusion.3.own_ref), channel_id=1, source_target_pairs={{0,8},{8,0},{1,9},{9,1},{2,10},{10,2},{3,11},{11,3},{4,12},{12,4},... | collective-permute-start | bytes 2359304 | tf_op jit(solution)/shard_map/ppermute | solution.py:28
  68.0 19.9 %collective-permute-start = (f32[32,9]{0,1:T(8,128)S(1)}, f32[32,9]{0,1:T(8,128)S(1)}, u32[]{:S(2)}, u32[]{:S(2)}) collective-permute-start(f32[32,9]{0,1:T(8,128)S(1)} %pad_maximum_fusion.5), channel_id=1, source_target_pairs={{0,1},{1,0},{2,3},{3,2},{4,5},{5,4},{6,7},{7,6},{8,9},{9,8},{10,11... | collective-permute-start | bytes 3464 | tf_op jit(solution)/shard_map/ppermute | solution.py:28
  77.4 17.2 %collective-permute-start.13 = (bf16[784,256]{1,0:T(8,128)(2,1)S(1)}, bf16[784,256]{1,0:T(8,128)(2,1)S(1)}, u32[]{:S(2)}, u32[]{:S(2)}) collective-permute-start(bf16[784,256]{1,0:T(8,128)(2,1)S(1)} %shard_map.77), channel_id=1, source_target_pairs={{0,4},{2,6},{4,0},{6,2},{1,5},{3,7},{5,1},{7,3},{8,12},{10,14},{12... | collective-permute-start | bytes 1204232 | tf_op jit(solution)/shard_map/ppermute | solution.py:28
  82.9 16.0 %collective-permute-start.10 = (bf16[784,256]{1,0:T(8,128)(2,1)S(1)}, bf16[784,256]{1,0:T(8,128)(2,1)S(1)}, u32[]{:S(2)}, u32[]{:S(2)}) collective-permute-start(bf16[784,256]{1,0:T(8,128)(2,1)S(1)} %shard_map.76), channel_id=1, source_target_pairs={{0,2},{2,4},{4,6},{6,0},{1,3},{3,5},{5,7},{7,1},{8,10},{10,12},{12... | collective-permute-start | bytes 1204232 | tf_op jit(solution)/shard_map/ppermute | solution.py:28
  88.0 14.0 %collective-permute-start.7 = (bf16[784,256]{1,0:T(8,128)(2,1)S(1)}, bf16[784,256]{1,0:T(8,128)(2,1)S(1)}, u32[]{:S(2)}, u32[]{:S(2)}) collective-permute-start(bf16[784,256]{1,0:T(8,128)(2,1)S(1)} %shard_map.75), channel_id=1, source_target_pairs={{0,6},{2,0},{4,2},{6,4},{1,7},{3,1},{5,3},{7,5},{8,14},{10,8},{12,... | collective-permute-start | bytes 1204232 | tf_op jit(solution)/shard_map/ppermute | solution.py:28
  90.7 16.4 %collective-permute-start.1 = (f32[32,9]{0,1:T(8,128)S(1)}, f32[32,9]{0,1:T(8,128)S(1)}, u32[]{:S(2)}, u32[]{:S(2)}) collective-permute-start(f32[32,9]{0,1:T(8,128)S(1)} %fusion.9), channel_id=1, source_target_pairs={{0,2},{2,0},{4,6},{6,4},{1,3},{3,1},{5,7},{7,5},{8,10},{10,8},{12,... | collective-permute-start | bytes 3464 | tf_op jit(solution)/shard_map/ppermute | solution.py:273
  102.3 17.6 %collective-permute-start.18 = (bf16[768,128]{1,0:T(8,128)(2,1)S(1)}, bf16[768,128]{1,0:T(8,128)(2,1)S(1)}, u32[]{:S(2)}, u32[]{:S(2)}) collective-permute-start(bf16[768,128]{1,0:T(8,128)(2,1)S(1)} %shard_map.79.refs_0_), channel_id=1, source_target_pairs={{0,1},{1,0},{2,3},{3,2},{4,5},{5,4},{6,7},{7,6},{8,9},{9,8},{10,11... | collective-permute-start | bytes 589832 | tf_op jit(solution)/shard_map/ppermute | solution.py:28
  104.9 22.9 %collective-permute-start.15 = (bf16[768,128]{1,0:T(8,128)(2,1)S(1)}, bf16[768,128]{1,0:T(8,128)(2,1)S(1)}, u32[]{:S(2)}, u32[]{:S(2)}) collective-permute-start(bf16[768,128]{1,0:T(8,128)(2,1)S(1)} %shard_map.79.refs_0_), channel_id=1, source_target_pairs={{0,2},{2,4},{4,6},{6,0},{1,3},{3,5},{5,7},{7,1},{8,10},{10,12},{12... | collective-permute-start | bytes 589832 | tf_op jit(solution)/shard_map/ppermute | solution.py:28
  107.2 7.0 %collective-permute-start.2 = (f32[32,9]{0,1:T(8,128)S(1)}, f32[32,9]{0,1:T(8,128)S(1)}, u32[]{:S(2)}, u32[]{:S(2)}) collective-permute-start(f32[32,9]{0,1:T(8,128)S(1)} %add.79), channel_id=1, source_target_pairs={{0,4},{2,6},{4,0},{6,2},{1,5},{3,7},{5,1},{7,3},{8,12},{10,14},{12... | collective-permute-start | bytes 3464 | tf_op jit(solution)/shard_map/ppermute | solution.py:273
  114.2 16.9 %collective-permute-start.16 = (bf16[768,128]{1,0:T(8,128)(2,1)S(1)}, bf16[768,128]{1,0:T(8,128)(2,1)S(1)}, u32[]{:S(2)}, u32[]{:S(2)}) collective-permute-start(bf16[768,128]{1,0:T(8,128)(2,1)S(1)} %shard_map.79.refs_0_), channel_id=1, source_target_pairs={{0,4},{2,6},{4,0},{6,2},{1,5},{3,7},{5,1},{7,3},{8,12},{10,14},{12... | collective-permute-start | bytes 589832 | tf_op jit(solution)/shard_map/ppermute | solution.py:28
  117.5 13.6 %collective-permute-start.17 = (bf16[768,128]{1,0:T(8,128)(2,1)S(1)}, bf16[768,128]{1,0:T(8,128)(2,1)S(1)}, u32[]{:S(2)}, u32[]{:S(2)}) collective-permute-start(bf16[768,128]{1,0:T(8,128)(2,1)S(1)} %shard_map.79.refs_0_), channel_id=1, source_target_pairs={{0,6},{2,0},{4,2},{6,4},{1,7},{3,1},{5,3},{7,5},{8,14},{10,8},{12,... | collective-permute-start | bytes 589832 | tf_op jit(solution)/shard_map/ppermute | solution.py:28
  119.9 11.2 %collective-permute-start.19 = (bf16[768,128]{1,0:T(8,128)(2,1)S(1)}, bf16[768,128]{1,0:T(8,128)(2,1)S(1)}, u32[]{:S(2)}, u32[]{:S(2)}) collective-permute-start(bf16[768,128]{1,0:T(8,128)(2,1)S(1)} %collective-permute-done.18.refs_4_), channel_id=1, source_target_pairs={{0,2},{2,4},{4,6},{6,0},{1,3},{3,5},{5,7},{7,1},{8,10},{10,12},{12... | collective-permute-start | bytes 589832 | tf_op jit(solution)/shard_map/ppermute | solution.py:28
  124.6 9.4 %collective-permute-start.20 = (bf16[768,128]{1,0:T(8,128)(2,1)S(1)}, bf16[768,128]{1,0:T(8,128)(2,1)S(1)}, u32[]{:S(2)}, u32[]{:S(2)}) collective-permute-start(bf16[768,128]{1,0:T(8,128)(2,1)S(1)} %collective-permute-done.18.refs_4_), channel_id=1, source_target_pairs={{0,4},{2,6},{4,0},{6,2},{1,5},{3,7},{5,1},{7,3},{8,12},{10,14},{12... | collective-permute-start | bytes 589832 | tf_op jit(solution)/shard_map/ppermute | solution.py:28
  127.7 8.8 %collective-permute-start.21 = (bf16[768,128]{1,0:T(8,128)(2,1)S(1)}, bf16[768,128]{1,0:T(8,128)(2,1)S(1)}, u32[]{:S(2)}, u32[]{:S(2)}) collective-permute-start(bf16[768,128]{1,0:T(8,128)(2,1)S(1)} %collective-permute-done.18.refs_4_), channel_id=1, source_target_pairs={{0,6},{2,0},{4,2},{6,4},{1,7},{3,1},{5,3},{7,5},{8,14},{10,8},{12,... | collective-permute-start | bytes 589832 | tf_op jit(solution)/shard_map/ppermute | solution.py:28
  141.5 26.4 %all-to-all-start.1 = ((bf16[32,8,1152]{2,1,0:T(8,128)(2,1)}), bf16[32,8,1152]{2,1,0:T(8,128)(2,1)S(1)}, u32[]{:S(2)}, u32[]{:S(2)}) async-start(bf16[32,8,1152]{2,1,0:T(8,128)(2,1)} %bitcast.10), calls=%async_computation.1 | async-start | bytes 1179648 | tf_op jit(solution)/shard_map/all_to_all | solution.py:325
  (7 other events, 150.6 us)

commit v3 on v2

--- a/solution.py
+++ b/solution.py
@@ -20,7 +20,10 @@
 HOMES = ("zlo", "yh", "yl")
 DISPATCH = ("zhi", "zlo", "yh", "yl")
 F32, BF16 = jnp.float32, jnp.bfloat16
-VMEM_LIMIT = 48 * 1024 * 1024
+VMEM_LIMIT = 16 * 1024 * 1024
+WINDOW_FLOPS = 10**10
+W_ORDER = (2, 1, 3)
+RS_ORDER = (1, 2, 3)
 
 
 def shift(value, axis, by):
@@ -28,7 +31,9 @@
     return lax.ppermute(value, axis, [(i, (i + by) % size) for i in range(size)])
 
 
-def local_kernel(body, out, *args, flops=0, scratch=(), smem=0):
+def local_kernel(body, out, *args, flops=0, scratch=(), smem=0, far=0, far_out=False):
+    near = len(args) - smem - far
+    spaces = [pltpu.SMEM] * smem + [pltpu.VMEM] * near + [pl.ANY] * far
     outs = out if isinstance(out, (list, tuple)) else [out]
     moved = sum(a.size * a.dtype.itemsize for a in args) + sum(
         o.size * o.dtype.itemsize for o in outs
@@ -36,12 +41,11 @@
     return pl.pallas_call(
         body,
         out_shape=out,
-        in_specs=[
-            pl.BlockSpec(memory_space=pltpu.SMEM if i < smem else pltpu.VMEM)
-            for i in range(len(args))
-        ],
+        in_specs=[pl.BlockSpec(memory_space=space) for space in spaces],
         scratch_shapes=list(scratch),
-        out_specs=jax.tree.map(lambda _: pl.BlockSpec(memory_space=pltpu.VMEM), out),
+        out_specs=jax.tree.map(
+            lambda _: pl.BlockSpec(memory_space=pl.ANY if far_out else pltpu.VMEM), out
+        ),
         compiler_params=pltpu.CompilerParams(vmem_limit_bytes=VMEM_LIMIT),
         cost_estimate=pl.CostEstimate(flops=flops, bytes_accessed=moved, transcendentals=0),
     )(*args)
@@ -126,18 +130,31 @@
     tail_ref[...] = tail.astype(BF16)
 
 
-def partial_kernel(rows_ref, own_ref, other_ref, tail_ref, out_ref):
+def partial_kernel(rows_ref, tail_ref, router_ref, own_ref, other_ref, out_ref, held_ref, sems):
     n = rows_ref.shape[0]
-    out_ref[:n, :] = dot(rows_ref[...], own_ref[...]).astype(BF16)
-    out_ref[n : 2 * n, :] = dot(rows_ref[...], other_ref[...]).astype(BF16)
-    out_ref[2 * n :, :] = tail_ref[...]
+    copies = [
+        pltpu.make_async_copy(w, held_ref.at[i], sems.at[i])
+        for i, w in enumerate((own_ref, other_ref))
+    ]
+    for copy in copies:
+        copy.start()
+    for i, copy in enumerate(copies):
+        copy.wait()
+        out_ref[i * n : (i + 1) * n, :] = dot(rows_ref[...], held_ref[i]).astype(BF16)
+    out_ref[2 * n : 2 * n + TAIL, :] = tail_ref[...]
+    out_ref[2 * n + TAIL :, :] = router_ref[...]
 
 
 def hidden_kernel(n_main, *refs):
-    out_ref = refs[-1]
+    parts, out_ref = refs[:-1], refs[-1]
     units = out_ref.shape[1]
-    n = out_ref.shape[0] // 2
-    tail = sum(r[2 * n :, :].astype(F32) for r in refs[:-1])
+    n = (out_ref.shape[0] - 2 * TAIL) // 2
+    router = sum(r[2 * n + TAIL :, :].astype(F32) for r in parts)
+    router = router[:, :units] + router[:, units:]
+    high = router.astype(BF16)
+    out_ref[2 * n : 2 * n + TAIL, :] = high
+    out_ref[2 * n + TAIL :, :] = (router - high.astype(F32)).astype(BF16)
+    tail = sum(r[2 * n : 2 * n + TAIL, :].astype(F32) for r in parts)
     mean_main = tail[0:1, :] + tail[1:2, :]
     mean_rest = (tail[2:3, :] + tail[3:4, :])[:, : n - n_main]
 
@@ -149,28 +166,48 @@
     inverse = lax.rsqrt(squares / D + epsilon)
     for c in range(2):
         at = pl.ds(c * n, n)
-        total = sum(r[at, :].astype(F32) for r in refs[:-1])
+        total = sum(r[at, :].astype(F32) for r in parts)
         gate, upward = total[:, :units] * inverse, total[:, units:] * inverse
         out_ref[at, :] = (jax.nn.silu(gate) * upward).astype(BF16)
 
 
-def down_kernel(homes, nx, nz, at_ref, own_ref, other_ref, *refs):
+def place_hidden(at_ref, dz, nx, nz, pieces, wide_ref):
+    units = pieces[0].shape[1]
+    for k, piece in enumerate(pieces):
+        where = (at_ref[0] + nx - k) % nx
+        cols = pl.ds(pl.multiple_of(where * units, units), units)
+        wide_ref[:, cols] = piece[: wide_ref.shape[0], :]
+
+
+def down_part(side, homes, nx, nz, pieces, own_ref, other_ref, wide_ref):
+    n = homes * CAP
+    units = pieces[0].shape[1]
+    total = None
+    for c, w_ref in enumerate((own_ref, other_ref)):
+        for x in range(nx):
+            at = pl.multiple_of((x * nz + side) * units, units)
+            term = dot(
+                wide_ref[c * n : (c + 1) * n, x * units : (x + 1) * units],
+                w_ref[pl.ds(at, units), :],
+            )
+            total = term if total is None else total + term
+    return total
+
+
+def down_first_kernel(homes, nx, nz, at_ref, own_ref, other_ref, *refs):
+    pieces, out_ref, wide_ref = refs[:-2], refs[-2], refs[-1]
+    place_hidden(at_ref, 0, nx, nz, pieces, wide_ref)
+    out_ref[...] = down_part(at_ref[1], homes, nx, nz, pieces, own_ref, other_ref, wide_ref)
+
+
+def down_last_kernel(homes, nx, nz, at_ref, own_ref, other_ref, first_ref, *refs):
     pieces, out_ref, wide_ref = refs[:-2], refs[-2], refs[-1]
     width = own_ref.shape[1]
     half = width // 2
-    units = pieces[0].shape[1]
-    n = homes * CAP
     n_main = homes * MAIN
-    total = None
-    for c, w_ref in enumerate((own_ref, other_ref)):
-        for dz in range(nz):
-            for k in range(nx):
-                t = (at_ref[0] + nx - k) % nx * nz + (at_ref[1] + dz) % nz
-                cols = pl.ds(pl.multiple_of(t * units, units), units)
-                wide_ref[c, :, cols] = pieces[dz * nx + k][c * n : (c + 1) * n, :]
-        term = dot(wide_ref[c], w_ref[...])
-        total = term if total is None else total + term
-    part = total.astype(BF16)
+    place_hidden(at_ref, 1, nx, nz, pieces, wide_ref)
+    total = down_part(1 - at_ref[1], homes, nx, nz, pieces, own_ref, other_ref, wide_ref)
+    part = (first_ref[...] + total).astype(BF16)
     out_ref[:, :width] = part[:n_main]
     rest = part[n_main:]
     out_ref[:, width:] = (
@@ -179,48 +216,82 @@
     ).astype(BF16)
 
 
-def route_weights(logits, routes, experts, homes):
-    ids = jnp.arange(experts, dtype=jnp.int32)
-    named = (routes[:, :, None] == ids[None, None, :]).astype(F32)
-    chosen = jnp.sum(named * logits[:, None, :], -1)
-    probs = jnp.stack(
-        [
-            jax.nn.sigmoid(chosen[:, 0] - chosen[:, 1]),
-            jax.nn.sigmoid(chosen[:, 1] - chosen[:, 0]),
-        ],
-        1,
-    )
-    count = routes.shape[0]
-    both = named.sum(1)
-    slot = jnp.cumsum(both, 0) - both
-    weight = (named * probs[:, :, None]).sum(1)
-    place = jnp.arange(MAIN, dtype=F32)
-    shape = (count, experts, homes // experts, MAIN)
-    main = jnp.where(slot[:, :, None] == place, weight[:, :, None], 0.0)[:, :, None, :]
-    rest_slot = MAIN + place % REST
-    rest = jnp.where(slot[:, :, None] == rest_slot, weight[:, :, None], 0.0)[:, :, None, :]
-    out = [jnp.broadcast_to(main, shape).reshape(count, -1)]
+def router_kernel(side_ref, tok_ref, gain_ref, gain_other_ref, router_ref, out_ref, gains_ref):
+    values = tok_ref[...].astype(F32)
+    count = values.shape[0]
+    experts = router_ref.shape[0]
+    sums = lax.dot_general(
+        router_ref[...],
+        values * gain_ref[...],
+        (((1,), (1,)), ((), ())),
+        precision=lax.Precision.HIGHEST,
+        preferred_element_type=F32,
+    )
+    squares = jnp.sum(values * values, 1, keepdims=True)
+    diagonal = iota((count, count), 0) == iota((count, count), 1)
+    line = jnp.sum(jnp.where(diagonal, squares, 0.0), 0, keepdims=True)
+    block = jnp.concatenate([sums, jnp.broadcast_to(line, (TAIL - experts, count))], 0)
+    high = block.astype(BF16)
+    low = (block - high.astype(F32)).astype(BF16)
+    lanes = out_ref.shape[1] // 2
+    blank = jnp.zeros((TAIL, lanes - count), BF16)
+    out_ref[...] = jnp.concatenate([high, blank, low, blank], 1)
+    mine = iota(gains_ref.shape, 0) == side_ref[0]
+    gains_ref[...] = jnp.where(mine, gain_ref[...], gain_other_ref[...])
+
+
+def weights_kernel(experts, routes_ref, own_ref, other_ref, out_ref):
+    count = routes_ref.shape[1]
+    rows = out_ref.shape[0] // 2 // 3
+    sums = jnp.zeros((TAIL, count), F32)
+    for ref in (own_ref, other_ref):
+        n = ref.shape[0]
+        for at in (n - 2 * TAIL, n - TAIL):
+            sums += ref[at : at + TAIL, :count].astype(F32)
+    logits = sums[:experts] * lax.rsqrt(sums[experts : experts + 1] / D + epsilon)
+    first, second = routes_ref[0:1, :], routes_ref[1:2, :]
+    ids = iota((experts, count), 0)
+    one = jnp.sum(jnp.where(ids == first, logits, 0.0), 0, keepdims=True)
+    two = jnp.sum(jnp.where(ids == second, logits, 0.0), 0, keepdims=True)
+    p_one, p_two = jax.nn.sigmoid(one - two), jax.nn.sigmoid(two - one)
+    row = iota((rows, count), 0)
+    expert = row // (rows // experts)
+    named = ((first == expert) | (second == expert)).astype(F32)
+    earlier = (iota((count, count), 0) < iota((count, count), 1)).astype(F32).astype(BF16)
+    slot = dot(named.astype(BF16), earlier)
+    weight = jnp.where(first == expert, p_one, 0.0) + jnp.where(second == expert, p_two, 0.0)
+    place = row % MAIN
+    main = jnp.where(slot == place.astype(F32), weight, 0.0)
+    rest = jnp.where(slot == (MAIN + place % REST).astype(F32), weight, 0.0)
+    blocks = [main, jnp.where(place < REST, rest, 0.0), jnp.where(place >= REST, rest, 0.0)]
+    for i, block in enumerate(blocks):
+        high = block.astype(BF16)
+        low = (block - high.astype(F32)).astype(BF16)
+        out_ref[i * rows : (i + 1) * rows, :] = high
+        out_ref[(3 + i) * rows : (4 + i) * rows, :] = low
+
+
+def combine_kernel(tok_ref, weight_ref, back_ref, out_ref):
+    width = tok_ref.shape[1]
+    half = width // 2
+    rows = back_ref.shape[0]
+
+    def mix(block, part):
+        total = 0.0
+        for i in (block, 3 + block):
+            total += lax.dot_general(
+                weight_ref[i * rows : (i + 1) * rows, :],
+                part,
+                (((0,), (0,)), ((), ())),
+                preferred_element_type=F32,
+            )
+        return total
+
+    total = tok_ref[...].astype(F32) + mix(0, back_ref[:, :width])
+    rest = back_ref[:, width:]
     for h in range(2):
-        mine = (place >= REST) == (h == 1)
-        out.append(jnp.broadcast_to(jnp.where(mine, rest, 0.0), shape).reshape(count, -1))
-    stacked = jnp.concatenate(out, 0)
-    high = stacked.astype(BF16)
-    low = (stacked - high.astype(F32)).astype(BF16)
-    return high, low
-
-
-def combine_kernel(tok_ref, hi_ref, lo_ref, back_ref, out_ref):
-    count, width = tok_ref.shape
-    half = width // 2
-    main = back_ref[:, :width]
-    rest = back_ref[:, width:]
-    at = slice(0, count)
-    total = tok_ref[...].astype(F32) + dot(hi_ref[at, :], main) + dot(lo_ref[at, :], main)
-    for h in range(2):
-        at = slice((h + 1) * count, (h + 2) * count)
         cols = slice(h * half, (h + 1) * half)
-        extra = dot(hi_ref[at, :], rest) + dot(lo_ref[at, :], rest)
-        out_ref[:, cols] = (total[:, cols] + extra).astype(BF16)
+        out_ref[:, cols] = (total[:, cols] + mix(1 + h, rest)).astype(BF16)
 
 
 def shards(tokens, norm_gain, router_weight, routes, w_gate, w_up, w_down):
@@ -247,38 +318,30 @@
         routes.T,
         tokens,
     )
-    outgoing, w_gate, w_up, w_down, norm_gain = lax.optimization_barrier(
-        (outgoing, w_gate, w_up, w_down, norm_gain)
+    outgoing, w_gate, w_up, norm_gain = lax.optimization_barrier(
+        (outgoing, w_gate, w_up, norm_gain)
     )
     arrived = lax.all_to_all(
         outgoing.reshape(nz * homes, MAIN, span), DISPATCH, 0, 0, tiled=True
     ).reshape(nz * homes * MAIN, span)
 
-    w_x = {k: shift(piece(k), "x", k) for k in (1, 3, 2)}
+    w_x = {k: shift(piece(k), "x", k) for k in W_ORDER}
     w_x[0] = piece(0)
     w_c = {k: shift(w_x[k], "core", 1) for k in (0, 1, 3, 2)}
-
     wd_other = shift(w_down, "core", 1)
-
-    values = tokens.astype(F32)
-    router_part = jnp.concatenate(
+    router, gains = local_kernel(
+        router_kernel,
         [
-            jnp.dot(values * norm_gain[None, :], router_weight, precision=lax.Precision.HIGHEST),
-            jnp.sum(values * values, -1, keepdims=True),
+            jax.ShapeDtypeStruct((TAIL, cols), BF16),
+            jax.ShapeDtypeStruct((nz, width), F32),
         ],
-        1,
-    )
-    summed = router_part + shift(router_part, "zhi", 1)
-    for by in (1, 2):
-        summed = summed + lax.ppermute(summed, "x", [(i, i ^ by) for i in range(nx)])
-    logits = summed[:, :experts] * lax.rsqrt(summed[:, experts:] / D + epsilon)
-    w_hi, w_lo = route_weights(logits, routes, experts, homes)
-
-    gain_other = shift(norm_gain, "zhi", 1)
-    gains = jnp.where(
-        zhi == 0,
-        jnp.stack([norm_gain, gain_other]),
-        jnp.stack([gain_other, norm_gain]),
+        zhi.astype(jnp.int32)[None],
+        tokens,
+        norm_gain[None, :],
+        shift(norm_gain, "zhi", 1)[None, :],
+        router_weight.T,
+        flops=WINDOW_FLOPS,
+        smem=1,
     )
     rows, tail = local_kernel(
         functools.partial(unpack_kernel, homes),
@@ -293,44 +356,72 @@
     def partial(k):
         return local_kernel(
             partial_kernel,
-            jax.ShapeDtypeStruct((2 * n + TAIL, cols), BF16),
+            jax.ShapeDtypeStruct((2 * n + 2 * TAIL, cols), BF16),
             rows,
+            tail,
+            router,
             w_x[k],
             w_c[k],
-            tail,
+            far=2,
+            scratch=[
+                pltpu.VMEM((2, nz * width, cols), BF16),
+                pltpu.SemaphoreType.DMA((2,)),
+            ],
             flops=4 * n * nz * width * cols,
         )
 
-    got = [shift(partial(k), "x", -k) for k in (1, 3, 2)] + [partial(0)]
+    got = [shift(partial(k), "x", -k) for k in RS_ORDER] + [partial(0)]
     hidden = local_kernel(
         functools.partial(hidden_kernel, homes * MAIN),
-        jax.ShapeDtypeStruct((2 * n, units), BF16),
+        jax.ShapeDtypeStruct((2 * n + 2 * TAIL, units), BF16),
         *got,
     )
 
-    gathered = []
-    for h in (hidden, shift(hidden, "zhi", 1)):
-        gathered += [h] + [shift(h, "x", k) for k in (1, 2, 3)]
-    back = local_kernel(
-        functools.partial(down_kernel, homes, nx, nz),
-        jax.ShapeDtypeStruct((homes * MAIN, span), BF16),
-        jnp.stack([x, zhi]).astype(jnp.int32),
+    at = jnp.stack([x, zhi]).astype(jnp.int32)
+    hid_other = shift(hidden, "zhi", 1)
+    own_rows = hidden[: 2 * n]
+    own_side = [own_rows] + [shift(own_rows, "x", k) for k in (1, 2, 3)]
+    first = local_kernel(
+        functools.partial(down_first_kernel, homes, nx, nz),
+        jax.ShapeDtypeStruct((n, width), F32),
+        at,
         w_down,
         wd_other,
-        *gathered,
-        flops=4 * n * w_down.size,
-        scratch=[pltpu.VMEM((2, n, nx * nz * units), BF16)],
+        *own_side,
+        flops=2 * n * w_down.size,
+        scratch=[pltpu.VMEM((2 * n, nx * units), BF16)],
         smem=1,
     )
+    other_rows = hid_other[: 2 * n]
+    other_side = [other_rows] + [shift(other_rows, "x", k) for k in (1, 2, 3)]
+    back = local_kernel(
+        functools.partial(down_last_kernel, homes, nx, nz),
+        jax.ShapeDtypeStruct((homes * MAIN, span), BF16),
+        at,
+        w_down,
+        wd_other,
+        first,
+        *other_side,
+        flops=2 * n * w_down.size,
+        scratch=[pltpu.VMEM((2 * n, nx * units), BF16)],
+        smem=1,
+    )
+    back, routes = lax.optimization_barrier((back, routes))
     returned = lax.all_to_all(
         back.reshape(homes, MAIN, span), HOMES, 0, 0, tiled=True
     ).reshape(homes * MAIN, span)
+    weights = local_kernel(
+        functools.partial(weights_kernel, experts),
+        jax.ShapeDtypeStruct((6 * homes * MAIN, count), BF16),
+        routes.T,
+        hidden,
+        hid_other,
+    )
     return local_kernel(
         combine_kernel,
         jax.ShapeDtypeStruct((count, width), BF16),
         tokens,
-        w_hi,
-        w_lo,
+        weights,
         returned,
     )
 

time: 170 us -> 170 us (level)
  starting transfers between devices: 97.4 us -> 87.7 us
  Pallas kernels: 16.4 us -> 20.2 us
  other arithmetic: 0.85 us -> 4.03 us
    ppermute x2 -> x0, starting transfers between devices: 5.29 us -> none  [shards(): lax.ppermute(summed, 'x', [(i, i ^ by) for i in range(nx)])]
    ppermute x20 -> x19, starting transfers between devices: 65.9 us -> 61.8 us  [shift(): lax.ppermute(value, axis, [(i, (i + by) % size) for i in range(size)])]
    pallas_call x9 -> x12, Pallas kernels: 16.4 us -> 20.2 us  [local_kernel(): pl.pallas_call(body, out_shape=out, in_specs=[pl.BlockSpec(memory_space=s...]
    ppermute x20 -> x19, waiting for transfers between devices: 30.1 us -> 33.8 us  [shift(): lax.ppermute(value, axis, [(i, (i + by) % size) for i in range(size)])]
    ppermute x2 -> x0, waiting for transfers between devices: 3.65 us -> none  [shards(): lax.ppermute(summed, 'x', [(i, i ^ by) for i in range(nx)])]
    concatenate x4, other arithmetic: 0.35 us -> 3.96 us  [piece(): jnp.concatenate([lax.dynamic_slice_in_dim(w, at, nz * width, 0) for w in...]
  transfers between devices with their start and end apart: 24 -> 21, of which waited for: 8 -> 8; matrix products, arithmetic and copies ran while one was open for 2% -> 3% of each run, Pallas kernels for 5% -> 9%
where the time goes in v3:
time: 170 us; the launch traced here: 168 us
  starting transfers between devices  87.7 us (52%)
  waiting for transfers between devices  51.4 us (30%)
  Pallas kernels  20.2 us (12%)
  local copies, waits for them, and re-layouts  4.59 us (3%)
  other arithmetic  4.03 us (2%)
    ppermute x19, starting transfers between devices, shift(): lax.ppermute(value, axis, [(i, (i + by) % size) for i in range(size)])  61.8 us
    ppermute x19, waiting for transfers between devices, shift(): lax.ppermute(value, axis, [(i, (i + by) % size) for i in range(size)])  33.8 us
    pallas_call x12, Pallas kernels, local_kernel(): pl.pallas_call(body, out_shape=out, in_specs=[pl.BlockSpec(memory_space=s...  20.2 us
    all_to_all x1, waiting for transfers between devices, shards(): lax.all_to_all(back.reshape(homes, MAIN, span), HOMES, 0, 0, tiled=True)  17.7 us
    all_to_all x1, starting transfers between devices, shards(): lax.all_to_all(outgoing.reshape(nz * homes, MAIN, span), DISPATCH, 0, 0,...  16.8 us
    all_to_all x1, starting transfers between devices, shards(): lax.all_to_all(back.reshape(homes, MAIN, span), HOMES, 0, 0, tiled=True)  9.04 us
    concatenate x4, other arithmetic, piece(): jnp.concatenate([lax.dynamic_slice_in_dim(w, at, nz * width, 0) for w in...  3.96 us
  transfers between devices with their start and end apart: 21, of which 8 were waited for; matrix products, arithmetic and copies ran while one was open for 3% of the time, Pallas kernels for 9%

profile of v3, /device:TPU:6, one launch (start us, length us, event | category | flops | bytes accessed | tf_op | source)
XLA Modules:
  0.0 168.4 jit_solution(2356807443516824177)
XLA Ops:
  2.8 16.8 %all-to-all-start = ((bf16[64,8,1152]{2,1,0:T(8,128)(2,1)}), bf16[64,8,1152]{2,1,0:T(8,128)(2,1)}, u32[]{:S(2)}, u32[]{:S(2)}) async-start(bf16[64,8,1152]{2,1,0:T(8,128)(2,1)} %bitcast.3), calls=%async_computation | async-start | bytes 2359296 | tf_op jit(solution)/shard_map/all_to_all | solution.py:324
  22.3 2.7 %collective-permute-start.8 = (bf16[1536,256]{1,0:T(8,128)(2,1)}, bf16[1536,256]{1,0:T(8,128)(2,1)}, u32[]{:S(2)}, u32[]{:S(2)}) collective-permute-start(bf16[1536,256]{1,0:T(8,128)(2,1)} %pad_maximum_fusion.2), channel_id=1, source_target_pairs={{0,6},{2,0},{4,2},{6,4},{1,7},{3,1},{5,3},{7,5},{8,14},{10,8},{12,... | collective-permute-start | bytes 2359304 | tf_op jit(solution)/shard_map/ppermute | solution.py:31
  26.1 3.0 %collective-permute-start.5 = (bf16[1536,256]{1,0:T(8,128)(2,1)}, bf16[1536,256]{1,0:T(8,128)(2,1)}, u32[]{:S(2)}, u32[]{:S(2)}) collective-permute-start(bf16[1536,256]{1,0:T(8,128)(2,1)} %pad_maximum_fusion.1), channel_id=1, source_target_pairs={{0,4},{2,6},{4,0},{6,2},{1,5},{3,7},{5,1},{7,3},{8,12},{10,14},{12... | collective-permute-start | bytes 2359304 | tf_op jit(solution)/shard_map/ppermute | solution.py:31
  30.1 4.0 %collective-permute-start.2 = (bf16[1536,256]{1,0:T(8,128)(2,1)}, bf16[1536,256]{1,0:T(8,128)(2,1)}, u32[]{:S(2)}, u32[]{:S(2)}) collective-permute-start(bf16[1536,256]{1,0:T(8,128)(2,1)} %pad_maximum_fusion), channel_id=1, source_target_pairs={{0,2},{2,4},{4,6},{6,0},{1,3},{3,5},{5,7},{7,1},{8,10},{10,12},{12... | collective-permute-start | bytes 2359304 | tf_op jit(solution)/shard_map/ppermute | solution.py:31
  34.1 7.4 %collective-permute-start.1 = (f32[768]{0:T(1024)S(1)}, f32[768]{0:T(1024)S(1)}, u32[]{:S(2)}, u32[]{:S(2)}) collective-permute-start(f32[768]{0:T(1024)S(1)} %copy-done.9), channel_id=1, source_target_pairs={{0,1},{1,0},{2,3},{3,2},{4,5},{5,4},{6,7},{7,6},{8,9},{9,8},{10,11... | collective-permute-start | bytes 9224 | tf_op jit(solution)/shard_map/ppermute | solution.py:31
  44.4 3.5 %collective-permute-done.1 = f32[768]{0:T(1024)S(1)} collective-permute-done((f32[768]{0:T(1024)S(1)}, f32[768]{0:T(1024)S(1)}, u32[]{:S(2)}, u32[]{:S(2)}) %collective-permute-start.1) | collective-permute-done | bytes 3104 | tf_op jit(solution)/shard_map/ppermute | solution.py:31
  49.9 11.7 %collective-permute-done.8.own_ref = bf16[1536,256]{1,0:T(8,128)(2,1)} collective-permute-done((bf16[1536,256]{1,0:T(8,128)(2,1)}, bf16[1536,256]{1,0:T(8,128)(2,1)}, u32[]{:S(2)}, u32[]{:S(2)}) %collective-permute-start.8) | collective-permute-done | bytes 786464 | tf_op jit(solution)/shard_map/ppermute | solution.py:31
  69.9 2.7 %shard_map.78 = bf16[800,256]{1,0:T(8,128)(2,1)S(1)} custom-call(bf16[384,1536]{1,0:T(8,128)(2,1)S(1)} %get-tuple-element.18.rows_ref, bf16[16,256]{1,0:T(8,128)(2,1)S(1)} %get-tuple-element.19.tail_ref, bf16[16,256]{1,0:T(8,128)(2,1)S(1)} %get-tuple-element.20.router_ref, bf16[1536,256]{1,0:T(8,128)(2,1)} %collective-permute-done.8.own_ref, ...), custom_call_target="tpu_custom_call" | custom-call | flops 603979776 | bytes 3178496 | tf_op jit(solution)/shard_map/pallas_call | solution.py:41
  72.6 3.7 %collective-permute-start.10 = (bf16[800,256]{1,0:T(8,128)(2,1)S(1)}, bf16[800,256]{1,0:T(8,128)(2,1)S(1)}, u32[]{:S(2)}, u32[]{:S(2)}) collective-permute-start(bf16[800,256]{1,0:T(8,128)(2,1)S(1)} %shard_map.78), channel_id=1, source_target_pairs={{0,2},{2,4},{4,6},{6,0},{1,3},{3,5},{5,7},{7,1},{8,10},{10,12},{12... | collective-permute-start | bytes 1228808 | tf_op jit(solution)/shard_map/ppermute | solution.py:31
  76.3 2.7 %shard_map.77 = bf16[800,256]{1,0:T(8,128)(2,1)S(1)} custom-call(bf16[384,1536]{1,0:T(8,128)(2,1)S(1)} %get-tuple-element.18.rows_ref, bf16[16,256]{1,0:T(8,128)(2,1)S(1)} %get-tuple-element.19.tail_ref, bf16[16,256]{1,0:T(8,128)(2,1)S(1)} %get-tuple-element.20.router_ref, bf16[1536,256]{1,0:T(8,128)(2,1)} %collective-permute-done.5.own_ref, ...), custom_call_target="tpu_custom_call" | custom-call | flops 603979776 | bytes 3178496 | tf_op jit(solution)/shard_map/pallas_call | solution.py:41
  81.1 2.7 %shard_map.76 = bf16[800,256]{1,0:T(8,128)(2,1)S(1)} custom-call(bf16[384,1536]{1,0:T(8,128)(2,1)S(1)} %get-tuple-element.18.rows_ref, bf16[16,256]{1,0:T(8,128)(2,1)S(1)} %get-tuple-element.19.tail_ref, bf16[16,256]{1,0:T(8,128)(2,1)S(1)} %get-tuple-element.20.router_ref, bf16[1536,256]{1,0:T(8,128)(2,1)} %collective-permute-done.2.own_ref, ...), custom_call_target="tpu_custom_call" | custom-call | flops 603979776 | bytes 3178496 | tf_op jit(solution)/shard_map/pallas_call | solution.py:41
  83.8 2.6 %collective-permute-start.4 = (bf16[800,256]{1,0:T(8,128)(2,1)S(1)}, bf16[800,256]{1,0:T(8,128)(2,1)S(1)}, u32[]{:S(2)}, u32[]{:S(2)}) collective-permute-start(bf16[800,256]{1,0:T(8,128)(2,1)S(1)} %shard_map.76), channel_id=1, source_target_pairs={{0,6},{2,0},{4,2},{6,4},{1,7},{3,1},{5,3},{7,5},{8,14},{10,8},{12,... | collective-permute-start | bytes 1228808 | tf_op jit(solution)/shard_map/ppermute | solution.py:31
  86.4 2.7 %shard_map.79.refs_3_ = bf16[800,256]{1,0:T(8,128)(2,1)S(1)} custom-call(bf16[384,1536]{1,0:T(8,128)(2,1)S(1)} %get-tuple-element.18.rows_ref, bf16[16,256]{1,0:T(8,128)(2,1)S(1)} %get-tuple-element.19.tail_ref, bf16[16,256]{1,0:T(8,128)(2,1)S(1)} %get-tuple-element.20.router_ref, bf16[1536,256]{1,0:T(8,128)(2,1)} %pad_maximum_fusion.3.own_ref, ...), custom_call_target="tpu_custom_call" | custom-call | flops 603979776 | bytes 3178496 | tf_op jit(solution)/shard_map/pallas_call | solution.py:41
  89.1 5.4 %collective-permute-done.10.refs_2_ = bf16[800,256]{1,0:T(8,128)(2,1)S(1)} collective-permute-done((bf16[800,256]{1,0:T(8,128)(2,1)S(1)}, bf16[800,256]{1,0:T(8,128)(2,1)S(1)}, u32[]{:S(2)}, u32[]{:S(2)}) %collective-permute-start.10) | collective-permute-done | bytes 409632 | tf_op jit(solution)/shard_map/ppermute | solution.py:31
  94.7 8.0 %collective-permute-done.4.refs_0_ = bf16[800,256]{1,0:T(8,128)(2,1)S(1)} collective-permute-done((bf16[800,256]{1,0:T(8,128)(2,1)S(1)}, bf16[800,256]{1,0:T(8,128)(2,1)S(1)}, u32[]{:S(2)}, u32[]{:S(2)}) %collective-permute-start.4) | collective-permute-done | bytes 409632 | tf_op jit(solution)/shard_map/ppermute | solution.py:31
  103.1 7.1 %collective-permute-start.15 = (bf16[800,128]{1,0:T(8,128)(2,1)S(1)}, bf16[800,128]{1,0:T(8,128)(2,1)S(1)}, u32[]{:S(2)}, u32[]{:S(2)}) collective-permute-start(bf16[800,128]{1,0:T(8,128)(2,1)S(1)} %shard_map.80.own_ref), channel_id=1, source_target_pairs={{0,1},{1,0},{2,3},{3,2},{4,5},{5,4},{6,7},{7,6},{8,9},{9,8},{10,11... | collective-permute-start | bytes 614408 | tf_op jit(solution)/shard_map/ppermute | solution.py:31
  110.3 2.5 %collective-permute-start.12 = (bf16[768,128]{1,0:T(8,128)(2,1)S(1)}, bf16[768,128]{1,0:T(8,128)(2,1)S(1)}, u32[]{:S(2)}, u32[]{:S(2)}) collective-permute-start(bf16[768,128]{1,0:T(8,128)(2,1)S(1)} %slice.8.refs_0_), channel_id=1, source_target_pairs={{0,2},{2,4},{4,6},{6,0},{1,3},{3,5},{5,7},{7,1},{8,10},{10,12},{12... | collective-permute-start | bytes 589832 | tf_op jit(solution)/shard_map/ppermute | solution.py:31
  115.0 3.0 %collective-permute-start.14 = (bf16[768,128]{1,0:T(8,128)(2,1)S(1)}, bf16[768,128]{1,0:T(8,128)(2,1)S(1)}, u32[]{:S(2)}, u32[]{:S(2)}) collective-permute-start(bf16[768,128]{1,0:T(8,128)(2,1)S(1)} %slice.8.refs_0_), channel_id=1, source_target_pairs={{0,6},{2,0},{4,2},{6,4},{1,7},{3,1},{5,3},{7,5},{8,14},{10,8},{12,... | collective-permute-start | bytes 589832 | tf_op jit(solution)/shard_map/ppermute | solution.py:31
  118.1 4.6 %collective-permute-start.16 = (bf16[768,128]{1,0:T(8,128)(2,1)S(1)}, bf16[768,128]{1,0:T(8,128)(2,1)S(1)}, u32[]{:S(2)}, u32[]{:S(2)}) collective-permute-start(bf16[768,128]{1,0:T(8,128)(2,1)S(1)} %slice.9.refs_0_), channel_id=1, source_target_pairs={{0,2},{2,4},{4,6},{6,0},{1,3},{3,5},{5,7},{7,1},{8,10},{10,12},{12... | collective-permute-start | bytes 589832 | tf_op jit(solution)/shard_map/ppermute | solution.py:31
  122.7 3.4 %collective-permute-start.17 = (bf16[768,128]{1,0:T(8,128)(2,1)S(1)}, bf16[768,128]{1,0:T(8,128)(2,1)S(1)}, u32[]{:S(2)}, u32[]{:S(2)}) collective-permute-start(bf16[768,128]{1,0:T(8,128)(2,1)S(1)} %slice.9.refs_0_), channel_id=1, source_target_pairs={{0,4},{2,6},{4,0},{6,2},{1,5},{3,7},{5,1},{7,3},{8,12},{10,14},{12... | collective-permute-start | bytes 589832 | tf_op jit(solution)/shard_map/ppermute | solution.py:31
  126.1 3.3 %collective-permute-start.18 = (bf16[768,128]{1,0:T(8,128)(2,1)S(1)}, bf16[768,128]{1,0:T(8,128)(2,1)S(1)}, u32[]{:S(2)}, u32[]{:S(2)}) collective-permute-start(bf16[768,128]{1,0:T(8,128)(2,1)S(1)} %slice.9.refs_0_), channel_id=1, source_target_pairs={{0,6},{2,0},{4,2},{6,4},{1,7},{3,1},{5,3},{7,5},{8,14},{10,8},{12,... | collective-permute-start | bytes 589832 | tf_op jit(solution)/shard_map/ppermute | solution.py:31
  136.4 2.5 %shard_map.82 = bf16[256,1152]{1,0:T(8,128)(2,1)S(1)} custom-call(s32[2]{0:T(128)S(1)} %pad_add_fusion.at_ref, bf16[1024,768]{1,0:T(8,128)(2,1)S(1)} %copy-done, bf16[1024,768]{1,0:T(8,128)(2,1)S(1)} %collective-permute-done.other_ref, f32[384,768]{1,0:T(8,128)S(1)} %shard_map.81.first_ref, bf16[768,128]{1,0:T(8,128)(2,1)S(1)} %slice.9.refs_0_, ...), custom_call_target="tpu_custom_call" | custom-call | flops 603979776 | bytes 5701640 | tf_op jit(solution)/shard_map/pallas_call | solution.py:41
  139.8 9.0 %all-to-all-start.1 = ((bf16[32,8,1152]{2,1,0:T(8,128)(2,1)}), bf16[32,8,1152]{2,1,0:T(8,128)(2,1)S(1)}, u32[]{:S(2)}, u32[]{:S(2)}) async-start(bf16[32,8,1152]{2,1,0:T(8,128)(2,1)} %bitcast.9), calls=%async_computation.1 | async-start | bytes 1179648 | tf_op jit(solution)/shard_map/all_to_all | solution.py:410
  149.7 17.7 %all-to-all-done.1 = bf16[32,8,1152]{2,1,0:T(8,128)(2,1)S(1)} async-done(((bf16[32,8,1152]{2,1,0:T(8,128)(2,1)}), bf16[32,8,1152]{2,1,0:T(8,128)(2,1)S(1)}, u32[]{:S(2)}, u32[]{:S(2)}) %all-to-all-start.1) | async-done | bytes 589856 | tf_op jit(solution)/shard_map/all_to_all | solution.py:410
  (60 shorter events, 35.1 us)
Async XLA Ops:
  2.8 65.2 %all-to-all-start = ((bf16[64,8,1152]{2,1,0:T(8,128)(2,1)}), bf16[64,8,1152]{2,1,0:T(8,128)(2,1)}, u32[]{:S(2)}, u32[]{:S(2)}) async-start(bf16[64,8,1152]{2,1,0:T(8,128)(2,1)} %bitcast.3), calls=%async_computation | async-start | bytes 2359296 | tf_op jit(solution)/shard_map/all_to_all | solution.py:324
  22.3 39.3 %collective-permute-start.8 = (bf16[1536,256]{1,0:T(8,128)(2,1)}, bf16[1536,256]{1,0:T(8,128)(2,1)}, u32[]{:S(2)}, u32[]{:S(2)}) collective-permute-start(bf16[1536,256]{1,0:T(8,128)(2,1)} %pad_maximum_fusion.2), channel_id=1, source_target_pairs={{0,6},{2,0},{4,2},{6,4},{1,7},{3,1},{5,3},{7,5},{8,14},{10,8},{12,... | collective-permute-start | bytes 2359304 | tf_op jit(solution)/shard_map/ppermute | solution.py:31
  26.1 37.4 %collective-permute-start.5 = (bf16[1536,256]{1,0:T(8,128)(2,1)}, bf16[1536,256]{1,0:T(8,128)(2,1)}, u32[]{:S(2)}, u32[]{:S(2)}) collective-permute-start(bf16[1536,256]{1,0:T(8,128)(2,1)} %pad_maximum_fusion.1), channel_id=1, source_target_pairs={{0,4},{2,6},{4,0},{6,2},{1,5},{3,7},{5,1},{7,3},{8,12},{10,14},{12... | collective-permute-start | bytes 2359304 | tf_op jit(solution)/shard_map/ppermute | solution.py:31
  29.1 38.8 %copy-start.3 = (bf16[32,768]{1,0:T(8,128)(2,1)S(1)}, bf16[32,768]{1,0:T(8,128)(2,1)}, u32[]{:S(2)}) copy-start(bf16[32,768]{1,0:T(8,128)(2,1)} %tok_ref.5) | copy-start | bytes 147460
  29.1 38.8 %copy-start.7 = (f32[768,8]{0,1:T(8,128)S(1)}, f32[768,8]{0,1:T(8,128)}, u32[]{:S(2)}) copy-start(f32[768,8]{0,1:T(8,128)} %param.9) | copy-start | bytes 73732
  30.1 35.8 %collective-permute-start.2 = (bf16[1536,256]{1,0:T(8,128)(2,1)}, bf16[1536,256]{1,0:T(8,128)(2,1)}, u32[]{:S(2)}, u32[]{:S(2)}) collective-permute-start(bf16[1536,256]{1,0:T(8,128)(2,1)} %pad_maximum_fusion), channel_id=1, source_target_pairs={{0,2},{2,4},{4,6},{6,0},{1,3},{3,5},{5,7},{7,1},{8,10},{10,12},{12... | collective-permute-start | bytes 2359304 | tf_op jit(solution)/shard_map/ppermute | solution.py:31
  34.1 13.8 %collective-permute-start.1 = (f32[768]{0:T(1024)S(1)}, f32[768]{0:T(1024)S(1)}, u32[]{:S(2)}, u32[]{:S(2)}) collective-permute-start(f32[768]{0:T(1024)S(1)} %copy-done.9), channel_id=1, source_target_pairs={{0,1},{1,0},{2,3},{3,2},{4,5},{5,4},{6,7},{7,6},{8,9},{9,8},{10,11... | collective-permute-start | bytes 9224 | tf_op jit(solution)/shard_map/ppermute | solution.py:31
  42.5 43.9 %collective-permute-start.11 = (bf16[1536,256]{1,0:T(8,128)(2,1)}, bf16[1536,256]{1,0:T(8,128)(2,1)}, u32[]{:S(2)}, u32[]{:S(2)}) collective-permute-start(bf16[1536,256]{1,0:T(8,128)(2,1)} %pad_maximum_fusion.3.own_ref), channel_id=1, source_target_pairs={{0,8},{8,0},{1,9},{9,1},{2,10},{10,2},{3,11},{11,3},{4,12},{12,4},... | collective-permute-start | bytes 2359304 | tf_op jit(solution)/shard_map/ppermute | solution.py:31
  47.9 74.8 %collective-permute-start = (bf16[1024,768]{1,0:T(8,128)(2,1)S(1)}, bf16[1024,768]{1,0:T(8,128)(2,1)S(1)}, u32[]{:S(2)}, u32[]{:S(2)}) collective-permute-start(bf16[1024,768]{1,0:T(8,128)(2,1)S(1)} %copy-done), channel_id=1, source_target_pairs={{0,8},{8,0},{1,9},{9,1},{2,10},{10,2},{3,11},{11,3},{4,12},{12,4},... | collective-permute-start | bytes 4718600 | tf_op jit(solution)/shard_map/ppermute | solution.py:31
  61.6 8.3 %collective-permute-start.9 = (bf16[1536,256]{1,0:T(8,128)(2,1)}, bf16[1536,256]{1,0:T(8,128)(2,1)}, u32[]{:S(2)}, u32[]{:S(2)}) collective-permute-start(bf16[1536,256]{1,0:T(8,128)(2,1)} %collective-permute-done.8.own_ref), channel_id=1, source_target_pairs={{0,8},{8,0},{1,9},{9,1},{2,10},{10,2},{3,11},{11,3},{4,12},{12,4},... | collective-permute-start | bytes 2359304 | tf_op jit(solution)/shard_map/ppermute | solution.py:31
  63.5 12.8 %collective-permute-start.6 = (bf16[1536,256]{1,0:T(8,128)(2,1)}, bf16[1536,256]{1,0:T(8,128)(2,1)}, u32[]{:S(2)}, u32[]{:S(2)}) collective-permute-start(bf16[1536,256]{1,0:T(8,128)(2,1)} %collective-permute-done.5.own_ref), channel_id=1, source_target_pairs={{0,8},{8,0},{1,9},{9,1},{2,10},{10,2},{3,11},{11,3},{4,12},{12,4},... | collective-permute-start | bytes 2359304 | tf_op jit(solution)/shard_map/ppermute | solution.py:31
  65.9 15.2 %collective-permute-start.3 = (bf16[1536,256]{1,0:T(8,128)(2,1)}, bf16[1536,256]{1,0:T(8,128)(2,1)}, u32[]{:S(2)}, u32[]{:S(2)}) collective-permute-start(bf16[1536,256]{1,0:T(8,128)(2,1)} %collective-permute-done.2.own_ref), channel_id=1, source_target_pairs={{0,8},{8,0},{1,9},{9,1},{2,10},{10,2},{3,11},{11,3},{4,12},{12,4},... | collective-permute-start | bytes 2359304 | tf_op jit(solution)/shard_map/ppermute | solution.py:31
  72.6 21.9 %collective-permute-start.10 = (bf16[800,256]{1,0:T(8,128)(2,1)S(1)}, bf16[800,256]{1,0:T(8,128)(2,1)S(1)}, u32[]{:S(2)}, u32[]{:S(2)}) collective-permute-start(bf16[800,256]{1,0:T(8,128)(2,1)S(1)} %shard_map.78), channel_id=1, source_target_pairs={{0,2},{2,4},{4,6},{6,0},{1,3},{3,5},{5,7},{7,1},{8,10},{10,12},{12... | collective-permute-start | bytes 1228808 | tf_op jit(solution)/shard_map/ppermute | solution.py:31
  79.0 15.7 %collective-permute-start.7 = (bf16[800,256]{1,0:T(8,128)(2,1)S(1)}, bf16[800,256]{1,0:T(8,128)(2,1)S(1)}, u32[]{:S(2)}, u32[]{:S(2)}) collective-permute-start(bf16[800,256]{1,0:T(8,128)(2,1)S(1)} %shard_map.77), channel_id=1, source_target_pairs={{0,4},{2,6},{4,0},{6,2},{1,5},{3,7},{5,1},{7,3},{8,12},{10,14},{12... | collective-permute-start | bytes 1228808 | tf_op jit(solution)/shard_map/ppermute | solution.py:31
  83.8 19.0 %collective-permute-start.4 = (bf16[800,256]{1,0:T(8,128)(2,1)S(1)}, bf16[800,256]{1,0:T(8,128)(2,1)S(1)}, u32[]{:S(2)}, u32[]{:S(2)}) collective-permute-start(bf16[800,256]{1,0:T(8,128)(2,1)S(1)} %shard_map.76), channel_id=1, source_target_pairs={{0,6},{2,0},{4,2},{6,4},{1,7},{3,1},{5,3},{7,5},{8,14},{10,8},{12,... | collective-permute-start | bytes 1228808 | tf_op jit(solution)/shard_map/ppermute | solution.py:31
  103.1 15.0 %collective-permute-start.15 = (bf16[800,128]{1,0:T(8,128)(2,1)S(1)}, bf16[800,128]{1,0:T(8,128)(2,1)S(1)}, u32[]{:S(2)}, u32[]{:S(2)}) collective-permute-start(bf16[800,128]{1,0:T(8,128)(2,1)S(1)} %shard_map.80.own_ref), channel_id=1, source_target_pairs={{0,1},{1,0},{2,3},{3,2},{4,5},{5,4},{6,7},{7,6},{8,9},{9,8},{10,11... | collective-permute-start | bytes 614408 | tf_op jit(solution)/shard_map/ppermute | solution.py:31
  110.3 15.8 %collective-permute-start.12 = (bf16[768,128]{1,0:T(8,128)(2,1)S(1)}, bf16[768,128]{1,0:T(8,128)(2,1)S(1)}, u32[]{:S(2)}, u32[]{:S(2)}) collective-permute-start(bf16[768,128]{1,0:T(8,128)(2,1)S(1)} %slice.8.refs_0_), channel_id=1, source_target_pairs={{0,2},{2,4},{4,6},{6,0},{1,3},{3,5},{5,7},{7,1},{8,10},{10,12},{12... | collective-permute-start | bytes 589832 | tf_op jit(solution)/shard_map/ppermute | solution.py:31
  112.8 16.7 %collective-permute-start.13 = (bf16[768,128]{1,0:T(8,128)(2,1)S(1)}, bf16[768,128]{1,0:T(8,128)(2,1)S(1)}, u32[]{:S(2)}, u32[]{:S(2)}) collective-permute-start(bf16[768,128]{1,0:T(8,128)(2,1)S(1)} %slice.8.refs_0_), channel_id=1, source_target_pairs={{0,4},{2,6},{4,0},{6,2},{1,5},{3,7},{5,1},{7,3},{8,12},{10,14},{12... | collective-permute-start | bytes 589832 | tf_op jit(solution)/shard_map/ppermute | solution.py:31
  115.0 14.5 %collective-permute-start.14 = (bf16[768,128]{1,0:T(8,128)(2,1)S(1)}, bf16[768,128]{1,0:T(8,128)(2,1)S(1)}, u32[]{:S(2)}, u32[]{:S(2)}) collective-permute-start(bf16[768,128]{1,0:T(8,128)(2,1)S(1)} %slice.8.refs_0_), channel_id=1, source_target_pairs={{0,6},{2,0},{4,2},{6,4},{1,7},{3,1},{5,3},{7,5},{8,14},{10,8},{12,... | collective-permute-start | bytes 589832 | tf_op jit(solution)/shard_map/ppermute | solution.py:31
  118.1 13.5 %collective-permute-start.16 = (bf16[768,128]{1,0:T(8,128)(2,1)S(1)}, bf16[768,128]{1,0:T(8,128)(2,1)S(1)}, u32[]{:S(2)}, u32[]{:S(2)}) collective-permute-start(bf16[768,128]{1,0:T(8,128)(2,1)S(1)} %slice.9.refs_0_), channel_id=1, source_target_pairs={{0,2},{2,4},{4,6},{6,0},{1,3},{3,5},{5,7},{7,1},{8,10},{10,12},{12... | collective-permute-start | bytes 589832 | tf_op jit(solution)/shard_map/ppermute | solution.py:31
  122.7 11.3 %collective-permute-start.17 = (bf16[768,128]{1,0:T(8,128)(2,1)S(1)}, bf16[768,128]{1,0:T(8,128)(2,1)S(1)}, u32[]{:S(2)}, u32[]{:S(2)}) collective-permute-start(bf16[768,128]{1,0:T(8,128)(2,1)S(1)} %slice.9.refs_0_), channel_id=1, source_target_pairs={{0,4},{2,6},{4,0},{6,2},{1,5},{3,7},{5,1},{7,3},{8,12},{10,14},{12... | collective-permute-start | bytes 589832 | tf_op jit(solution)/shard_map/ppermute | solution.py:31
  126.1 10.3 %collective-permute-start.18 = (bf16[768,128]{1,0:T(8,128)(2,1)S(1)}, bf16[768,128]{1,0:T(8,128)(2,1)S(1)}, u32[]{:S(2)}, u32[]{:S(2)}) collective-permute-start(bf16[768,128]{1,0:T(8,128)(2,1)S(1)} %slice.9.refs_0_), channel_id=1, source_target_pairs={{0,6},{2,0},{4,2},{6,4},{1,7},{3,1},{5,3},{7,5},{8,14},{10,8},{12,... | collective-permute-start | bytes 589832 | tf_op jit(solution)/shard_map/ppermute | solution.py:31
  139.7 27.7 %copy-start.4 = (bf16[32,768]{1,0:T(8,128)(2,1)S(1)}, bf16[32,768]{1,0:T(8,128)(2,1)}, u32[]{:S(2)}) copy-start(bf16[32,768]{1,0:T(8,128)(2,1)} %tok_ref.5) | copy-start | bytes 147460
  139.8 27.6 %all-to-all-start.1 = ((bf16[32,8,1152]{2,1,0:T(8,128)(2,1)}), bf16[32,8,1152]{2,1,0:T(8,128)(2,1)S(1)}, u32[]{:S(2)}, u32[]{:S(2)}) async-start(bf16[32,8,1152]{2,1,0:T(8,128)(2,1)} %bitcast.9), calls=%async_computation.1 | async-start | bytes 1179648 | tf_op jit(solution)/shard_map/all_to_all | solution.py:410
  (7 other events, 49.1 us)

commit v4 on v3

--- a/solution.py
+++ b/solution.py
@@ -21,9 +21,7 @@
 DISPATCH = ("zhi", "zlo", "yh", "yl")
 F32, BF16 = jnp.float32, jnp.bfloat16
 VMEM_LIMIT = 16 * 1024 * 1024
-WINDOW_FLOPS = 10**10
-W_ORDER = (2, 1, 3)
-RS_ORDER = (1, 2, 3)
+WINDOW_FLOPS = 10**11
 
 
 def shift(value, axis, by):
@@ -31,10 +29,14 @@
     return lax.ppermute(value, axis, [(i, (i + by) % size) for i in range(size)])
 
 
-def local_kernel(body, out, *args, flops=0, scratch=(), smem=0, far=0, far_out=False):
+def local_kernel(body, out, *args, flops=0, scratch=(), smem=0, far=0, far_outs=(), aliases=None):
     near = len(args) - smem - far
     spaces = [pltpu.SMEM] * smem + [pltpu.VMEM] * near + [pl.ANY] * far
     outs = out if isinstance(out, (list, tuple)) else [out]
+    out_specs = [
+        pl.BlockSpec(memory_space=pl.ANY if i in far_outs else pltpu.VMEM)
+        for i in range(len(outs))
+    ]
     moved = sum(a.size * a.dtype.itemsize for a in args) + sum(
         o.size * o.dtype.itemsize for o in outs
     )
@@ -43,9 +45,8 @@
         out_shape=out,
         in_specs=[pl.BlockSpec(memory_space=space) for space in spaces],
         scratch_shapes=list(scratch),
-        out_specs=jax.tree.map(
-            lambda _: pl.BlockSpec(memory_space=pl.ANY if far_out else pltpu.VMEM), out
-        ),
+        out_specs=out_specs if isinstance(out, list) else out_specs[0],
+        input_output_aliases=aliases or {},
         compiler_params=pltpu.CompilerParams(vmem_limit_bytes=VMEM_LIMIT),
         cost_estimate=pl.CostEstimate(flops=flops, bytes_accessed=moved, transcendentals=0),
     )(*args)
@@ -130,31 +131,41 @@
     tail_ref[...] = tail.astype(BF16)
 
 
-def partial_kernel(rows_ref, tail_ref, router_ref, own_ref, other_ref, out_ref, held_ref, sems):
+def partial_kernel(at_ref, rows_ref, tail_ref, router_ref, *refs):
+    weights, (out_ref, parts_ref, sems) = refs[:-3], refs[-3:]
     n = rows_ref.shape[0]
-    copies = [
-        pltpu.make_async_copy(w, held_ref.at[i], sems.at[i])
-        for i, w in enumerate((own_ref, other_ref))
-    ]
-    for copy in copies:
+    block = 2 * n + 2 * TAIL
+    nx = len(weights) // 2
+    sent = []
+    for k in range(nx):
+        for c in range(2):
+            part = dot(rows_ref[...], weights[2 * k + c][...])
+            parts_ref[k, c * n : (c + 1) * n, :] = part.astype(BF16)
+        parts_ref[k, 2 * n : 2 * n + TAIL, :] = tail_ref[...]
+        parts_ref[k, 2 * n + TAIL :, :] = router_ref[...]
+        to = pl.multiple_of((at_ref[0] + nx - k) % nx * block, block)
+        copy = pltpu.make_async_copy(parts_ref.at[k], out_ref.at[pl.ds(to, block), :], sems.at[k])
         copy.start()
-    for i, copy in enumerate(copies):
+        sent.append(copy)
+    for copy in sent:
         copy.wait()
-        out_ref[i * n : (i + 1) * n, :] = dot(rows_ref[...], held_ref[i]).astype(BF16)
-    out_ref[2 * n : 2 * n + TAIL, :] = tail_ref[...]
-    out_ref[2 * n + TAIL :, :] = router_ref[...]
-
-
-def hidden_kernel(n_main, *refs):
-    parts, out_ref = refs[:-1], refs[-1]
+
+
+def hidden_kernel(n_main, nx, in_ref, out_ref):
     units = out_ref.shape[1]
     n = (out_ref.shape[0] - 2 * TAIL) // 2
-    router = sum(r[2 * n + TAIL :, :].astype(F32) for r in parts)
+    block = 2 * n + 2 * TAIL
+
+    def total(at, rows):
+        parts = [in_ref[i * block + at : i * block + at + rows, :].astype(F32) for i in range(nx)]
+        return sum(parts[1:], parts[0])
+
+    router = total(2 * n + TAIL, TAIL)
     router = router[:, :units] + router[:, units:]
     high = router.astype(BF16)
     out_ref[2 * n : 2 * n + TAIL, :] = high
     out_ref[2 * n + TAIL :, :] = (router - high.astype(F32)).astype(BF16)
-    tail = sum(r[2 * n : 2 * n + TAIL, :].astype(F32) for r in parts)
+    tail = total(2 * n, TAIL)
     mean_main = tail[0:1, :] + tail[1:2, :]
     mean_rest = (tail[2:3, :] + tail[3:4, :])[:, : n - n_main]
 
@@ -165,48 +176,38 @@
     squares = jnp.concatenate([column(mean_main), column(mean_rest)], 0)
     inverse = lax.rsqrt(squares / D + epsilon)
     for c in range(2):
-        at = pl.ds(c * n, n)
-        total = sum(r[at, :].astype(F32) for r in parts)
-        gate, upward = total[:, :units] * inverse, total[:, units:] * inverse
-        out_ref[at, :] = (jax.nn.silu(gate) * upward).astype(BF16)
-
-
-def place_hidden(at_ref, dz, nx, nz, pieces, wide_ref):
+        both = total(c * n, n)
+        gate, upward = both[:, :units] * inverse, both[:, units:] * inverse
+        out_ref[c * n : (c + 1) * n, :] = (jax.nn.silu(gate) * upward).astype(BF16)
+
+
+def down_part(at_ref, dz, n, nx, nz, pieces, own_ref, other_ref):
     units = pieces[0].shape[1]
-    for k, piece in enumerate(pieces):
-        where = (at_ref[0] + nx - k) % nx
-        cols = pl.ds(pl.multiple_of(where * units, units), units)
-        wide_ref[:, cols] = piece[: wide_ref.shape[0], :]
-
-
-def down_part(side, homes, nx, nz, pieces, own_ref, other_ref, wide_ref):
-    n = homes * CAP
-    units = pieces[0].shape[1]
+    side = (at_ref[1] + dz) % nz
     total = None
     for c, w_ref in enumerate((own_ref, other_ref)):
-        for x in range(nx):
-            at = pl.multiple_of((x * nz + side) * units, units)
-            term = dot(
-                wide_ref[c * n : (c + 1) * n, x * units : (x + 1) * units],
-                w_ref[pl.ds(at, units), :],
+        for k in range(0, nx, 2):
+            wide = jnp.concatenate([p[c * n : (c + 1) * n, :] for p in pieces[k : k + 2]], 1)
+            blocks = [(at_ref[0] + nx - k - i) % nx * nz + side for i in range(2)]
+            w = jnp.concatenate(
+                [w_ref[pl.ds(pl.multiple_of(t * units, units), units), :] for t in blocks], 0
             )
+            term = dot(wide, w)
             total = term if total is None else total + term
     return total
 
 
 def down_first_kernel(homes, nx, nz, at_ref, own_ref, other_ref, *refs):
-    pieces, out_ref, wide_ref = refs[:-2], refs[-2], refs[-1]
-    place_hidden(at_ref, 0, nx, nz, pieces, wide_ref)
-    out_ref[...] = down_part(at_ref[1], homes, nx, nz, pieces, own_ref, other_ref, wide_ref)
+    pieces, out_ref = refs[:-1], refs[-1]
+    out_ref[...] = down_part(at_ref, 0, homes * CAP, nx, nz, pieces, own_ref, other_ref)
 
 
 def down_last_kernel(homes, nx, nz, at_ref, own_ref, other_ref, first_ref, *refs):
-    pieces, out_ref, wide_ref = refs[:-2], refs[-2], refs[-1]
+    pieces, out_ref = refs[:-1], refs[-1]
     width = own_ref.shape[1]
     half = width // 2
     n_main = homes * MAIN
-    place_hidden(at_ref, 1, nx, nz, pieces, wide_ref)
-    total = down_part(1 - at_ref[1], homes, nx, nz, pieces, own_ref, other_ref, wide_ref)
+    total = down_part(at_ref, 1, homes * CAP, nx, nz, pieces, own_ref, other_ref)
     part = (first_ref[...] + total).astype(BF16)
     out_ref[:, :width] = part[:n_main]
     rest = part[n_main:]
@@ -216,7 +217,7 @@
     ).astype(BF16)
 
 
-def router_kernel(side_ref, tok_ref, gain_ref, gain_other_ref, router_ref, out_ref, gains_ref):
+def router_kernel(tok_ref, gain_ref, router_ref, _, __, out_ref, ___):
     values = tok_ref[...].astype(F32)
     count = values.shape[0]
     experts = router_ref.shape[0]
@@ -236,8 +237,15 @@
     lanes = out_ref.shape[1] // 2
     blank = jnp.zeros((TAIL, lanes - count), BF16)
     out_ref[...] = jnp.concatenate([high, blank, low, blank], 1)
-    mine = iota(gains_ref.shape, 0) == side_ref[0]
-    gains_ref[...] = jnp.where(mine, gain_ref[...], gain_other_ref[...])
+
+
+def join_kernel(in_ref, _, __, out_ref, *___):
+    out_ref[...] = in_ref[...]
+
+
+def gains_kernel(at_ref, gain_ref, other_ref, _, out_ref, __):
+    mine = iota(out_ref.shape, 0) == at_ref[1]
+    out_ref[...] = jnp.where(mine, gain_ref[...], other_ref[...])
 
 
 def weights_kernel(experts, routes_ref, own_ref, other_ref, out_ref):
@@ -306,43 +314,67 @@
     n = homes * CAP
     cols = 2 * units
 
-    def piece(k):
-        at = ((x + k) % nx) * (nz * width)
+    at = jnp.stack([x, zhi]).astype(jnp.int32)
+    depth = nz * width
+    piece = jax.ShapeDtypeStruct((depth, cols), BF16)
+
+    def rows_for(k):
+        start = ((x + k) % nx) * depth
         return jnp.concatenate(
-            [lax.dynamic_slice_in_dim(w, at, nz * width, 0) for w in (w_gate, w_up)], 1
+            [lax.dynamic_slice_in_dim(w, start, depth, 0) for w in (w_gate, w_up)], 1
         )
 
+    pieces = [rows_for(k) for k in range(nx)]
+    w_x = {0: pieces[0], 1: shift(pieces[1], "x", 1), 3: shift(pieces[3], "x", 3)}
     outgoing = local_kernel(
         functools.partial(pack_kernel, (nz, ny)),
         jax.ShapeDtypeStruct((nz * homes * MAIN, span), BF16),
         routes.T,
         tokens,
     )
-    outgoing, w_gate, w_up, norm_gain = lax.optimization_barrier(
-        (outgoing, w_gate, w_up, norm_gain)
-    )
     arrived = lax.all_to_all(
         outgoing.reshape(nz * homes, MAIN, span), DISPATCH, 0, 0, tiled=True
     ).reshape(nz * homes * MAIN, span)
 
-    w_x = {k: shift(piece(k), "x", k) for k in W_ORDER}
-    w_x[0] = piece(0)
-    w_c = {k: shift(w_x[k], "core", 1) for k in (0, 1, 3, 2)}
-    wd_other = shift(w_down, "core", 1)
-    router, gains = local_kernel(
+    router, far_piece = local_kernel(
         router_kernel,
-        [
-            jax.ShapeDtypeStruct((TAIL, cols), BF16),
-            jax.ShapeDtypeStruct((nz, width), F32),
-        ],
-        zhi.astype(jnp.int32)[None],
+        [jax.ShapeDtypeStruct((TAIL, cols), BF16), piece],
         tokens,
         norm_gain[None, :],
+        router_weight.T,
+        outgoing,
+        pieces[2],
+        far=2,
+        far_outs=(1,),
+        aliases={4: 1},
+        flops=WINDOW_FLOPS,
+    )
+    w_x[2] = shift(far_piece, "x", 2)
+    router, w_x[1], w_x[3] = local_kernel(
+        join_kernel,
+        [jax.ShapeDtypeStruct((TAIL, cols), BF16), piece, piece],
+        router,
+        w_x[1],
+        w_x[3],
+        far=2,
+        far_outs=(1, 2),
+        aliases={1: 1, 2: 2},
+    )
+    w_c = {k: shift(w_x[k], "core", 1) for k in (0, 1, 3)}
+    wd_other = shift(w_down, "core", 1)
+    gains, w_x[2] = local_kernel(
+        gains_kernel,
+        [jax.ShapeDtypeStruct((nz, width), F32), piece],
+        at,
+        norm_gain[None, :],
         shift(norm_gain, "zhi", 1)[None, :],
-        router_weight.T,
-        flops=WINDOW_FLOPS,
+        w_x[2],
         smem=1,
-    )
+        far=1,
+        far_outs=(1,),
+        aliases={3: 1},
+    )
+    w_c[2] = shift(w_x[2], "core", 1)
     rows, tail = local_kernel(
         functools.partial(unpack_kernel, homes),
         [
@@ -353,47 +385,43 @@
         gains,
     )
 
-    def partial(k):
-        return local_kernel(
-            partial_kernel,
-            jax.ShapeDtypeStruct((2 * n + 2 * TAIL, cols), BF16),
-            rows,
-            tail,
-            router,
-            w_x[k],
-            w_c[k],
-            far=2,
-            scratch=[
-                pltpu.VMEM((2, nz * width, cols), BF16),
-                pltpu.SemaphoreType.DMA((2,)),
-            ],
-            flops=4 * n * nz * width * cols,
-        )
-
-    got = [shift(partial(k), "x", -k) for k in RS_ORDER] + [partial(0)]
+    block = 2 * n + 2 * TAIL
+    parts = local_kernel(
+        partial_kernel,
+        [jax.ShapeDtypeStruct((nx * block, cols), BF16)],
+        at,
+        rows,
+        tail,
+        router,
+        *[w[k] for k in range(nx) for w in (w_x, w_c)],
+        smem=1,
+        far_outs=(0,),
+        flops=4 * nx * n * depth * cols,
+        scratch=[pltpu.VMEM((nx, block, cols), BF16), pltpu.SemaphoreType.DMA((nx,))],
+    )[0]
+
+    def exchange(stacked):
+        sent = stacked.reshape(nx, -1, stacked.shape[1])
+        return lax.all_to_all(sent, "x", 0, 0, tiled=True).reshape(stacked.shape)
+
     hidden = local_kernel(
-        functools.partial(hidden_kernel, homes * MAIN),
-        jax.ShapeDtypeStruct((2 * n + 2 * TAIL, units), BF16),
-        *got,
-    )
-
-    at = jnp.stack([x, zhi]).astype(jnp.int32)
+        functools.partial(hidden_kernel, homes * MAIN, nx),
+        jax.ShapeDtypeStruct((block, units), BF16),
+        exchange(parts),
+    )
+
     hid_other = shift(hidden, "zhi", 1)
-    own_rows = hidden[: 2 * n]
-    own_side = [own_rows] + [shift(own_rows, "x", k) for k in (1, 2, 3)]
+    own_rows, other_rows = hidden[: 2 * n], hid_other[: 2 * n]
     first = local_kernel(
         functools.partial(down_first_kernel, homes, nx, nz),
         jax.ShapeDtypeStruct((n, width), F32),
         at,
         w_down,
         wd_other,
-        *own_side,
+        *[shift(own_rows, "x", k) if k else own_rows for k in range(nx)],
         flops=2 * n * w_down.size,
-        scratch=[pltpu.VMEM((2 * n, nx * units), BF16)],
         smem=1,
     )
-    other_rows = hid_other[: 2 * n]
-    other_side = [other_rows] + [shift(other_rows, "x", k) for k in (1, 2, 3)]
     back = local_kernel(
         functools.partial(down_last_kernel, homes, nx, nz),
         jax.ShapeDtypeStruct((homes * MAIN, span), BF16),
@@ -401,9 +429,8 @@
         w_down,
         wd_other,
         first,
-        *other_side,
+        *[shift(other_rows, "x", k) if k else other_rows for k in range(nx)],
         flops=2 * n * w_down.size,
-        scratch=[pltpu.VMEM((2 * n, nx * units), BF16)],
         smem=1,
     )
     back, routes = lax.optimization_barrier((back, routes))

time: 170 us -> 162 us (0.953)
  blocking collectives: 0 us -> 20.4 us
  waiting for transfers between devices: 51.4 us -> 31.3 us
  Pallas kernels: 20.2 us -> 15.4 us
    ppermute x19 -> x16, waiting for transfers between devices: 33.8 us -> 8.89 us  [shift(): lax.ppermute(value, axis, [(i, (i + by) % size) for i in range(size)])]
    all_to_all x0 -> x1, blocking collectives: none -> 20.4 us  [exchange(): return lax.all_to_all(sent, 'x', 0, 0, tiled=True).reshape(stacked.shape)]
    all_to_all x1, starting transfers between devices: 9.04 us -> 17.4 us  [shards(): lax.all_to_all(back.reshape(homes, MAIN, span), HOMES, 0, 0, tiled=True)]
    ppermute x19 -> x16, starting transfers between devices: 61.8 us -> 56.1 us  [shift(): lax.ppermute(value, axis, [(i, (i + by) % size) for i in range(size)])]
    pallas_call x12 -> x11, Pallas kernels: 20.2 us -> 15.4 us  [local_kernel(): pl.pallas_call(body, out_shape=out, in_specs=[pl.BlockSpec(memory_space=s...]
    all_to_all x1, waiting for transfers between devices: 0.01 us -> 4.7 us  [shards(): lax.all_to_all(outgoing.reshape(nz * homes, MAIN, span), DISPATCH, 0, 0,...]
    all_to_all x1, starting transfers between devices: 16.8 us -> 13.1 us  [shards(): lax.all_to_all(outgoing.reshape(nz * homes, MAIN, span), DISPATCH, 0, 0,...]
  transfers between devices with their start and end apart: 21 -> 18, of which waited for: 8 -> 6; matrix products, arithmetic and copies ran while one was open for 3% -> 1% of each run, Pallas kernels for 9% -> 8%
where the time goes in v4:
time: 162 us; the launch traced here: 161 us
  starting transfers between devices  86.6 us (53%)
  waiting for transfers between devices  31.3 us (19%)
  blocking collectives  20.4 us (13%)
  Pallas kernels  15.4 us (10%)
  local copies, waits for them, and re-layouts  3.59 us (2%)
  other arithmetic  3.1 us (2%)
    ppermute x16, starting transfers between devices, shift(): lax.ppermute(value, axis, [(i, (i + by) % size) for i in range(size)])  56.1 us
    all_to_all x1, blocking collectives, exchange(): return lax.all_to_all(sent, 'x', 0, 0, tiled=True).reshape(stacked.shape)  20.4 us
    all_to_all x1, waiting for transfers between devices, shards(): lax.all_to_all(back.reshape(homes, MAIN, span), HOMES, 0, 0, tiled=True)  17.7 us
    all_to_all x1, starting transfers between devices, shards(): lax.all_to_all(back.reshape(homes, MAIN, span), HOMES, 0, 0, tiled=True)  17.4 us
    pallas_call x11, Pallas kernels, local_kernel(): pl.pallas_call(body, out_shape=out, in_specs=[pl.BlockSpec(memory_space=s...  15.4 us
    all_to_all x1, starting transfers between devices, shards(): lax.all_to_all(outgoing.reshape(nz * homes, MAIN, span), DISPATCH, 0, 0,...  13.1 us
    ppermute x16, waiting for transfers between devices, shift(): lax.ppermute(value, axis, [(i, (i + by) % size) for i in range(size)])  8.89 us
    all_to_all x1, waiting for transfers between devices, shards(): lax.all_to_all(outgoing.reshape(nz * homes, MAIN, span), DISPATCH, 0, 0,...  4.7 us
  transfers between devices with their start and end apart: 18, of which 6 were waited for; matrix products, arithmetic and copies ran while one was open for 1% of the time, Pallas kernels for 8%

profile of v4, /device:TPU:6, one launch (start us, length us, event | category | flops | bytes accessed | tf_op | source)
XLA Modules:
  0.0 160.7 jit_solution(14967898926722441683)
XLA Ops:
  0.0 2.0 %constant_dynamic-slice_fusion = (bf16[1536,128]{1,0:T(8,128)(2,1)S(1)}, bf16[1536,128]{1,0:T(8,128)(2,1)S(1)}, bf16[1536,128]{1,0:T(8,128)(2,1)S(1)}, bf16[1536...) fusion(bf16[6144,128]{1,0:T(8,128)(2,1)} %param.12, ...), kind=kLoop, calls=%fused_computation.4 | loop fusion | bytes 6291472 | tf_op jit(solution)/shard_map/dynamic_slice | solution.py:324
  3.0 7.7 %collective-permute-start.3 = (bf16[1536,256]{1,0:T(8,128)(2,1)}, bf16[1536,256]{1,0:T(8,128)(2,1)}, u32[]{:S(2)}, u32[]{:S(2)}) collective-permute-start(bf16[1536,256]{1,0:T(8,128)(2,1)} %pad_maximum_fusion.1), channel_id=1, source_target_pairs={{0,2},{2,4},{4,6},{6,0},{1,3},{3,5},{5,7},{7,1},{8,10},{10,12},{12... | collective-permute-start | bytes 2359304 | tf_op jit(solution)/shard_map/ppermute | solution.py:29
  15.1 13.1 %all-to-all-start = ((bf16[64,8,1152]{2,1,0:T(8,128)(2,1)}), bf16[64,8,1152]{2,1,0:T(8,128)(2,1)}, u32[]{:S(2)}, u32[]{:S(2)}) async-start(bf16[64,8,1152]{2,1,0:T(8,128)(2,1)} %bitcast.3), calls=%async_computation | async-start | bytes 2359296 | tf_op jit(solution)/shard_map/all_to_all | solution.py:335
  28.6 3.3 %collective-permute-start.2 = (bf16[1536,256]{1,0:T(8,128)(2,1)S(1)}, bf16[1536,256]{1,0:T(8,128)(2,1)}, u32[]{:S(2)}, u32[]{:S(2)}) collective-permute-start(bf16[1536,256]{1,0:T(8,128)(2,1)S(1)} %get-tuple-element.16), channel_id=1, source_target_pairs={{0,4},{2,6},{4,0},{6,2},{1,5},{3,7},{5,1},{7,3},{8,12},{10,14},{12... | collective-permute-start | bytes 2359304 | tf_op jit(solution)/shard_map/ppermute | solution.py:29
  31.9 7.4 %collective-permute-start.1 = (f32[768]{0:T(1024)S(1)}, f32[768]{0:T(1024)S(1)}, u32[]{:S(2)}, u32[]{:S(2)}) collective-permute-start(f32[768]{0:T(1024)S(1)} %copy-done.9), channel_id=1, source_target_pairs={{0,1},{1,0},{2,3},{3,2},{4,5},{5,4},{6,7},{7,6},{8,9},{9,8},{10,11... | collective-permute-start | bytes 9224 | tf_op jit(solution)/shard_map/ppermute | solution.py:29
  40.3 2.0 %collective-permute-start.5 = (bf16[1536,256]{1,0:T(8,128)(2,1)}, bf16[1536,256]{1,0:T(8,128)(2,1)}, u32[]{:S(2)}, u32[]{:S(2)}) collective-permute-start(bf16[1536,256]{1,0:T(8,128)(2,1)} %pad_maximum_fusion.3.refs_0_), channel_id=1, source_target_pairs={{0,8},{8,0},{1,9},{9,1},{2,10},{10,2},{3,11},{11,3},{4,12},{12,4},... | collective-permute-start | bytes 2359304 | tf_op jit(solution)/shard_map/ppermute | solution.py:29
  42.5 2.4 %collective-permute-start.6 = (bf16[1536,256]{1,0:T(8,128)(2,1)}, bf16[1536,256]{1,0:T(8,128)(2,1)}, u32[]{:S(2)}, u32[]{:S(2)}) collective-permute-start(bf16[1536,256]{1,0:T(8,128)(2,1)} %get-tuple-element.22.refs_2_), channel_id=1, source_target_pairs={{0,8},{8,0},{1,9},{9,1},{2,10},{10,2},{3,11},{11,3},{4,12},{12,4},... | collective-permute-start | bytes 2359304 | tf_op jit(solution)/shard_map/ppermute | solution.py:29
  44.9 1.9 %collective-permute-start.8 = (bf16[1536,256]{1,0:T(8,128)(2,1)}, bf16[1536,256]{1,0:T(8,128)(2,1)}, u32[]{:S(2)}, u32[]{:S(2)}) collective-permute-start(bf16[1536,256]{1,0:T(8,128)(2,1)} %get-tuple-element.24.refs_6_), channel_id=1, source_target_pairs={{0,8},{8,0},{1,9},{9,1},{2,10},{10,2},{3,11},{11,3},{4,12},{12,4},... | collective-permute-start | bytes 2359304 | tf_op jit(solution)/shard_map/ppermute | solution.py:29
  46.8 3.7 %collective-permute-done.2._ = bf16[1536,256]{1,0:T(8,128)(2,1)} collective-permute-done((bf16[1536,256]{1,0:T(8,128)(2,1)S(1)}, bf16[1536,256]{1,0:T(8,128)(2,1)}, u32[]{:S(2)}, u32[]{:S(2)}) %collective-permute-start.2) | collective-permute-done | bytes 786464 | tf_op jit(solution)/shard_map/ppermute | solution.py:29
  51.1 1.9 %collective-permute-start.7 = (bf16[1536,256]{1,0:T(8,128)(2,1)}, bf16[1536,256]{1,0:T(8,128)(2,1)}, u32[]{:S(2)}, u32[]{:S(2)}) collective-permute-start(bf16[1536,256]{1,0:T(8,128)(2,1)} %get-tuple-element.23.refs_4_), channel_id=1, source_target_pairs={{0,8},{8,0},{1,9},{9,1},{2,10},{10,2},{3,11},{11,3},{4,12},{12,4},... | collective-permute-start | bytes 2359304 | tf_op jit(solution)/shard_map/ppermute | solution.py:29
  53.0 2.4 %collective-permute-start = (bf16[1024,768]{1,0:T(8,128)(2,1)S(1)}, bf16[1024,768]{1,0:T(8,128)(2,1)S(1)}, u32[]{:S(2)}, u32[]{:S(2)}) collective-permute-start(bf16[1024,768]{1,0:T(8,128)(2,1)S(1)} %copy-done), channel_id=1, source_target_pairs={{0,8},{8,0},{1,9},{9,1},{2,10},{10,2},{3,11},{11,3},{4,12},{12,4},... | collective-permute-start | bytes 4718600 | tf_op jit(solution)/shard_map/ppermute | solution.py:29
  55.4 4.7 %all-to-all-done = bf16[64,8,1152]{2,1,0:T(8,128)(2,1)} async-done(((bf16[64,8,1152]{2,1,0:T(8,128)(2,1)}), bf16[64,8,1152]{2,1,0:T(8,128)(2,1)}, u32[]{:S(2)}, u32[]{:S(2)}) %all-to-all-start) | async-done | bytes 1179680 | tf_op jit(solution)/shard_map/all_to_all | solution.py:335
  61.9 6.8 %shard_map.78 = bf16[3200,256]{1,0:T(8,128)(2,1)S(1)} custom-call(s32[2]{0:T(128)S(1)} %pad_add_fusion.at_ref, bf16[384,1536]{1,0:T(8,128)(2,1)S(1)} %get-tuple-element.18.rows_ref, bf16[16,256]{1,0:T(8,128)(2,1)S(1)} %get-tuple-element.19.tail_ref, bf16[16,256]{1,0:T(8,128)(2,1)S(1)} %get-tuple-element.21.router_ref, ...), custom_call_target="tpu_custom_call" | custom-call | flops 2415919104 | bytes 9125896 | tf_op jit(solution)/shard_map/pallas_call | solution.py:43
  68.7 20.4 %all_to_all.15 = bf16[4,800,256]{2,1,0:T(8,128)(2,1)S(1)} all-to-all(bf16[4,800,256]{2,1,0:T(8,128)(2,1)S(1)} %bitcast.11), channel_id=1, replica_groups=mesh['zlo'=4,'yh'=2,'yl'=4,'core'=2,'x'=4,'zhi'=2] {'x'}, dimensions={0} | all-to-all | bytes 3276800 | tf_op jit(solution)/shard_map/all_to_all | solution.py:405
  89.5 6.2 %collective-permute-start.12 = (bf16[800,128]{1,0:T(8,128)(2,1)S(1)}, bf16[800,128]{1,0:T(8,128)(2,1)S(1)}, u32[]{:S(2)}, u32[]{:S(2)}) collective-permute-start(bf16[800,128]{1,0:T(8,128)(2,1)S(1)} %shard_map.79.own_ref), channel_id=1, source_target_pairs={{0,1},{1,0},{2,3},{3,2},{4,5},{5,4},{6,7},{7,6},{8,9},{9,8},{10,11... | collective-permute-start | bytes 614408 | tf_op jit(solution)/shard_map/ppermute | solution.py:29
  95.7 4.0 %collective-permute-start.10 = (bf16[768,128]{1,0:T(8,128)(2,1)S(1)}, bf16[768,128]{1,0:T(8,128)(2,1)S(1)}, u32[]{:S(2)}, u32[]{:S(2)}) collective-permute-start(bf16[768,128]{1,0:T(8,128)(2,1)S(1)} %slice.8.refs_0_), channel_id=1, source_target_pairs={{0,4},{2,6},{4,0},{6,2},{1,5},{3,7},{5,1},{7,3},{8,12},{10,14},{12... | collective-permute-start | bytes 589832 | tf_op jit(solution)/shard_map/ppermute | solution.py:29
  99.7 2.8 %collective-permute-start.11 = (bf16[768,128]{1,0:T(8,128)(2,1)S(1)}, bf16[768,128]{1,0:T(8,128)(2,1)S(1)}, u32[]{:S(2)}, u32[]{:S(2)}) collective-permute-start(bf16[768,128]{1,0:T(8,128)(2,1)S(1)} %slice.8.refs_0_), channel_id=1, source_target_pairs={{0,6},{2,0},{4,2},{6,4},{1,7},{3,1},{5,3},{7,5},{8,14},{10,8},{12,... | collective-permute-start | bytes 589832 | tf_op jit(solution)/shard_map/ppermute | solution.py:29
  102.5 4.3 %collective-permute-start.9 = (bf16[768,128]{1,0:T(8,128)(2,1)S(1)}, bf16[768,128]{1,0:T(8,128)(2,1)S(1)}, u32[]{:S(2)}, u32[]{:S(2)}) collective-permute-start(bf16[768,128]{1,0:T(8,128)(2,1)S(1)} %slice.8.refs_0_), channel_id=1, source_target_pairs={{0,2},{2,4},{4,6},{6,0},{1,3},{3,5},{5,7},{7,1},{8,10},{10,12},{12... | collective-permute-start | bytes 589832 | tf_op jit(solution)/shard_map/ppermute | solution.py:29
  106.8 1.9 %collective-permute-start.13 = (bf16[768,128]{1,0:T(8,128)(2,1)S(1)}, bf16[768,128]{1,0:T(8,128)(2,1)S(1)}, u32[]{:S(2)}, u32[]{:S(2)}) collective-permute-start(bf16[768,128]{1,0:T(8,128)(2,1)S(1)} %slice.9.refs_0_), channel_id=1, source_target_pairs={{0,2},{2,4},{4,6},{6,0},{1,3},{3,5},{5,7},{7,1},{8,10},{10,12},{12... | collective-permute-start | bytes 589832 | tf_op jit(solution)/shard_map/ppermute | solution.py:29
  108.7 3.6 %collective-permute-start.14 = (bf16[768,128]{1,0:T(8,128)(2,1)S(1)}, bf16[768,128]{1,0:T(8,128)(2,1)S(1)}, u32[]{:S(2)}, u32[]{:S(2)}) collective-permute-start(bf16[768,128]{1,0:T(8,128)(2,1)S(1)} %slice.9.refs_0_), channel_id=1, source_target_pairs={{0,4},{2,6},{4,0},{6,2},{1,5},{3,7},{5,1},{7,3},{8,12},{10,14},{12... | collective-permute-start | bytes 589832 | tf_op jit(solution)/shard_map/ppermute | solution.py:29
  112.4 2.2 %collective-permute-start.15 = (bf16[768,128]{1,0:T(8,128)(2,1)S(1)}, bf16[768,128]{1,0:T(8,128)(2,1)S(1)}, u32[]{:S(2)}, u32[]{:S(2)}) collective-permute-start(bf16[768,128]{1,0:T(8,128)(2,1)S(1)} %slice.9.refs_0_), channel_id=1, source_target_pairs={{0,6},{2,0},{4,2},{6,4},{1,7},{3,1},{5,3},{7,5},{8,14},{10,8},{12,... | collective-permute-start | bytes 589832 | tf_op jit(solution)/shard_map/ppermute | solution.py:29
  117.9 3.2 %collective-permute-done.15.refs_3_ = bf16[768,128]{1,0:T(8,128)(2,1)S(1)} collective-permute-done((bf16[768,128]{1,0:T(8,128)(2,1)S(1)}, bf16[768,128]{1,0:T(8,128)(2,1)S(1)}, u32[]{:S(2)}, u32[]{:S(2)}) %collective-permute-start.15) | collective-permute-done | bytes 196640 | tf_op jit(solution)/shard_map/ppermute | solution.py:29
  123.7 17.4 %all-to-all-start.2 = ((bf16[32,8,1152]{2,1,0:T(8,128)(2,1)}), bf16[32,8,1152]{2,1,0:T(8,128)(2,1)S(1)}, u32[]{:S(2)}, u32[]{:S(2)}) async-start(bf16[32,8,1152]{2,1,0:T(8,128)(2,1)} %bitcast.13), calls=%async_computation.2 | async-start | bytes 1179648 | tf_op jit(solution)/shard_map/all_to_all | solution.py:437
  142.0 17.7 %all-to-all-done.2 = bf16[32,8,1152]{2,1,0:T(8,128)(2,1)S(1)} async-done(((bf16[32,8,1152]{2,1,0:T(8,128)(2,1)}), bf16[32,8,1152]{2,1,0:T(8,128)(2,1)S(1)}, u32[]{:S(2)}, u32[]{:S(2)}) %all-to-all-start.2) | async-done | bytes 589856 | tf_op jit(solution)/shard_map/all_to_all | solution.py:437
  (54 shorter events, 17.2 us)
Async XLA Ops:
  3.0 39.4 %collective-permute-start.3 = (bf16[1536,256]{1,0:T(8,128)(2,1)}, bf16[1536,256]{1,0:T(8,128)(2,1)}, u32[]{:S(2)}, u32[]{:S(2)}) collective-permute-start(bf16[1536,256]{1,0:T(8,128)(2,1)} %pad_maximum_fusion.1), channel_id=1, source_target_pairs={{0,2},{2,4},{4,6},{6,0},{1,3},{3,5},{5,7},{7,1},{8,10},{10,12},{12... | collective-permute-start | bytes 2359304 | tf_op jit(solution)/shard_map/ppermute | solution.py:29
  11.8 30.6 %collective-permute-start.4 = (bf16[1536,256]{1,0:T(8,128)(2,1)}, bf16[1536,256]{1,0:T(8,128)(2,1)}, u32[]{:S(2)}, u32[]{:S(2)}) collective-permute-start(bf16[1536,256]{1,0:T(8,128)(2,1)} %pad_maximum_fusion.2), channel_id=1, source_target_pairs={{0,6},{2,0},{4,2},{6,4},{1,7},{3,1},{5,3},{7,5},{8,14},{10,8},{12,... | collective-permute-start | bytes 2359304 | tf_op jit(solution)/shard_map/ppermute | solution.py:29
  13.7 14.5 %copy-start.9 = (f32[768]{0:T(1024)S(1)}, f32[768]{0:T(1024)}, u32[]{:S(2)}) copy-start(f32[768]{0:T(1024)} %param.8) | copy-start | bytes 9220
  15.1 13.2 %copy-start.8 = (f32[768,8]{0,1:T(8,128)S(1)}, f32[768,8]{0,1:T(8,128)}, u32[]{:S(2)}) copy-start(f32[768,8]{0,1:T(8,128)} %param.9) | copy-start | bytes 73732
  15.1 45.0 %all-to-all-start = ((bf16[64,8,1152]{2,1,0:T(8,128)(2,1)}), bf16[64,8,1152]{2,1,0:T(8,128)(2,1)}, u32[]{:S(2)}, u32[]{:S(2)}) async-start(bf16[64,8,1152]{2,1,0:T(8,128)(2,1)} %bitcast.3), calls=%async_computation | async-start | bytes 2359296 | tf_op jit(solution)/shard_map/all_to_all | solution.py:335
  28.6 22.0 %collective-permute-start.2 = (bf16[1536,256]{1,0:T(8,128)(2,1)S(1)}, bf16[1536,256]{1,0:T(8,128)(2,1)}, u32[]{:S(2)}, u32[]{:S(2)}) collective-permute-start(bf16[1536,256]{1,0:T(8,128)(2,1)S(1)} %get-tuple-element.16), channel_id=1, source_target_pairs={{0,4},{2,6},{4,0},{6,2},{1,5},{3,7},{5,1},{7,3},{8,12},{10,14},{12... | collective-permute-start | bytes 2359304 | tf_op jit(solution)/shard_map/ppermute | solution.py:29
  31.9 10.5 %collective-permute-start.1 = (f32[768]{0:T(1024)S(1)}, f32[768]{0:T(1024)S(1)}, u32[]{:S(2)}, u32[]{:S(2)}) collective-permute-start(f32[768]{0:T(1024)S(1)} %copy-done.9), channel_id=1, source_target_pairs={{0,1},{1,0},{2,3},{3,2},{4,5},{5,4},{6,7},{7,6},{8,9},{9,8},{10,11... | collective-permute-start | bytes 9224 | tf_op jit(solution)/shard_map/ppermute | solution.py:29
  40.3 12.7 %copy-start = (bf16[1024,768]{1,0:T(8,128)(2,1)S(1)}, bf16[1024,768]{1,0:T(8,128)(2,1)}, u32[]{:S(2)}) copy-start(bf16[1024,768]{1,0:T(8,128)(2,1)} %own_ref.3) | copy-start | bytes 4718596
  40.3 21.6 %collective-permute-start.5 = (bf16[1536,256]{1,0:T(8,128)(2,1)}, bf16[1536,256]{1,0:T(8,128)(2,1)}, u32[]{:S(2)}, u32[]{:S(2)}) collective-permute-start(bf16[1536,256]{1,0:T(8,128)(2,1)} %pad_maximum_fusion.3.refs_0_), channel_id=1, source_target_pairs={{0,8},{8,0},{1,9},{9,1},{2,10},{10,2},{3,11},{11,3},{4,12},{12,4},... | collective-permute-start | bytes 2359304 | tf_op jit(solution)/shard_map/ppermute | solution.py:29
  42.4 19.5 %copy-start.4 = (s32[2]{0:T(128)}, s32[2]{0:T(128)S(1)}, u32[]{:S(2)}) copy-start(s32[2]{0:T(128)S(1)} %pad_add_fusion.at_ref) | copy-start | bytes 28
  42.5 19.5 %collective-permute-start.6 = (bf16[1536,256]{1,0:T(8,128)(2,1)}, bf16[1536,256]{1,0:T(8,128)(2,1)}, u32[]{:S(2)}, u32[]{:S(2)}) collective-permute-start(bf16[1536,256]{1,0:T(8,128)(2,1)} %get-tuple-element.22.refs_2_), channel_id=1, source_target_pairs={{0,8},{8,0},{1,9},{9,1},{2,10},{10,2},{3,11},{11,3},{4,12},{12,4},... | collective-permute-start | bytes 2359304 | tf_op jit(solution)/shard_map/ppermute | solution.py:29
  44.9 17.0 %collective-permute-start.8 = (bf16[1536,256]{1,0:T(8,128)(2,1)}, bf16[1536,256]{1,0:T(8,128)(2,1)}, u32[]{:S(2)}, u32[]{:S(2)}) collective-permute-start(bf16[1536,256]{1,0:T(8,128)(2,1)} %get-tuple-element.24.refs_6_), channel_id=1, source_target_pairs={{0,8},{8,0},{1,9},{9,1},{2,10},{10,2},{3,11},{11,3},{4,12},{12,4},... | collective-permute-start | bytes 2359304 | tf_op jit(solution)/shard_map/ppermute | solution.py:29
  51.1 10.9 %collective-permute-start.7 = (bf16[1536,256]{1,0:T(8,128)(2,1)}, bf16[1536,256]{1,0:T(8,128)(2,1)}, u32[]{:S(2)}, u32[]{:S(2)}) collective-permute-start(bf16[1536,256]{1,0:T(8,128)(2,1)} %get-tuple-element.23.refs_4_), channel_id=1, source_target_pairs={{0,8},{8,0},{1,9},{9,1},{2,10},{10,2},{3,11},{11,3},{4,12},{12,4},... | collective-permute-start | bytes 2359304 | tf_op jit(solution)/shard_map/ppermute | solution.py:29
  53.0 55.7 %collective-permute-start = (bf16[1024,768]{1,0:T(8,128)(2,1)S(1)}, bf16[1024,768]{1,0:T(8,128)(2,1)S(1)}, u32[]{:S(2)}, u32[]{:S(2)}) collective-permute-start(bf16[1024,768]{1,0:T(8,128)(2,1)S(1)} %copy-done), channel_id=1, source_target_pairs={{0,8},{8,0},{1,9},{9,1},{2,10},{10,2},{3,11},{11,3},{4,12},{12,4},... | collective-permute-start | bytes 4718600 | tf_op jit(solution)/shard_map/ppermute | solution.py:29
  89.1 25.5 %copy-start.5 = (s32[2]{0:T(128)S(1)}, s32[2]{0:T(128)}, u32[]{:S(2)}) copy-start(s32[2]{0:T(128)} %copy-done.4) | copy-start | bytes 28
  89.5 17.3 %collective-permute-start.12 = (bf16[800,128]{1,0:T(8,128)(2,1)S(1)}, bf16[800,128]{1,0:T(8,128)(2,1)S(1)}, u32[]{:S(2)}, u32[]{:S(2)}) collective-permute-start(bf16[800,128]{1,0:T(8,128)(2,1)S(1)} %shard_map.79.own_ref), channel_id=1, source_target_pairs={{0,1},{1,0},{2,3},{3,2},{4,5},{5,4},{6,7},{7,6},{8,9},{9,8},{10,11... | collective-permute-start | bytes 614408 | tf_op jit(solution)/shard_map/ppermute | solution.py:29
  95.7 16.6 %collective-permute-start.10 = (bf16[768,128]{1,0:T(8,128)(2,1)S(1)}, bf16[768,128]{1,0:T(8,128)(2,1)S(1)}, u32[]{:S(2)}, u32[]{:S(2)}) collective-permute-start(bf16[768,128]{1,0:T(8,128)(2,1)S(1)} %slice.8.refs_0_), channel_id=1, source_target_pairs={{0,4},{2,6},{4,0},{6,2},{1,5},{3,7},{5,1},{7,3},{8,12},{10,14},{12... | collective-permute-start | bytes 589832 | tf_op jit(solution)/shard_map/ppermute | solution.py:29
  99.7 14.9 %collective-permute-start.11 = (bf16[768,128]{1,0:T(8,128)(2,1)S(1)}, bf16[768,128]{1,0:T(8,128)(2,1)S(1)}, u32[]{:S(2)}, u32[]{:S(2)}) collective-permute-start(bf16[768,128]{1,0:T(8,128)(2,1)S(1)} %slice.8.refs_0_), channel_id=1, source_target_pairs={{0,6},{2,0},{4,2},{6,4},{1,7},{3,1},{5,3},{7,5},{8,14},{10,8},{12,... | collective-permute-start | bytes 589832 | tf_op jit(solution)/shard_map/ppermute | solution.py:29
  102.5 12.2 %collective-permute-start.9 = (bf16[768,128]{1,0:T(8,128)(2,1)S(1)}, bf16[768,128]{1,0:T(8,128)(2,1)S(1)}, u32[]{:S(2)}, u32[]{:S(2)}) collective-permute-start(bf16[768,128]{1,0:T(8,128)(2,1)S(1)} %slice.8.refs_0_), channel_id=1, source_target_pairs={{0,2},{2,4},{4,6},{6,0},{1,3},{3,5},{5,7},{7,1},{8,10},{10,12},{12... | collective-permute-start | bytes 589832 | tf_op jit(solution)/shard_map/ppermute | solution.py:29
  106.8 9.5 %collective-permute-start.13 = (bf16[768,128]{1,0:T(8,128)(2,1)S(1)}, bf16[768,128]{1,0:T(8,128)(2,1)S(1)}, u32[]{:S(2)}, u32[]{:S(2)}) collective-permute-start(bf16[768,128]{1,0:T(8,128)(2,1)S(1)} %slice.9.refs_0_), channel_id=1, source_target_pairs={{0,2},{2,4},{4,6},{6,0},{1,3},{3,5},{5,7},{7,1},{8,10},{10,12},{12... | collective-permute-start | bytes 589832 | tf_op jit(solution)/shard_map/ppermute | solution.py:29
  108.7 9.2 %collective-permute-start.14 = (bf16[768,128]{1,0:T(8,128)(2,1)S(1)}, bf16[768,128]{1,0:T(8,128)(2,1)S(1)}, u32[]{:S(2)}, u32[]{:S(2)}) collective-permute-start(bf16[768,128]{1,0:T(8,128)(2,1)S(1)} %slice.9.refs_0_), channel_id=1, source_target_pairs={{0,4},{2,6},{4,0},{6,2},{1,5},{3,7},{5,1},{7,3},{8,12},{10,14},{12... | collective-permute-start | bytes 589832 | tf_op jit(solution)/shard_map/ppermute | solution.py:29
  112.4 8.8 %collective-permute-start.15 = (bf16[768,128]{1,0:T(8,128)(2,1)S(1)}, bf16[768,128]{1,0:T(8,128)(2,1)S(1)}, u32[]{:S(2)}, u32[]{:S(2)}) collective-permute-start(bf16[768,128]{1,0:T(8,128)(2,1)S(1)} %slice.9.refs_0_), channel_id=1, source_target_pairs={{0,6},{2,0},{4,2},{6,4},{1,7},{3,1},{5,3},{7,5},{8,14},{10,8},{12,... | collective-permute-start | bytes 589832 | tf_op jit(solution)/shard_map/ppermute | solution.py:29
  123.7 36.0 %copy-start.3 = (bf16[32,768]{1,0:T(8,128)(2,1)S(1)}, bf16[32,768]{1,0:T(8,128)(2,1)}, u32[]{:S(2)}) copy-start(bf16[32,768]{1,0:T(8,128)(2,1)} %tok_ref.5) | copy-start | bytes 147460
  123.7 36.0 %all-to-all-start.2 = ((bf16[32,8,1152]{2,1,0:T(8,128)(2,1)}), bf16[32,8,1152]{2,1,0:T(8,128)(2,1)S(1)}, u32[]{:S(2)}, u32[]{:S(2)}) async-start(bf16[32,8,1152]{2,1,0:T(8,128)(2,1)} %bitcast.13), calls=%async_computation.2 | async-start | bytes 1179648 | tf_op jit(solution)/shard_map/all_to_all | solution.py:437
  (4 other events, 24.8 us)

commit v5 on v4

--- a/solution.py
+++ b/solution.py
@@ -217,7 +217,7 @@
     ).astype(BF16)
 
 
-def router_kernel(tok_ref, gain_ref, router_ref, _, __, out_ref, ___):
+def router_kernel(tok_ref, gain_ref, router_ref, _, __, ___, out_ref, *passed):
     values = tok_ref[...].astype(F32)
     count = values.shape[0]
     experts = router_ref.shape[0]
@@ -239,11 +239,11 @@
     out_ref[...] = jnp.concatenate([high, blank, low, blank], 1)
 
 
-def join_kernel(in_ref, _, __, out_ref, *___):
+def join_kernel(in_ref, _, out_ref, __):
     out_ref[...] = in_ref[...]
 
 
-def gains_kernel(at_ref, gain_ref, other_ref, _, out_ref, __):
+def gains_kernel(at_ref, gain_ref, other_ref, _, __, out_ref, *passed):
     mine = iota(out_ref.shape, 0) == at_ref[1]
     out_ref[...] = jnp.where(mine, gain_ref[...], other_ref[...])
 
@@ -318,63 +318,63 @@
     depth = nz * width
     piece = jax.ShapeDtypeStruct((depth, cols), BF16)
 
-    def rows_for(k):
+    def rows_for(k, *ws):
         start = ((x + k) % nx) * depth
-        return jnp.concatenate(
-            [lax.dynamic_slice_in_dim(w, start, depth, 0) for w in (w_gate, w_up)], 1
-        )
-
-    pieces = [rows_for(k) for k in range(nx)]
-    w_x = {0: pieces[0], 1: shift(pieces[1], "x", 1), 3: shift(pieces[3], "x", 3)}
+        return jnp.concatenate([lax.dynamic_slice_in_dim(w, start, depth, 0) for w in ws], 1)
+
+    w_x = {2: shift(rows_for(2, w_gate, w_up), "x", 2)}
     outgoing = local_kernel(
         functools.partial(pack_kernel, (nz, ny)),
         jax.ShapeDtypeStruct((nz * homes * MAIN, span), BF16),
         routes.T,
         tokens,
     )
+    outgoing, w_gate, w_up = lax.optimization_barrier((outgoing, w_gate, w_up))
     arrived = lax.all_to_all(
         outgoing.reshape(nz * homes, MAIN, span), DISPATCH, 0, 0, tiled=True
     ).reshape(nz * homes * MAIN, span)
 
-    router, far_piece = local_kernel(
+    router, right, left = local_kernel(
         router_kernel,
-        [jax.ShapeDtypeStruct((TAIL, cols), BF16), piece],
+        [jax.ShapeDtypeStruct((TAIL, cols), BF16), piece, piece],
         tokens,
         norm_gain[None, :],
         router_weight.T,
         outgoing,
-        pieces[2],
-        far=2,
+        rows_for(1, w_gate, w_up),
+        rows_for(3, w_gate, w_up),
+        far=3,
+        far_outs=(1, 2),
+        aliases={4: 1, 5: 2},
+        flops=WINDOW_FLOPS,
+    )
+    w_x[0] = rows_for(0, w_gate, w_up)
+    w_x[1], w_x[3] = shift(right, "x", 1), shift(left, "x", 3)
+    router, w_x[2] = local_kernel(
+        join_kernel,
+        [jax.ShapeDtypeStruct((TAIL, cols), BF16), piece],
+        router,
+        w_x[2],
+        far=1,
         far_outs=(1,),
-        aliases={4: 1},
-        flops=WINDOW_FLOPS,
-    )
-    w_x[2] = shift(far_piece, "x", 2)
-    router, w_x[1], w_x[3] = local_kernel(
-        join_kernel,
-        [jax.ShapeDtypeStruct((TAIL, cols), BF16), piece, piece],
-        router,
-        w_x[1],
-        w_x[3],
-        far=2,
-        far_outs=(1, 2),
-        aliases={1: 1, 2: 2},
-    )
-    w_c = {k: shift(w_x[k], "core", 1) for k in (0, 1, 3)}
+        aliases={1: 1},
+    )
+    w_c = {k: shift(w_x[k], "core", 1) for k in (2, 0)}
     wd_other = shift(w_down, "core", 1)
-    gains, w_x[2] = local_kernel(
+    gains, w_x[1], w_x[3] = local_kernel(
         gains_kernel,
-        [jax.ShapeDtypeStruct((nz, width), F32), piece],
+        [jax.ShapeDtypeStruct((nz, width), F32), piece, piece],
         at,
         norm_gain[None, :],
         shift(norm_gain, "zhi", 1)[None, :],
-        w_x[2],
+        w_x[1],
+        w_x[3],
         smem=1,
-        far=1,
-        far_outs=(1,),
-        aliases={3: 1},
-    )
-    w_c[2] = shift(w_x[2], "core", 1)
+        far=2,
+        far_outs=(1, 2),
+        aliases={3: 1, 4: 2},
+    )
+    w_c[1], w_c[3] = shift(w_x[1], "core", 1), shift(w_x[3], "core", 1)
     rows, tail = local_kernel(
         functools.partial(unpack_kernel, homes),
         [

time: 162 us -> 157 us (0.969)
  starting transfers between devices: 86.6 us -> 79.3 us
  blocking collectives: 20.4 us -> 24.3 us
    all_to_all x1, starting transfers between devices: 17.4 us -> 9.16 us  [shards(): lax.all_to_all(back.reshape(homes, MAIN, span), HOMES, 0, 0, tiled=True)]
    all_to_all x1, waiting for transfers between devices: 4.7 us -> 0.01 us  [shards(): lax.all_to_all(outgoing.reshape(nz * homes, MAIN, span), DISPATCH, 0, 0,...]
    all_to_all x1, blocking collectives: 20.4 us -> 24.3 us  [exchange(): return lax.all_to_all(sent, 'x', 0, 0, tiled=True).reshape(stacked.shape)]
    ppermute x16, waiting for transfers between devices: 8.89 us -> 12.6 us  [shift(): lax.ppermute(value, axis, [(i, (i + by) % size) for i in range(size)])]
    all_to_all x1, starting transfers between devices: 13.1 us -> 16.8 us  [shards(): lax.all_to_all(outgoing.reshape(nz * homes, MAIN, span), DISPATCH, 0, 0,...]
    ppermute x16, starting transfers between devices: 56.1 us -> 53.3 us  [shift(): lax.ppermute(value, axis, [(i, (i + by) % size) for i in range(size)])]
  transfers between devices with their start and end apart: 18 -> 18, of which waited for: 6 -> 6; matrix products, arithmetic and copies ran while one was open for 1% -> 2% of each run, Pallas kernels for 8% -> 8%
where the time goes in v5:
time: 157 us; the launch traced here: 156 us
  starting transfers between devices  79.3 us (51%)
  waiting for transfers between devices  30.1 us (19%)
  blocking collectives  24.3 us (15%)
  Pallas kernels  15.4 us (10%)
  local copies, waits for them, and re-layouts  4.66 us (3%)
  other arithmetic  2.2 us (1%)
    ppermute x16, starting transfers between devices, shift(): lax.ppermute(value, axis, [(i, (i + by) % size) for i in range(size)])  53.3 us
    all_to_all x1, blocking collectives, exchange(): return lax.all_to_all(sent, 'x', 0, 0, tiled=True).reshape(stacked.shape)  24.3 us
    all_to_all x1, waiting for transfers between devices, shards(): lax.all_to_all(back.reshape(homes, MAIN, span), HOMES, 0, 0, tiled=True)  17.5 us
    all_to_all x1, starting transfers between devices, shards(): lax.all_to_all(outgoing.reshape(nz * homes, MAIN, span), DISPATCH, 0, 0,...  16.8 us
    pallas_call x11, Pallas kernels, local_kernel(): pl.pallas_call(body, out_shape=out, in_specs=[pl.BlockSpec(memory_space=s...  15.4 us
    ppermute x16, waiting for transfers between devices, shift(): lax.ppermute(value, axis, [(i, (i + by) % size) for i in range(size)])  12.6 us
    all_to_all x1, starting transfers between devices, shards(): lax.all_to_all(back.reshape(homes, MAIN, span), HOMES, 0, 0, tiled=True)  9.16 us
  transfers between devices with their start and end apart: 18, of which 6 were waited for; matrix products, arithmetic and copies ran while one was open for 2% of the time, Pallas kernels for 8%

profile of v5, /device:TPU:6, one launch (start us, length us, event | category | flops | bytes accessed | tf_op | source)
XLA Modules:
  0.0 156.4 jit_solution(1768481669277714023)
XLA Ops:
  2.2 3.3 %collective-permute-start.4 = (bf16[1536,256]{1,0:T(8,128)(2,1)}, bf16[1536,256]{1,0:T(8,128)(2,1)}, u32[]{:S(2)}, u32[]{:S(2)}) collective-permute-start(bf16[1536,256]{1,0:T(8,128)(2,1)} %pad_maximum_fusion.2), channel_id=1, source_target_pairs={{0,4},{2,6},{4,0},{6,2},{1,5},{3,7},{5,1},{7,3},{8,12},{10,14},{12... | collective-permute-start | bytes 2359304 | tf_op jit(solution)/shard_map/ppermute | solution.py:29
  6.9 16.8 %all-to-all-start = ((bf16[64,8,1152]{2,1,0:T(8,128)(2,1)}), bf16[64,8,1152]{2,1,0:T(8,128)(2,1)}, u32[]{:S(2)}, u32[]{:S(2)}) async-start(bf16[64,8,1152]{2,1,0:T(8,128)(2,1)} %bitcast.3), calls=%async_computation | async-start | bytes 2359296 | tf_op jit(solution)/shard_map/all_to_all | solution.py:333
  26.1 4.0 %collective-permute-start.2 = (bf16[1536,256]{1,0:T(8,128)(2,1)S(1)}, bf16[1536,256]{1,0:T(8,128)(2,1)}, u32[]{:S(2)}, u32[]{:S(2)}) collective-permute-start(bf16[1536,256]{1,0:T(8,128)(2,1)S(1)} %get-tuple-element.23), channel_id=1, source_target_pairs={{0,2},{2,4},{4,6},{6,0},{1,3},{3,5},{5,7},{7,1},{8,10},{10,12},{12... | collective-permute-start | bytes 2359304 | tf_op jit(solution)/shard_map/ppermute | solution.py:29
  30.1 1.9 %collective-permute-start.3 = (bf16[1536,256]{1,0:T(8,128)(2,1)S(1)}, bf16[1536,256]{1,0:T(8,128)(2,1)}, u32[]{:S(2)}, u32[]{:S(2)}) collective-permute-start(bf16[1536,256]{1,0:T(8,128)(2,1)S(1)} %get-tuple-element.24), channel_id=1, source_target_pairs={{0,6},{2,0},{4,2},{6,4},{1,7},{3,1},{5,3},{7,5},{8,14},{10,8},{12,... | collective-permute-start | bytes 2359304 | tf_op jit(solution)/shard_map/ppermute | solution.py:29
  32.1 7.4 %collective-permute-start.1 = (f32[768]{0:T(1024)S(1)}, f32[768]{0:T(1024)S(1)}, u32[]{:S(2)}, u32[]{:S(2)}) collective-permute-start(f32[768]{0:T(1024)S(1)} %copy-done.10), channel_id=1, source_target_pairs={{0,1},{1,0},{2,3},{3,2},{4,5},{5,4},{6,7},{7,6},{8,9},{9,8},{10,11... | collective-permute-start | bytes 9224 | tf_op jit(solution)/shard_map/ppermute | solution.py:29
  40.5 2.0 %collective-permute-start.5 = (bf16[1536,256]{1,0:T(8,128)(2,1)}, bf16[1536,256]{1,0:T(8,128)(2,1)}, u32[]{:S(2)}, u32[]{:S(2)}) collective-permute-start(bf16[1536,256]{1,0:T(8,128)(2,1)} %pad_maximum_fusion.3.refs_0_), channel_id=1, source_target_pairs={{0,8},{8,0},{1,9},{9,1},{2,10},{10,2},{3,11},{11,3},{4,12},{12,4},... | collective-permute-start | bytes 2359304 | tf_op jit(solution)/shard_map/ppermute | solution.py:29
  42.6 2.4 %collective-permute-start.7 = (bf16[1536,256]{1,0:T(8,128)(2,1)}, bf16[1536,256]{1,0:T(8,128)(2,1)}, u32[]{:S(2)}, u32[]{:S(2)}) collective-permute-start(bf16[1536,256]{1,0:T(8,128)(2,1)} %get-tuple-element.31.refs_4_), channel_id=1, source_target_pairs={{0,8},{8,0},{1,9},{9,1},{2,10},{10,2},{3,11},{11,3},{4,12},{12,4},... | collective-permute-start | bytes 2359304 | tf_op jit(solution)/shard_map/ppermute | solution.py:29
  45.0 1.8 %collective-permute-done.2._ = bf16[1536,256]{1,0:T(8,128)(2,1)} collective-permute-done((bf16[1536,256]{1,0:T(8,128)(2,1)S(1)}, bf16[1536,256]{1,0:T(8,128)(2,1)}, u32[]{:S(2)}, u32[]{:S(2)}) %collective-permute-start.2) | collective-permute-done | bytes 786464 | tf_op jit(solution)/shard_map/ppermute | solution.py:29
  46.8 4.9 %collective-permute-done.3.__ = bf16[1536,256]{1,0:T(8,128)(2,1)} collective-permute-done((bf16[1536,256]{1,0:T(8,128)(2,1)S(1)}, bf16[1536,256]{1,0:T(8,128)(2,1)}, u32[]{:S(2)}, u32[]{:S(2)}) %collective-permute-start.3) | collective-permute-done | bytes 786464 | tf_op jit(solution)/shard_map/ppermute | solution.py:29
  52.3 1.9 %collective-permute-start.6 = (bf16[1536,256]{1,0:T(8,128)(2,1)}, bf16[1536,256]{1,0:T(8,128)(2,1)}, u32[]{:S(2)}, u32[]{:S(2)}) collective-permute-start(bf16[1536,256]{1,0:T(8,128)(2,1)} %get-tuple-element.30.refs_2_), channel_id=1, source_target_pairs={{0,8},{8,0},{1,9},{9,1},{2,10},{10,2},{3,11},{11,3},{4,12},{12,4},... | collective-permute-start | bytes 2359304 | tf_op jit(solution)/shard_map/ppermute | solution.py:29
  54.3 2.4 %collective-permute-start.8 = (bf16[1536,256]{1,0:T(8,128)(2,1)}, bf16[1536,256]{1,0:T(8,128)(2,1)}, u32[]{:S(2)}, u32[]{:S(2)}) collective-permute-start(bf16[1536,256]{1,0:T(8,128)(2,1)} %get-tuple-element.32.refs_6_), channel_id=1, source_target_pairs={{0,8},{8,0},{1,9},{9,1},{2,10},{10,2},{3,11},{11,3},{4,12},{12,4},... | collective-permute-start | bytes 2359304 | tf_op jit(solution)/shard_map/ppermute | solution.py:29
  56.7 1.9 %collective-permute-start = (bf16[1024,768]{1,0:T(8,128)(2,1)S(1)}, bf16[1024,768]{1,0:T(8,128)(2,1)S(1)}, u32[]{:S(2)}, u32[]{:S(2)}) collective-permute-start(bf16[1024,768]{1,0:T(8,128)(2,1)S(1)} %copy-done), channel_id=1, source_target_pairs={{0,8},{8,0},{1,9},{9,1},{2,10},{10,2},{3,11},{11,3},{4,12},{12,4},... | collective-permute-start | bytes 4718600 | tf_op jit(solution)/shard_map/ppermute | solution.py:29
  60.5 6.8 %shard_map.78 = bf16[3200,256]{1,0:T(8,128)(2,1)S(1)} custom-call(s32[2]{0:T(128)S(1)} %pad_add_fusion.at_ref, bf16[384,1536]{1,0:T(8,128)(2,1)S(1)} %get-tuple-element.26.rows_ref, bf16[16,256]{1,0:T(8,128)(2,1)S(1)} %get-tuple-element.27.tail_ref, bf16[16,256]{1,0:T(8,128)(2,1)S(1)} %get-tuple-element.29.router_ref, ...), custom_call_target="tpu_custom_call" | custom-call | flops 2415919104 | bytes 9125896 | tf_op jit(solution)/shard_map/pallas_call | solution.py:43
  67.2 24.3 %all_to_all.15 = bf16[4,800,256]{2,1,0:T(8,128)(2,1)S(1)} all-to-all(bf16[4,800,256]{2,1,0:T(8,128)(2,1)S(1)} %bitcast.11), channel_id=1, replica_groups=mesh['zlo'=4,'yh'=2,'yl'=4,'core'=2,'x'=4,'zhi'=2] {'x'}, dimensions={0} | all-to-all | bytes 3276800 | tf_op jit(solution)/shard_map/all_to_all | solution.py:405
  92.0 7.1 %collective-permute-start.12 = (bf16[800,128]{1,0:T(8,128)(2,1)S(1)}, bf16[800,128]{1,0:T(8,128)(2,1)S(1)}, u32[]{:S(2)}, u32[]{:S(2)}) collective-permute-start(bf16[800,128]{1,0:T(8,128)(2,1)S(1)} %shard_map.79.own_ref), channel_id=1, source_target_pairs={{0,1},{1,0},{2,3},{3,2},{4,5},{5,4},{6,7},{7,6},{8,9},{9,8},{10,11... | collective-permute-start | bytes 614408 | tf_op jit(solution)/shard_map/ppermute | solution.py:29
  99.1 4.0 %collective-permute-start.10 = (bf16[768,128]{1,0:T(8,128)(2,1)S(1)}, bf16[768,128]{1,0:T(8,128)(2,1)S(1)}, u32[]{:S(2)}, u32[]{:S(2)}) collective-permute-start(bf16[768,128]{1,0:T(8,128)(2,1)S(1)} %slice.8.refs_0_), channel_id=1, source_target_pairs={{0,4},{2,6},{4,0},{6,2},{1,5},{3,7},{5,1},{7,3},{8,12},{10,14},{12... | collective-permute-start | bytes 589832 | tf_op jit(solution)/shard_map/ppermute | solution.py:29
  103.1 2.8 %collective-permute-start.11 = (bf16[768,128]{1,0:T(8,128)(2,1)S(1)}, bf16[768,128]{1,0:T(8,128)(2,1)S(1)}, u32[]{:S(2)}, u32[]{:S(2)}) collective-permute-start(bf16[768,128]{1,0:T(8,128)(2,1)S(1)} %slice.8.refs_0_), channel_id=1, source_target_pairs={{0,6},{2,0},{4,2},{6,4},{1,7},{3,1},{5,3},{7,5},{8,14},{10,8},{12,... | collective-permute-start | bytes 589832 | tf_op jit(solution)/shard_map/ppermute | solution.py:29
  105.9 4.3 %collective-permute-start.9 = (bf16[768,128]{1,0:T(8,128)(2,1)S(1)}, bf16[768,128]{1,0:T(8,128)(2,1)S(1)}, u32[]{:S(2)}, u32[]{:S(2)}) collective-permute-start(bf16[768,128]{1,0:T(8,128)(2,1)S(1)} %slice.8.refs_0_), channel_id=1, source_target_pairs={{0,2},{2,4},{4,6},{6,0},{1,3},{3,5},{5,7},{7,1},{8,10},{10,12},{12... | collective-permute-start | bytes 589832 | tf_op jit(solution)/shard_map/ppermute | solution.py:29
  110.2 1.9 %collective-permute-start.13 = (bf16[768,128]{1,0:T(8,128)(2,1)S(1)}, bf16[768,128]{1,0:T(8,128)(2,1)S(1)}, u32[]{:S(2)}, u32[]{:S(2)}) collective-permute-start(bf16[768,128]{1,0:T(8,128)(2,1)S(1)} %slice.9.refs_0_), channel_id=1, source_target_pairs={{0,2},{2,4},{4,6},{6,0},{1,3},{3,5},{5,7},{7,1},{8,10},{10,12},{12... | collective-permute-start | bytes 589832 | tf_op jit(solution)/shard_map/ppermute | solution.py:29
  112.2 3.6 %collective-permute-start.14 = (bf16[768,128]{1,0:T(8,128)(2,1)S(1)}, bf16[768,128]{1,0:T(8,128)(2,1)S(1)}, u32[]{:S(2)}, u32[]{:S(2)}) collective-permute-start(bf16[768,128]{1,0:T(8,128)(2,1)S(1)} %slice.9.refs_0_), channel_id=1, source_target_pairs={{0,4},{2,6},{4,0},{6,2},{1,5},{3,7},{5,1},{7,3},{8,12},{10,14},{12... | collective-permute-start | bytes 589832 | tf_op jit(solution)/shard_map/ppermute | solution.py:29
  115.8 2.2 %collective-permute-start.15 = (bf16[768,128]{1,0:T(8,128)(2,1)S(1)}, bf16[768,128]{1,0:T(8,128)(2,1)S(1)}, u32[]{:S(2)}, u32[]{:S(2)}) collective-permute-start(bf16[768,128]{1,0:T(8,128)(2,1)S(1)} %slice.9.refs_0_), channel_id=1, source_target_pairs={{0,6},{2,0},{4,2},{6,4},{1,7},{3,1},{5,3},{7,5},{8,14},{10,8},{12,... | collective-permute-start | bytes 589832 | tf_op jit(solution)/shard_map/ppermute | solution.py:29
  122.4 2.9 %collective-permute-done.15.refs_3_ = bf16[768,128]{1,0:T(8,128)(2,1)S(1)} collective-permute-done((bf16[768,128]{1,0:T(8,128)(2,1)S(1)}, bf16[768,128]{1,0:T(8,128)(2,1)S(1)}, u32[]{:S(2)}, u32[]{:S(2)}) %collective-permute-start.15) | collective-permute-done | bytes 196640 | tf_op jit(solution)/shard_map/ppermute | solution.py:29
  127.8 9.2 %all-to-all-start.2 = ((bf16[32,8,1152]{2,1,0:T(8,128)(2,1)}), bf16[32,8,1152]{2,1,0:T(8,128)(2,1)S(1)}, u32[]{:S(2)}, u32[]{:S(2)}) async-start(bf16[32,8,1152]{2,1,0:T(8,128)(2,1)} %bitcast.13), calls=%async_computation.2 | async-start | bytes 1179648 | tf_op jit(solution)/shard_map/all_to_all | solution.py:437
  137.9 17.5 %all-to-all-done.2 = bf16[32,8,1152]{2,1,0:T(8,128)(2,1)S(1)} async-done(((bf16[32,8,1152]{2,1,0:T(8,128)(2,1)}), bf16[32,8,1152]{2,1,0:T(8,128)(2,1)S(1)}, u32[]{:S(2)}, u32[]{:S(2)}) %all-to-all-start.2) | async-done | bytes 589856 | tf_op jit(solution)/shard_map/all_to_all | solution.py:437
  (57 shorter events, 18.5 us)
Async XLA Ops:
  2.2 40.4 %collective-permute-start.4 = (bf16[1536,256]{1,0:T(8,128)(2,1)}, bf16[1536,256]{1,0:T(8,128)(2,1)}, u32[]{:S(2)}, u32[]{:S(2)}) collective-permute-start(bf16[1536,256]{1,0:T(8,128)(2,1)} %pad_maximum_fusion.2), channel_id=1, source_target_pairs={{0,4},{2,6},{4,0},{6,2},{1,5},{3,7},{5,1},{7,3},{8,12},{10,14},{12... | collective-permute-start | bytes 2359304 | tf_op jit(solution)/shard_map/ppermute | solution.py:29
  5.5 18.3 %copy-start.10 = (f32[768]{0:T(1024)S(1)}, f32[768]{0:T(1024)}, u32[]{:S(2)}) copy-start(f32[768]{0:T(1024)} %param.8) | copy-start | bytes 9220
  5.5 18.3 %copy-start.9 = (bf16[6144,128]{1,0:T(8,128)(2,1)S(1)}, bf16[6144,128]{1,0:T(8,128)(2,1)}, u32[]{:S(2)}) copy-start(bf16[6144,128]{1,0:T(8,128)(2,1)} %param.12) | copy-start | bytes 4718596
  6.9 51.8 %all-to-all-start = ((bf16[64,8,1152]{2,1,0:T(8,128)(2,1)}), bf16[64,8,1152]{2,1,0:T(8,128)(2,1)}, u32[]{:S(2)}, u32[]{:S(2)}) async-start(bf16[64,8,1152]{2,1,0:T(8,128)(2,1)} %bitcast.3), calls=%async_computation | async-start | bytes 2359296 | tf_op jit(solution)/shard_map/all_to_all | solution.py:333
  26.1 20.7 %collective-permute-start.2 = (bf16[1536,256]{1,0:T(8,128)(2,1)S(1)}, bf16[1536,256]{1,0:T(8,128)(2,1)}, u32[]{:S(2)}, u32[]{:S(2)}) collective-permute-start(bf16[1536,256]{1,0:T(8,128)(2,1)S(1)} %get-tuple-element.23), channel_id=1, source_target_pairs={{0,2},{2,4},{4,6},{6,0},{1,3},{3,5},{5,7},{7,1},{8,10},{10,12},{12... | collective-permute-start | bytes 2359304 | tf_op jit(solution)/shard_map/ppermute | solution.py:29
  30.1 21.7 %collective-permute-start.3 = (bf16[1536,256]{1,0:T(8,128)(2,1)S(1)}, bf16[1536,256]{1,0:T(8,128)(2,1)}, u32[]{:S(2)}, u32[]{:S(2)}) collective-permute-start(bf16[1536,256]{1,0:T(8,128)(2,1)S(1)} %get-tuple-element.24), channel_id=1, source_target_pairs={{0,6},{2,0},{4,2},{6,4},{1,7},{3,1},{5,3},{7,5},{8,14},{10,8},{12,... | collective-permute-start | bytes 2359304 | tf_op jit(solution)/shard_map/ppermute | solution.py:29
  32.1 10.5 %collective-permute-start.1 = (f32[768]{0:T(1024)S(1)}, f32[768]{0:T(1024)S(1)}, u32[]{:S(2)}, u32[]{:S(2)}) collective-permute-start(f32[768]{0:T(1024)S(1)} %copy-done.10), channel_id=1, source_target_pairs={{0,1},{1,0},{2,3},{3,2},{4,5},{5,4},{6,7},{7,6},{8,9},{9,8},{10,11... | collective-permute-start | bytes 9224 | tf_op jit(solution)/shard_map/ppermute | solution.py:29
  40.5 16.2 %copy-start = (bf16[1024,768]{1,0:T(8,128)(2,1)S(1)}, bf16[1024,768]{1,0:T(8,128)(2,1)}, u32[]{:S(2)}) copy-start(bf16[1024,768]{1,0:T(8,128)(2,1)} %own_ref.3) | copy-start | bytes 4718596
  40.5 20.0 %collective-permute-start.5 = (bf16[1536,256]{1,0:T(8,128)(2,1)}, bf16[1536,256]{1,0:T(8,128)(2,1)}, u32[]{:S(2)}, u32[]{:S(2)}) collective-permute-start(bf16[1536,256]{1,0:T(8,128)(2,1)} %pad_maximum_fusion.3.refs_0_), channel_id=1, source_target_pairs={{0,8},{8,0},{1,9},{9,1},{2,10},{10,2},{3,11},{11,3},{4,12},{12,4},... | collective-permute-start | bytes 2359304 | tf_op jit(solution)/shard_map/ppermute | solution.py:29
  42.6 17.9 %copy-start.4 = (s32[2]{0:T(128)}, s32[2]{0:T(128)S(1)}, u32[]{:S(2)}) copy-start(s32[2]{0:T(128)S(1)} %pad_add_fusion.at_ref) | copy-start | bytes 28
  42.6 17.8 %collective-permute-start.7 = (bf16[1536,256]{1,0:T(8,128)(2,1)}, bf16[1536,256]{1,0:T(8,128)(2,1)}, u32[]{:S(2)}, u32[]{:S(2)}) collective-permute-start(bf16[1536,256]{1,0:T(8,128)(2,1)} %get-tuple-element.31.refs_4_), channel_id=1, source_target_pairs={{0,8},{8,0},{1,9},{9,1},{2,10},{10,2},{3,11},{11,3},{4,12},{12,4},... | collective-permute-start | bytes 2359304 | tf_op jit(solution)/shard_map/ppermute | solution.py:29
  52.3 8.1 %collective-permute-start.6 = (bf16[1536,256]{1,0:T(8,128)(2,1)}, bf16[1536,256]{1,0:T(8,128)(2,1)}, u32[]{:S(2)}, u32[]{:S(2)}) collective-permute-start(bf16[1536,256]{1,0:T(8,128)(2,1)} %get-tuple-element.30.refs_2_), channel_id=1, source_target_pairs={{0,8},{8,0},{1,9},{9,1},{2,10},{10,2},{3,11},{11,3},{4,12},{12,4},... | collective-permute-start | bytes 2359304 | tf_op jit(solution)/shard_map/ppermute | solution.py:29
  54.3 6.2 %collective-permute-start.8 = (bf16[1536,256]{1,0:T(8,128)(2,1)}, bf16[1536,256]{1,0:T(8,128)(2,1)}, u32[]{:S(2)}, u32[]{:S(2)}) collective-permute-start(bf16[1536,256]{1,0:T(8,128)(2,1)} %get-tuple-element.32.refs_6_), channel_id=1, source_target_pairs={{0,8},{8,0},{1,9},{9,1},{2,10},{10,2},{3,11},{11,3},{4,12},{12,4},... | collective-permute-start | bytes 2359304 | tf_op jit(solution)/shard_map/ppermute | solution.py:29
  56.7 55.5 %collective-permute-start = (bf16[1024,768]{1,0:T(8,128)(2,1)S(1)}, bf16[1024,768]{1,0:T(8,128)(2,1)S(1)}, u32[]{:S(2)}, u32[]{:S(2)}) collective-permute-start(bf16[1024,768]{1,0:T(8,128)(2,1)S(1)} %copy-done), channel_id=1, source_target_pairs={{0,8},{8,0},{1,9},{9,1},{2,10},{10,2},{3,11},{11,3},{4,12},{12,4},... | collective-permute-start | bytes 4718600 | tf_op jit(solution)/shard_map/ppermute | solution.py:29
  91.6 26.5 %copy-start.5 = (s32[2]{0:T(128)S(1)}, s32[2]{0:T(128)}, u32[]{:S(2)}) copy-start(s32[2]{0:T(128)} %copy-done.4) | copy-start | bytes 28
  92.0 18.2 %collective-permute-start.12 = (bf16[800,128]{1,0:T(8,128)(2,1)S(1)}, bf16[800,128]{1,0:T(8,128)(2,1)S(1)}, u32[]{:S(2)}, u32[]{:S(2)}) collective-permute-start(bf16[800,128]{1,0:T(8,128)(2,1)S(1)} %shard_map.79.own_ref), channel_id=1, source_target_pairs={{0,1},{1,0},{2,3},{3,2},{4,5},{5,4},{6,7},{7,6},{8,9},{9,8},{10,11... | collective-permute-start | bytes 614408 | tf_op jit(solution)/shard_map/ppermute | solution.py:29
  99.1 16.6 %collective-permute-start.10 = (bf16[768,128]{1,0:T(8,128)(2,1)S(1)}, bf16[768,128]{1,0:T(8,128)(2,1)S(1)}, u32[]{:S(2)}, u32[]{:S(2)}) collective-permute-start(bf16[768,128]{1,0:T(8,128)(2,1)S(1)} %slice.8.refs_0_), channel_id=1, source_target_pairs={{0,4},{2,6},{4,0},{6,2},{1,5},{3,7},{5,1},{7,3},{8,12},{10,14},{12... | collective-permute-start | bytes 589832 | tf_op jit(solution)/shard_map/ppermute | solution.py:29
  103.1 14.9 %collective-permute-start.11 = (bf16[768,128]{1,0:T(8,128)(2,1)S(1)}, bf16[768,128]{1,0:T(8,128)(2,1)S(1)}, u32[]{:S(2)}, u32[]{:S(2)}) collective-permute-start(bf16[768,128]{1,0:T(8,128)(2,1)S(1)} %slice.8.refs_0_), channel_id=1, source_target_pairs={{0,6},{2,0},{4,2},{6,4},{1,7},{3,1},{5,3},{7,5},{8,14},{10,8},{12,... | collective-permute-start | bytes 589832 | tf_op jit(solution)/shard_map/ppermute | solution.py:29
  105.9 12.2 %collective-permute-start.9 = (bf16[768,128]{1,0:T(8,128)(2,1)S(1)}, bf16[768,128]{1,0:T(8,128)(2,1)S(1)}, u32[]{:S(2)}, u32[]{:S(2)}) collective-permute-start(bf16[768,128]{1,0:T(8,128)(2,1)S(1)} %slice.8.refs_0_), channel_id=1, source_target_pairs={{0,2},{2,4},{4,6},{6,0},{1,3},{3,5},{5,7},{7,1},{8,10},{10,12},{12... | collective-permute-start | bytes 589832 | tf_op jit(solution)/shard_map/ppermute | solution.py:29
  110.2 11.0 %collective-permute-start.13 = (bf16[768,128]{1,0:T(8,128)(2,1)S(1)}, bf16[768,128]{1,0:T(8,128)(2,1)S(1)}, u32[]{:S(2)}, u32[]{:S(2)}) collective-permute-start(bf16[768,128]{1,0:T(8,128)(2,1)S(1)} %slice.9.refs_0_), channel_id=1, source_target_pairs={{0,2},{2,4},{4,6},{6,0},{1,3},{3,5},{5,7},{7,1},{8,10},{10,12},{12... | collective-permute-start | bytes 589832 | tf_op jit(solution)/shard_map/ppermute | solution.py:29
  112.2 10.3 %collective-permute-start.14 = (bf16[768,128]{1,0:T(8,128)(2,1)S(1)}, bf16[768,128]{1,0:T(8,128)(2,1)S(1)}, u32[]{:S(2)}, u32[]{:S(2)}) collective-permute-start(bf16[768,128]{1,0:T(8,128)(2,1)S(1)} %slice.9.refs_0_), channel_id=1, source_target_pairs={{0,4},{2,6},{4,0},{6,2},{1,5},{3,7},{5,1},{7,3},{8,12},{10,14},{12... | collective-permute-start | bytes 589832 | tf_op jit(solution)/shard_map/ppermute | solution.py:29
  115.8 9.5 %collective-permute-start.15 = (bf16[768,128]{1,0:T(8,128)(2,1)S(1)}, bf16[768,128]{1,0:T(8,128)(2,1)S(1)}, u32[]{:S(2)}, u32[]{:S(2)}) collective-permute-start(bf16[768,128]{1,0:T(8,128)(2,1)S(1)} %slice.9.refs_0_), channel_id=1, source_target_pairs={{0,6},{2,0},{4,2},{6,4},{1,7},{3,1},{5,3},{7,5},{8,14},{10,8},{12,... | collective-permute-start | bytes 589832 | tf_op jit(solution)/shard_map/ppermute | solution.py:29
  127.8 27.5 %copy-start.3 = (bf16[32,768]{1,0:T(8,128)(2,1)S(1)}, bf16[32,768]{1,0:T(8,128)(2,1)}, u32[]{:S(2)}) copy-start(bf16[32,768]{1,0:T(8,128)(2,1)} %tok_ref.5) | copy-start | bytes 147460
  127.8 27.5 %all-to-all-start.2 = ((bf16[32,8,1152]{2,1,0:T(8,128)(2,1)}), bf16[32,8,1152]{2,1,0:T(8,128)(2,1)S(1)}, u32[]{:S(2)}, u32[]{:S(2)}) async-start(bf16[32,8,1152]{2,1,0:T(8,128)(2,1)} %bitcast.13), calls=%async_computation.2 | async-start | bytes 1179648 | tf_op jit(solution)/shard_map/all_to_all | solution.py:437
  (5 other events, 13.2 us)

commit v6 on v5

--- a/solution.py
+++ b/solution.py
@@ -11,6 +11,7 @@
 CAP = 12
 MAIN = 8
 REST = CAP - MAIN
+SIDE = 128
 TAIL = 16
 
 epsilon = 1e-05
@@ -68,9 +69,15 @@
     return (same & (a % (2 * REST) // REST == half)).astype(F32).astype(BF16)
 
 
-def pack_kernel(fan, routes_ref, tok_ref, out_ref):
+def split(values):
+    high = values.astype(BF16)
+    return high, (values - high.astype(F32)).astype(BF16)
+
+
+def pack_kernel(fan, routes_ref, tok_ref, gain_ref, out_ref):
     count, width = tok_ref.shape
     half = width // 2
+    span = width + half
     first, second = routes_ref[0:1, :], routes_ref[1:2, :]
     experts = out_ref.shape[0] // (fan[0] * fan[1] * MAIN)
     n = experts * MAIN
@@ -82,48 +89,57 @@
     pick_main = jnp.where(slot == place, named, 0.0).astype(BF16)
     rest_place = (MAIN + row % REST).astype(F32)
     pick_rest = jnp.where(slot == rest_place, named, 0.0).astype(BF16)
-    tok = tok_ref[...]
+    values = tok_ref[...].astype(F32)
+    tok = (values * gain_ref[...]).astype(BF16)
+    high, low = split(jnp.sum(values * values, 1, keepdims=True))
+    lane = iota((count, SIDE), 1)
+    zero = jnp.zeros((count, SIDE), F32)
+    high, low = high.astype(F32) + zero, low.astype(F32) + zero
+    side = 0.0
+    for pick, at in ((pick_main, 0), (pick_rest, 2)):
+        lanes = jnp.where(lane == at, high, jnp.where(lane == at + 1, low, 0.0))
+        side += dot(pick, lanes.astype(BF16))
     main = dot(pick_main, tok).astype(BF16)
     rest = dot(pick_rest, tok)
     is_first = iota((n, half), 0) % MAIN < REST
     rest = jnp.where(is_first, rest[:, :half], rest[:, half:]).astype(BF16)
+    side = side.astype(BF16)
     for e in range(experts):
         block = slice(e * MAIN, (e + 1) * MAIN)
-        main_e = jnp.concatenate([main[block]] * fan[1], 0)
-        rest_e = jnp.concatenate([rest[block]] * fan[1], 0)
+        parts = [jnp.concatenate([p[block]] * fan[1], 0) for p in (main, rest, side)]
         for z in range(fan[0]):
             at = pl.ds((z * experts + e) * fan[1] * MAIN, fan[1] * MAIN)
-            out_ref[at, :width] = main_e
-            out_ref[at, width:] = rest_e
-
-
-def unpack_kernel(homes, in_ref, gain_ref, rows_ref, tail_ref):
-    width = gain_ref.shape[1]
+            out_ref[at, :width] = parts[0]
+            out_ref[at, width:span] = parts[1]
+            out_ref[at, span:] = parts[2]
+
+
+def unpack_kernel(homes, width, in_ref, rows_ref, tail_ref):
     half = width // 2
+    span = width + half
     n_main, n_rest = homes * MAIN, homes * REST
-    squares_main = jnp.zeros((n_main, 1), F32)
-    squares_rest = jnp.zeros((n_rest, 1), F32)
+    squares = jnp.zeros((n_main, SIDE), F32)
     picks = [rest_pick(homes, h, False) for h in range(2)]
     for z in range(2):
         block = pl.ds(z * n_main, n_main)
-        gain = gain_ref[z : z + 1, :]
-        main = in_ref[block, :width].astype(F32)
-        rows_ref[:n_main, z * width : (z + 1) * width] = (main * gain).astype(BF16)
-        squares_main += jnp.sum(main * main, 1, keepdims=True)
-        halves = in_ref[block, width:]
+        rows_ref[:n_main, z * width : (z + 1) * width] = in_ref[block, :width]
+        halves = in_ref[block, width:span]
         for h in range(2):
-            rest = dot(picks[h], halves)
             at = slice(z * width + h * half, z * width + (h + 1) * half)
-            rows_ref[n_main:, at] = (rest * gain[:, h * half : (h + 1) * half]).astype(BF16)
-            squares_rest += jnp.sum(rest * rest, 1, keepdims=True)
+            rows_ref[n_main:, at] = dot(picks[h], halves).astype(BF16)
+        squares += in_ref[block, span:].astype(F32)
+    squares_main = squares[:, 0:1] + squares[:, 1:2]
+    of_first = (iota((n_main, 1), 0) % MAIN < REST).astype(F32)
+    squares_rest = (squares[:, 2:3] + squares[:, 3:4]) * of_first
 
     def lanes(column):
         n = column.shape[0]
         return jnp.sum(jnp.where(iota((n, n), 0) == iota((n, n), 1), column, 0.0), 0, keepdims=True)
 
     a = lanes(squares_main)
-    b = lanes(squares_rest)
-    b = jnp.concatenate([b, jnp.zeros((1, n_main - n_rest), F32)], 1)
+    source, lane = iota((n_main, n_main), 0), iota((n_main, n_main), 1)
+    same = (source // MAIN == lane // REST) & (source % MAIN == lane % REST) & (lane < n_rest)
+    b = jnp.sum(jnp.where(same, squares_rest, 0.0), 0, keepdims=True)
     row = iota((TAIL, n_main), 0)
     a_hi, b_hi = a.astype(BF16).astype(F32), b.astype(BF16).astype(F32)
     tail = jnp.where(row == 0, a_hi, jnp.where(row == 1, a - a_hi, 0.0))
@@ -131,33 +147,21 @@
     tail_ref[...] = tail.astype(BF16)
 
 
-def partial_kernel(at_ref, rows_ref, tail_ref, router_ref, *refs):
-    weights, (out_ref, parts_ref, sems) = refs[:-3], refs[-3:]
+def partial_kernel(rows_ref, tail_ref, router_ref, own_ref, other_ref, out_ref):
     n = rows_ref.shape[0]
-    block = 2 * n + 2 * TAIL
-    nx = len(weights) // 2
-    sent = []
-    for k in range(nx):
-        for c in range(2):
-            part = dot(rows_ref[...], weights[2 * k + c][...])
-            parts_ref[k, c * n : (c + 1) * n, :] = part.astype(BF16)
-        parts_ref[k, 2 * n : 2 * n + TAIL, :] = tail_ref[...]
-        parts_ref[k, 2 * n + TAIL :, :] = router_ref[...]
-        to = pl.multiple_of((at_ref[0] + nx - k) % nx * block, block)
-        copy = pltpu.make_async_copy(parts_ref.at[k], out_ref.at[pl.ds(to, block), :], sems.at[k])
-        copy.start()
-        sent.append(copy)
-    for copy in sent:
-        copy.wait()
-
-
-def hidden_kernel(n_main, nx, in_ref, out_ref):
+    for c, w_ref in enumerate((own_ref, other_ref)):
+        out_ref[c * n : (c + 1) * n, :] = dot(rows_ref[...], w_ref[...]).astype(BF16)
+    out_ref[2 * n : 2 * n + TAIL, :] = tail_ref[...]
+    out_ref[2 * n + TAIL :, :] = router_ref[...]
+
+
+def hidden_kernel(n_main, *refs):
+    out_ref = refs[-1]
     units = out_ref.shape[1]
     n = (out_ref.shape[0] - 2 * TAIL) // 2
-    block = 2 * n + 2 * TAIL
 
     def total(at, rows):
-        parts = [in_ref[i * block + at : i * block + at + rows, :].astype(F32) for i in range(nx)]
+        parts = [r[at : at + rows, :].astype(F32) for r in refs[:-1]]
         return sum(parts[1:], parts[0])
 
     router = total(2 * n + TAIL, TAIL)
@@ -217,7 +221,8 @@
     ).astype(BF16)
 
 
-def router_kernel(tok_ref, gain_ref, router_ref, _, __, ___, out_ref, *passed):
+def router_kernel(_, tok_ref, gain_ref, router_ref, *refs):
+    out_ref = refs[4]
     values = tok_ref[...].astype(F32)
     count = values.shape[0]
     experts = router_ref.shape[0]
@@ -241,11 +246,6 @@
 
 def join_kernel(in_ref, _, out_ref, __):
     out_ref[...] = in_ref[...]
-
-
-def gains_kernel(at_ref, gain_ref, other_ref, _, __, out_ref, *passed):
-    mine = iota(out_ref.shape, 0) == at_ref[1]
-    out_ref[...] = jnp.where(mine, gain_ref[...], other_ref[...])
 
 
 def weights_kernel(experts, routes_ref, own_ref, other_ref, out_ref):
@@ -325,30 +325,33 @@
     w_x = {2: shift(rows_for(2, w_gate, w_up), "x", 2)}
     outgoing = local_kernel(
         functools.partial(pack_kernel, (nz, ny)),
-        jax.ShapeDtypeStruct((nz * homes * MAIN, span), BF16),
+        jax.ShapeDtypeStruct((nz * homes * MAIN, span + SIDE), BF16),
         routes.T,
         tokens,
+        norm_gain[None, :],
     )
     outgoing, w_gate, w_up = lax.optimization_barrier((outgoing, w_gate, w_up))
     arrived = lax.all_to_all(
-        outgoing.reshape(nz * homes, MAIN, span), DISPATCH, 0, 0, tiled=True
-    ).reshape(nz * homes * MAIN, span)
-
-    router, right, left = local_kernel(
+        outgoing.reshape(nz * homes, MAIN, span + SIDE), DISPATCH, 0, 0, tiled=True
+    ).reshape(nz * homes * MAIN, span + SIDE)
+
+    router, right, left, w_x[0] = local_kernel(
         router_kernel,
-        [jax.ShapeDtypeStruct((TAIL, cols), BF16), piece, piece],
+        [jax.ShapeDtypeStruct((TAIL, cols), BF16), piece, piece, piece],
+        at,
         tokens,
         norm_gain[None, :],
         router_weight.T,
         outgoing,
         rows_for(1, w_gate, w_up),
         rows_for(3, w_gate, w_up),
-        far=3,
-        far_outs=(1, 2),
-        aliases={4: 1, 5: 2},
+        rows_for(0, w_gate, w_up),
+        smem=1,
+        far=4,
+        far_outs=(1, 2, 3),
+        aliases={5: 1, 6: 2, 7: 3},
         flops=WINDOW_FLOPS,
     )
-    w_x[0] = rows_for(0, w_gate, w_up)
     w_x[1], w_x[3] = shift(right, "x", 1), shift(left, "x", 3)
     router, w_x[2] = local_kernel(
         join_kernel,
@@ -360,54 +363,37 @@
         aliases={1: 1},
     )
     w_c = {k: shift(w_x[k], "core", 1) for k in (2, 0)}
-    wd_other = shift(w_down, "core", 1)
-    gains, w_x[1], w_x[3] = local_kernel(
-        gains_kernel,
-        [jax.ShapeDtypeStruct((nz, width), F32), piece, piece],
-        at,
-        norm_gain[None, :],
-        shift(norm_gain, "zhi", 1)[None, :],
-        w_x[1],
-        w_x[3],
-        smem=1,
-        far=2,
-        far_outs=(1, 2),
-        aliases={3: 1, 4: 2},
-    )
     w_c[1], w_c[3] = shift(w_x[1], "core", 1), shift(w_x[3], "core", 1)
     rows, tail = local_kernel(
-        functools.partial(unpack_kernel, homes),
+        functools.partial(unpack_kernel, homes, width),
         [
             jax.ShapeDtypeStruct((n, nz * width), BF16),
             jax.ShapeDtypeStruct((TAIL, homes * MAIN), BF16),
         ],
         arrived,
-        gains,
     )
 
     block = 2 * n + 2 * TAIL
-    parts = local_kernel(
-        partial_kernel,
-        [jax.ShapeDtypeStruct((nx * block, cols), BF16)],
-        at,
-        rows,
-        tail,
-        router,
-        *[w[k] for k in range(nx) for w in (w_x, w_c)],
-        smem=1,
-        far_outs=(0,),
-        flops=4 * nx * n * depth * cols,
-        scratch=[pltpu.VMEM((nx, block, cols), BF16), pltpu.SemaphoreType.DMA((nx,))],
-    )[0]
-
-    def exchange(stacked):
-        sent = stacked.reshape(nx, -1, stacked.shape[1])
-        return lax.all_to_all(sent, "x", 0, 0, tiled=True).reshape(stacked.shape)
+    def partial(k):
+        return local_kernel(
+            partial_kernel,
+            jax.ShapeDtypeStruct((block, cols), BF16),
+            rows,
+            tail,
+            router,
+            w_x[k],
+            w_c[k],
+            flops=4 * n * depth * cols,
+        )
+
+    mine = partial(0)
+    got = [shift(partial(k), "x", -k) for k in (1, 3, 2)] + [mine]
+    wd_other = shift(w_down, "core", 1)
 
     hidden = local_kernel(
-        functools.partial(hidden_kernel, homes * MAIN, nx),
+        functools.partial(hidden_kernel, homes * MAIN),
         jax.ShapeDtypeStruct((block, units), BF16),
-        exchange(parts),
+        *got,
     )
 
     hid_other = shift(hidden, "zhi", 1)

time: 157 us -> 152 us (0.968)
  blocking collectives: 24.3 us -> 0 us
  waiting for transfers between devices: 30.1 us -> 43.3 us
  starting transfers between devices: 79.3 us -> 83.2 us
  Pallas kernels: 15.4 us -> 17.1 us
    all_to_all x1 -> x0, blocking collectives: 24.3 us -> none  [exchange(): return lax.all_to_all(sent, 'x', 0, 0, tiled=True).reshape(stacked.shape)]
    ppermute x16 -> x18, waiting for transfers between devices: 12.6 us -> 21.7 us  [shift(): lax.ppermute(value, axis, [(i, (i + by) % size) for i in range(size)])]
    all_to_all x1, waiting for transfers between devices: 0.01 us -> 3.94 us  [shards(): lax.all_to_all(outgoing.reshape(nz * homes, MAIN, span + SIDE), DISPATCH,...]
    ppermute x16 -> x18, starting transfers between devices: 53.3 us -> 56.6 us  [shift(): lax.ppermute(value, axis, [(i, (i + by) % size) for i in range(size)])]
    pallas_call x11 -> x13, Pallas kernels: 15.4 us -> 17.1 us  [local_kernel(): pl.pallas_call(body, out_shape=out, in_specs=[pl.BlockSpec(memory_space=s...]
  transfers between devices with their start and end apart: 18 -> 20, of which waited for: 6 -> 7; matrix products, arithmetic and copies ran while one was open for 2% -> 1% of each run, Pallas kernels for 8% -> 10%
where the time goes in v6:
time: 152 us; the launch traced here: 150 us
  starting transfers between devices  83.2 us (55%)
  waiting for transfers between devices  43.3 us (28%)
  Pallas kernels  17.1 us (11%)
  local copies, waits for them, and re-layouts  3.49 us (2%)
  other arithmetic  2.28 us (1%)
    ppermute x18, starting transfers between devices, shift(): lax.ppermute(value, axis, [(i, (i + by) % size) for i in range(size)])  56.6 us
    ppermute x18, waiting for transfers between devices, shift(): lax.ppermute(value, axis, [(i, (i + by) % size) for i in range(size)])  21.7 us
    all_to_all x1, waiting for transfers between devices, shards(): lax.all_to_all(back.reshape(homes, MAIN, span), HOMES, 0, 0, tiled=True)  17.7 us
    pallas_call x13, Pallas kernels, local_kernel(): pl.pallas_call(body, out_shape=out, in_specs=[pl.BlockSpec(memory_space=s...  17.1 us
    all_to_all x1, starting transfers between devices, shards(): lax.all_to_all(outgoing.reshape(nz * homes, MAIN, span + SIDE), DISPATCH,...  16.9 us
    all_to_all x1, starting transfers between devices, shards(): lax.all_to_all(back.reshape(homes, MAIN, span), HOMES, 0, 0, tiled=True)  9.69 us
    all_to_all x1, waiting for transfers between devices, shards(): lax.all_to_all(outgoing.reshape(nz * homes, MAIN, span + SIDE), DISPATCH,...  3.94 us
  transfers between devices with their start and end apart: 20, of which 7 were waited for; matrix products, arithmetic and copies ran while one was open for 1% of the time, Pallas kernels for 10%

profile of v6, /device:TPU:6, one launch (start us, length us, event | category | flops | bytes accessed | tf_op | source)
XLA Modules:
  0.0 150.0 jit_solution(6221055802906982761)
XLA Ops:
  2.2 3.3 %collective-permute-start.1 = (bf16[1536,256]{1,0:T(8,128)(2,1)}, bf16[1536,256]{1,0:T(8,128)(2,1)}, u32[]{:S(2)}, u32[]{:S(2)}) collective-permute-start(bf16[1536,256]{1,0:T(8,128)(2,1)} %pad_maximum_fusion.3), channel_id=1, source_target_pairs={{0,4},{2,6},{4,0},{6,2},{1,5},{3,7},{5,1},{7,3},{8,12},{10,14},{12... | collective-permute-start | bytes 2359304 | tf_op jit(solution)/shard_map/ppermute | solution.py:30
  7.0 16.9 %all-to-all-start = ((bf16[64,8,1280]{2,1,0:T(8,128)(2,1)}), bf16[64,8,1280]{2,1,0:T(8,128)(2,1)}, u32[]{:S(2)}, u32[]{:S(2)}) async-start(bf16[64,8,1280]{2,1,0:T(8,128)(2,1)} %bitcast.3), calls=%async_computation | async-start | bytes 2621440 | tf_op jit(solution)/shard_map/all_to_all | solution.py:334
  28.8 5.1 %collective-permute-start.2 = (bf16[1536,256]{1,0:T(8,128)(2,1)S(1)}, bf16[1536,256]{1,0:T(8,128)(2,1)}, u32[]{:S(2)}, u32[]{:S(2)}) collective-permute-start(bf16[1536,256]{1,0:T(8,128)(2,1)S(1)} %get-tuple-element.25), channel_id=1, source_target_pairs={{0,2},{2,4},{4,6},{6,0},{1,3},{3,5},{5,7},{7,1},{8,10},{10,12},{12... | collective-permute-start | bytes 2359304 | tf_op jit(solution)/shard_map/ppermute | solution.py:30
  35.9 2.4 %collective-permute-start.8 = (bf16[1536,256]{1,0:T(8,128)(2,1)}, bf16[1536,256]{1,0:T(8,128)(2,1)}, u32[]{:S(2)}, u32[]{:S(2)}) collective-permute-start(bf16[1536,256]{1,0:T(8,128)(2,1)} %get-tuple-element.27.own_ref), channel_id=1, source_target_pairs={{0,8},{8,0},{1,9},{9,1},{2,10},{10,2},{3,11},{11,3},{4,12},{12,4},... | collective-permute-start | bytes 2359304 | tf_op jit(solution)/shard_map/ppermute | solution.py:30
  38.3 10.5 %collective-permute-done.5.own_ref = bf16[1536,256]{1,0:T(8,128)(2,1)} collective-permute-done((bf16[1536,256]{1,0:T(8,128)(2,1)S(1)}, bf16[1536,256]{1,0:T(8,128)(2,1)}, u32[]{:S(2)}, u32[]{:S(2)}) %collective-permute-start.5) | collective-permute-done | bytes 786464 | tf_op jit(solution)/shard_map/ppermute | solution.py:30
  50.7 2.4 %collective-permute-start.3 = (bf16[1536,256]{1,0:T(8,128)(2,1)}, bf16[1536,256]{1,0:T(8,128)(2,1)}, u32[]{:S(2)}, u32[]{:S(2)}) collective-permute-start(bf16[1536,256]{1,0:T(8,128)(2,1)} %collective-permute-done.2.own_ref), channel_id=1, source_target_pairs={{0,8},{8,0},{1,9},{9,1},{2,10},{10,2},{3,11},{11,3},{4,12},{12,4},... | collective-permute-start | bytes 2359304 | tf_op jit(solution)/shard_map/ppermute | solution.py:30
  55.0 3.9 %all-to-all-done = bf16[64,8,1280]{2,1,0:T(8,128)(2,1)} async-done(((bf16[64,8,1280]{2,1,0:T(8,128)(2,1)}), bf16[64,8,1280]{2,1,0:T(8,128)(2,1)}, u32[]{:S(2)}, u32[]{:S(2)}) %all-to-all-start) | async-done | bytes 1310752 | tf_op jit(solution)/shard_map/all_to_all | solution.py:334
  60.6 2.1 %shard_map.79 = bf16[800,256]{1,0:T(8,128)(2,1)S(1)} custom-call(bf16[384,1536]{1,0:T(8,128)(2,1)S(1)} %get-tuple-element.19.rows_ref, bf16[16,256]{1,0:T(8,128)(2,1)S(1)} %get-tuple-element.20.tail_ref, bf16[16,256]{1,0:T(8,128)(2,1)S(1)} %get-tuple-element.24.router_ref, bf16[1536,256]{1,0:T(8,128)(2,1)} %get-tuple-element.27.own_ref, ...), custom_call_target="tpu_custom_call" | custom-call | flops 603979776 | bytes 3178496 | tf_op jit(solution)/shard_map/pallas_call | solution.py:44
  62.8 4.0 %collective-permute-start.9 = (bf16[800,256]{1,0:T(8,128)(2,1)S(1)}, bf16[800,256]{1,0:T(8,128)(2,1)S(1)}, u32[]{:S(2)}, u32[]{:S(2)}) collective-permute-start(bf16[800,256]{1,0:T(8,128)(2,1)S(1)} %shard_map.79), channel_id=1, source_target_pairs={{0,4},{2,6},{4,0},{6,2},{1,5},{3,7},{5,1},{7,3},{8,12},{10,14},{12... | collective-permute-start | bytes 1228808 | tf_op jit(solution)/shard_map/ppermute | solution.py:30
  69.0 2.4 %collective-permute-start.7 = (bf16[800,256]{1,0:T(8,128)(2,1)S(1)}, bf16[800,256]{1,0:T(8,128)(2,1)S(1)}, u32[]{:S(2)}, u32[]{:S(2)}) collective-permute-start(bf16[800,256]{1,0:T(8,128)(2,1)S(1)} %shard_map.78), channel_id=1, source_target_pairs={{0,2},{2,4},{4,6},{6,0},{1,3},{3,5},{5,7},{7,1},{8,10},{10,12},{12... | collective-permute-start | bytes 1228808 | tf_op jit(solution)/shard_map/ppermute | solution.py:30
  71.4 2.1 %shard_map.77 = bf16[800,256]{1,0:T(8,128)(2,1)S(1)} custom-call(bf16[384,1536]{1,0:T(8,128)(2,1)S(1)} %get-tuple-element.19.rows_ref, bf16[16,256]{1,0:T(8,128)(2,1)S(1)} %get-tuple-element.20.tail_ref, bf16[16,256]{1,0:T(8,128)(2,1)S(1)} %get-tuple-element.24.router_ref, bf16[1536,256]{1,0:T(8,128)(2,1)} %collective-permute-done.2.own_ref, ...), custom_call_target="tpu_custom_call" | custom-call | flops 603979776 | bytes 3178496 | tf_op jit(solution)/shard_map/pallas_call | solution.py:44
  73.6 3.5 %collective-permute-start.4 = (bf16[800,256]{1,0:T(8,128)(2,1)S(1)}, bf16[800,256]{1,0:T(8,128)(2,1)S(1)}, u32[]{:S(2)}, u32[]{:S(2)}) collective-permute-start(bf16[800,256]{1,0:T(8,128)(2,1)S(1)} %shard_map.77), channel_id=1, source_target_pairs={{0,6},{2,0},{4,2},{6,4},{1,7},{3,1},{5,3},{7,5},{8,14},{10,8},{12,... | collective-permute-start | bytes 1228808 | tf_op jit(solution)/shard_map/ppermute | solution.py:30
  79.2 3.5 %collective-permute-done.7.refs_1_ = bf16[800,256]{1,0:T(8,128)(2,1)S(1)} collective-permute-done((bf16[800,256]{1,0:T(8,128)(2,1)S(1)}, bf16[800,256]{1,0:T(8,128)(2,1)S(1)}, u32[]{:S(2)}, u32[]{:S(2)}) %collective-permute-start.7) | collective-permute-done | bytes 409632 | tf_op jit(solution)/shard_map/ppermute | solution.py:30
  85.0 6.7 %collective-permute-start.14 = (bf16[800,128]{1,0:T(8,128)(2,1)S(1)}, bf16[800,128]{1,0:T(8,128)(2,1)S(1)}, u32[]{:S(2)}, u32[]{:S(2)}) collective-permute-start(bf16[800,128]{1,0:T(8,128)(2,1)S(1)} %shard_map.81.own_ref), channel_id=1, source_target_pairs={{0,1},{1,0},{2,3},{3,2},{4,5},{5,4},{6,7},{7,6},{8,9},{9,8},{10,11... | collective-permute-start | bytes 614408 | tf_op jit(solution)/shard_map/ppermute | solution.py:30
  91.8 3.1 %collective-permute-start.11 = (bf16[768,128]{1,0:T(8,128)(2,1)S(1)}, bf16[768,128]{1,0:T(8,128)(2,1)S(1)}, u32[]{:S(2)}, u32[]{:S(2)}) collective-permute-start(bf16[768,128]{1,0:T(8,128)(2,1)S(1)} %slice.8.refs_0_), channel_id=1, source_target_pairs={{0,2},{2,4},{4,6},{6,0},{1,3},{3,5},{5,7},{7,1},{8,10},{10,12},{12... | collective-permute-start | bytes 589832 | tf_op jit(solution)/shard_map/ppermute | solution.py:30
  94.9 2.4 %collective-permute-start.12 = (bf16[768,128]{1,0:T(8,128)(2,1)S(1)}, bf16[768,128]{1,0:T(8,128)(2,1)S(1)}, u32[]{:S(2)}, u32[]{:S(2)}) collective-permute-start(bf16[768,128]{1,0:T(8,128)(2,1)S(1)} %slice.8.refs_0_), channel_id=1, source_target_pairs={{0,4},{2,6},{4,0},{6,2},{1,5},{3,7},{5,1},{7,3},{8,12},{10,14},{12... | collective-permute-start | bytes 589832 | tf_op jit(solution)/shard_map/ppermute | solution.py:30
  97.3 3.0 %collective-permute-start.13 = (bf16[768,128]{1,0:T(8,128)(2,1)S(1)}, bf16[768,128]{1,0:T(8,128)(2,1)S(1)}, u32[]{:S(2)}, u32[]{:S(2)}) collective-permute-start(bf16[768,128]{1,0:T(8,128)(2,1)S(1)} %slice.8.refs_0_), channel_id=1, source_target_pairs={{0,6},{2,0},{4,2},{6,4},{1,7},{3,1},{5,3},{7,5},{8,14},{10,8},{12,... | collective-permute-start | bytes 589832 | tf_op jit(solution)/shard_map/ppermute | solution.py:30
  100.4 4.0 %collective-permute-start.15 = (bf16[768,128]{1,0:T(8,128)(2,1)S(1)}, bf16[768,128]{1,0:T(8,128)(2,1)S(1)}, u32[]{:S(2)}, u32[]{:S(2)}) collective-permute-start(bf16[768,128]{1,0:T(8,128)(2,1)S(1)} %slice.9.refs_0_), channel_id=1, source_target_pairs={{0,2},{2,4},{4,6},{6,0},{1,3},{3,5},{5,7},{7,1},{8,10},{10,12},{12... | collective-permute-start | bytes 589832 | tf_op jit(solution)/shard_map/ppermute | solution.py:30
  104.4 3.7 %collective-permute-start.16 = (bf16[768,128]{1,0:T(8,128)(2,1)S(1)}, bf16[768,128]{1,0:T(8,128)(2,1)S(1)}, u32[]{:S(2)}, u32[]{:S(2)}) collective-permute-start(bf16[768,128]{1,0:T(8,128)(2,1)S(1)} %slice.9.refs_0_), channel_id=1, source_target_pairs={{0,4},{2,6},{4,0},{6,2},{1,5},{3,7},{5,1},{7,3},{8,12},{10,14},{12... | collective-permute-start | bytes 589832 | tf_op jit(solution)/shard_map/ppermute | solution.py:30
  108.1 2.8 %collective-permute-start.17 = (bf16[768,128]{1,0:T(8,128)(2,1)S(1)}, bf16[768,128]{1,0:T(8,128)(2,1)S(1)}, u32[]{:S(2)}, u32[]{:S(2)}) collective-permute-start(bf16[768,128]{1,0:T(8,128)(2,1)S(1)} %slice.9.refs_0_), channel_id=1, source_target_pairs={{0,6},{2,0},{4,2},{6,4},{1,7},{3,1},{5,3},{7,5},{8,14},{10,8},{12,... | collective-permute-start | bytes 589832 | tf_op jit(solution)/shard_map/ppermute | solution.py:30
  112.3 3.3 %collective-permute-done.16.refs_2_ = bf16[768,128]{1,0:T(8,128)(2,1)S(1)} collective-permute-done((bf16[768,128]{1,0:T(8,128)(2,1)S(1)}, bf16[768,128]{1,0:T(8,128)(2,1)S(1)}, u32[]{:S(2)}, u32[]{:S(2)}) %collective-permute-start.16) | collective-permute-done | bytes 196640 | tf_op jit(solution)/shard_map/ppermute | solution.py:30
  115.6 2.5 %collective-permute-done.17.refs_3_ = bf16[768,128]{1,0:T(8,128)(2,1)S(1)} collective-permute-done((bf16[768,128]{1,0:T(8,128)(2,1)S(1)}, bf16[768,128]{1,0:T(8,128)(2,1)S(1)}, u32[]{:S(2)}, u32[]{:S(2)}) %collective-permute-start.17) | collective-permute-done | bytes 196640 | tf_op jit(solution)/shard_map/ppermute | solution.py:30
  120.7 9.7 %all-to-all-start.1 = ((bf16[32,8,1152]{2,1,0:T(8,128)(2,1)}), bf16[32,8,1152]{2,1,0:T(8,128)(2,1)S(1)}, u32[]{:S(2)}, u32[]{:S(2)}) async-start(bf16[32,8,1152]{2,1,0:T(8,128)(2,1)} %bitcast.9), calls=%async_computation.1 | async-start | bytes 1179648 | tf_op jit(solution)/shard_map/all_to_all | solution.py:423
  131.3 17.7 %all-to-all-done.1 = bf16[32,8,1152]{2,1,0:T(8,128)(2,1)S(1)} async-done(((bf16[32,8,1152]{2,1,0:T(8,128)(2,1)}), bf16[32,8,1152]{2,1,0:T(8,128)(2,1)S(1)}, u32[]{:S(2)}, u32[]{:S(2)}) %all-to-all-start.1) | async-done | bytes 589856 | tf_op jit(solution)/shard_map/all_to_all | solution.py:423
  (63 shorter events, 28.2 us)
Async XLA Ops:
  2.2 33.6 %collective-permute-start.1 = (bf16[1536,256]{1,0:T(8,128)(2,1)}, bf16[1536,256]{1,0:T(8,128)(2,1)}, u32[]{:S(2)}, u32[]{:S(2)}) collective-permute-start(bf16[1536,256]{1,0:T(8,128)(2,1)} %pad_maximum_fusion.3), channel_id=1, source_target_pairs={{0,4},{2,6},{4,0},{6,2},{1,5},{3,7},{5,1},{7,3},{8,12},{10,14},{12... | collective-permute-start | bytes 2359304 | tf_op jit(solution)/shard_map/ppermute | solution.py:30
  5.6 18.5 %copy-start.10 = (bf16[6144,128]{1,0:T(8,128)(2,1)S(1)}, bf16[6144,128]{1,0:T(8,128)(2,1)}, u32[]{:S(2)}) copy-start(bf16[6144,128]{1,0:T(8,128)(2,1)} %param.11) | copy-start | bytes 4718596
  7.0 17.0 %copy-start.9 = (bf16[6144,128]{1,0:T(8,128)(2,1)S(1)}, bf16[6144,128]{1,0:T(8,128)(2,1)}, u32[]{:S(2)}) copy-start(bf16[6144,128]{1,0:T(8,128)(2,1)} %param.12) | copy-start | bytes 4718596
  7.0 52.0 %all-to-all-start = ((bf16[64,8,1280]{2,1,0:T(8,128)(2,1)}), bf16[64,8,1280]{2,1,0:T(8,128)(2,1)}, u32[]{:S(2)}, u32[]{:S(2)}) async-start(bf16[64,8,1280]{2,1,0:T(8,128)(2,1)} %bitcast.3), calls=%async_computation | async-start | bytes 2621440 | tf_op jit(solution)/shard_map/all_to_all | solution.py:334
  26.8 21.9 %collective-permute-start.5 = (bf16[1536,256]{1,0:T(8,128)(2,1)S(1)}, bf16[1536,256]{1,0:T(8,128)(2,1)}, u32[]{:S(2)}, u32[]{:S(2)}) collective-permute-start(bf16[1536,256]{1,0:T(8,128)(2,1)S(1)} %get-tuple-element.26), channel_id=1, source_target_pairs={{0,6},{2,0},{4,2},{6,4},{1,7},{3,1},{5,3},{7,5},{8,14},{10,8},{12,... | collective-permute-start | bytes 2359304 | tf_op jit(solution)/shard_map/ppermute | solution.py:30
  28.8 21.9 %collective-permute-start.2 = (bf16[1536,256]{1,0:T(8,128)(2,1)S(1)}, bf16[1536,256]{1,0:T(8,128)(2,1)}, u32[]{:S(2)}, u32[]{:S(2)}) collective-permute-start(bf16[1536,256]{1,0:T(8,128)(2,1)S(1)} %get-tuple-element.25), channel_id=1, source_target_pairs={{0,2},{2,4},{4,6},{6,0},{1,3},{3,5},{5,7},{7,1},{8,10},{10,12},{12... | collective-permute-start | bytes 2359304 | tf_op jit(solution)/shard_map/ppermute | solution.py:30
  33.9 70.5 %collective-permute-start = (bf16[1024,768]{1,0:T(8,128)(2,1)S(1)}, bf16[1024,768]{1,0:T(8,128)(2,1)S(1)}, u32[]{:S(2)}, u32[]{:S(2)}) collective-permute-start(bf16[1024,768]{1,0:T(8,128)(2,1)S(1)} %copy-done), channel_id=1, source_target_pairs={{0,8},{8,0},{1,9},{9,1},{2,10},{10,2},{3,11},{11,3},{4,12},{12,4},... | collective-permute-start | bytes 4718600 | tf_op jit(solution)/shard_map/ppermute | solution.py:30
  35.9 24.8 %collective-permute-start.8 = (bf16[1536,256]{1,0:T(8,128)(2,1)}, bf16[1536,256]{1,0:T(8,128)(2,1)}, u32[]{:S(2)}, u32[]{:S(2)}) collective-permute-start(bf16[1536,256]{1,0:T(8,128)(2,1)} %get-tuple-element.27.own_ref), channel_id=1, source_target_pairs={{0,8},{8,0},{1,9},{9,1},{2,10},{10,2},{3,11},{11,3},{4,12},{12,4},... | collective-permute-start | bytes 2359304 | tf_op jit(solution)/shard_map/ppermute | solution.py:30
  48.8 18.1 %collective-permute-start.6 = (bf16[1536,256]{1,0:T(8,128)(2,1)}, bf16[1536,256]{1,0:T(8,128)(2,1)}, u32[]{:S(2)}, u32[]{:S(2)}) collective-permute-start(bf16[1536,256]{1,0:T(8,128)(2,1)} %collective-permute-done.5.own_ref), channel_id=1, source_target_pairs={{0,8},{8,0},{1,9},{9,1},{2,10},{10,2},{3,11},{11,3},{4,12},{12,4},... | collective-permute-start | bytes 2359304 | tf_op jit(solution)/shard_map/ppermute | solution.py:30
  50.7 20.7 %collective-permute-start.3 = (bf16[1536,256]{1,0:T(8,128)(2,1)}, bf16[1536,256]{1,0:T(8,128)(2,1)}, u32[]{:S(2)}, u32[]{:S(2)}) collective-permute-start(bf16[1536,256]{1,0:T(8,128)(2,1)} %collective-permute-done.2.own_ref), channel_id=1, source_target_pairs={{0,8},{8,0},{1,9},{9,1},{2,10},{10,2},{3,11},{11,3},{4,12},{12,4},... | collective-permute-start | bytes 2359304 | tf_op jit(solution)/shard_map/ppermute | solution.py:30
  53.1 23.9 %collective-permute-start.10 = (bf16[1536,256]{1,0:T(8,128)(2,1)}, bf16[1536,256]{1,0:T(8,128)(2,1)}, u32[]{:S(2)}, u32[]{:S(2)}) collective-permute-start(bf16[1536,256]{1,0:T(8,128)(2,1)} %get-tuple-element.28.own_ref), channel_id=1, source_target_pairs={{0,8},{8,0},{1,9},{9,1},{2,10},{10,2},{3,11},{11,3},{4,12},{12,4},... | collective-permute-start | bytes 2359304 | tf_op jit(solution)/shard_map/ppermute | solution.py:30
  62.8 16.4 %collective-permute-start.9 = (bf16[800,256]{1,0:T(8,128)(2,1)S(1)}, bf16[800,256]{1,0:T(8,128)(2,1)S(1)}, u32[]{:S(2)}, u32[]{:S(2)}) collective-permute-start(bf16[800,256]{1,0:T(8,128)(2,1)S(1)} %shard_map.79), channel_id=1, source_target_pairs={{0,4},{2,6},{4,0},{6,2},{1,5},{3,7},{5,1},{7,3},{8,12},{10,14},{12... | collective-permute-start | bytes 1228808 | tf_op jit(solution)/shard_map/ppermute | solution.py:30
  69.0 13.7 %collective-permute-start.7 = (bf16[800,256]{1,0:T(8,128)(2,1)S(1)}, bf16[800,256]{1,0:T(8,128)(2,1)S(1)}, u32[]{:S(2)}, u32[]{:S(2)}) collective-permute-start(bf16[800,256]{1,0:T(8,128)(2,1)S(1)} %shard_map.78), channel_id=1, source_target_pairs={{0,2},{2,4},{4,6},{6,0},{1,3},{3,5},{5,7},{7,1},{8,10},{10,12},{12... | collective-permute-start | bytes 1228808 | tf_op jit(solution)/shard_map/ppermute | solution.py:30
  73.6 11.1 %collective-permute-start.4 = (bf16[800,256]{1,0:T(8,128)(2,1)S(1)}, bf16[800,256]{1,0:T(8,128)(2,1)S(1)}, u32[]{:S(2)}, u32[]{:S(2)}) collective-permute-start(bf16[800,256]{1,0:T(8,128)(2,1)S(1)} %shard_map.77), channel_id=1, source_target_pairs={{0,6},{2,0},{4,2},{6,4},{1,7},{3,1},{5,3},{7,5},{8,14},{10,8},{12,... | collective-permute-start | bytes 1228808 | tf_op jit(solution)/shard_map/ppermute | solution.py:30
  79.2 31.7 %copy-start.7 = (s32[2]{0:T(128)S(1)}, s32[2]{0:T(128)}, u32[]{:S(2)}) copy-start(s32[2]{0:T(128)} %copy-done.6) | copy-start | bytes 28
  85.0 15.3 %collective-permute-start.14 = (bf16[800,128]{1,0:T(8,128)(2,1)S(1)}, bf16[800,128]{1,0:T(8,128)(2,1)S(1)}, u32[]{:S(2)}, u32[]{:S(2)}) collective-permute-start(bf16[800,128]{1,0:T(8,128)(2,1)S(1)} %shard_map.81.own_ref), channel_id=1, source_target_pairs={{0,1},{1,0},{2,3},{3,2},{4,5},{5,4},{6,7},{7,6},{8,9},{9,8},{10,11... | collective-permute-start | bytes 614408 | tf_op jit(solution)/shard_map/ppermute | solution.py:30
  91.8 16.3 %collective-permute-start.11 = (bf16[768,128]{1,0:T(8,128)(2,1)S(1)}, bf16[768,128]{1,0:T(8,128)(2,1)S(1)}, u32[]{:S(2)}, u32[]{:S(2)}) collective-permute-start(bf16[768,128]{1,0:T(8,128)(2,1)S(1)} %slice.8.refs_0_), channel_id=1, source_target_pairs={{0,2},{2,4},{4,6},{6,0},{1,3},{3,5},{5,7},{7,1},{8,10},{10,12},{12... | collective-permute-start | bytes 589832 | tf_op jit(solution)/shard_map/ppermute | solution.py:30
  94.9 16.1 %collective-permute-start.12 = (bf16[768,128]{1,0:T(8,128)(2,1)S(1)}, bf16[768,128]{1,0:T(8,128)(2,1)S(1)}, u32[]{:S(2)}, u32[]{:S(2)}) collective-permute-start(bf16[768,128]{1,0:T(8,128)(2,1)S(1)} %slice.8.refs_0_), channel_id=1, source_target_pairs={{0,4},{2,6},{4,0},{6,2},{1,5},{3,7},{5,1},{7,3},{8,12},{10,14},{12... | collective-permute-start | bytes 589832 | tf_op jit(solution)/shard_map/ppermute | solution.py:30
  97.3 13.6 %collective-permute-start.13 = (bf16[768,128]{1,0:T(8,128)(2,1)S(1)}, bf16[768,128]{1,0:T(8,128)(2,1)S(1)}, u32[]{:S(2)}, u32[]{:S(2)}) collective-permute-start(bf16[768,128]{1,0:T(8,128)(2,1)S(1)} %slice.8.refs_0_), channel_id=1, source_target_pairs={{0,6},{2,0},{4,2},{6,4},{1,7},{3,1},{5,3},{7,5},{8,14},{10,8},{12,... | collective-permute-start | bytes 589832 | tf_op jit(solution)/shard_map/ppermute | solution.py:30
  100.4 11.9 %collective-permute-start.15 = (bf16[768,128]{1,0:T(8,128)(2,1)S(1)}, bf16[768,128]{1,0:T(8,128)(2,1)S(1)}, u32[]{:S(2)}, u32[]{:S(2)}) collective-permute-start(bf16[768,128]{1,0:T(8,128)(2,1)S(1)} %slice.9.refs_0_), channel_id=1, source_target_pairs={{0,2},{2,4},{4,6},{6,0},{1,3},{3,5},{5,7},{7,1},{8,10},{10,12},{12... | collective-permute-start | bytes 589832 | tf_op jit(solution)/shard_map/ppermute | solution.py:30
  104.4 11.2 %collective-permute-start.16 = (bf16[768,128]{1,0:T(8,128)(2,1)S(1)}, bf16[768,128]{1,0:T(8,128)(2,1)S(1)}, u32[]{:S(2)}, u32[]{:S(2)}) collective-permute-start(bf16[768,128]{1,0:T(8,128)(2,1)S(1)} %slice.9.refs_0_), channel_id=1, source_target_pairs={{0,4},{2,6},{4,0},{6,2},{1,5},{3,7},{5,1},{7,3},{8,12},{10,14},{12... | collective-permute-start | bytes 589832 | tf_op jit(solution)/shard_map/ppermute | solution.py:30
  108.1 10.0 %collective-permute-start.17 = (bf16[768,128]{1,0:T(8,128)(2,1)S(1)}, bf16[768,128]{1,0:T(8,128)(2,1)S(1)}, u32[]{:S(2)}, u32[]{:S(2)}) collective-permute-start(bf16[768,128]{1,0:T(8,128)(2,1)S(1)} %slice.9.refs_0_), channel_id=1, source_target_pairs={{0,6},{2,0},{4,2},{6,4},{1,7},{3,1},{5,3},{7,5},{8,14},{10,8},{12,... | collective-permute-start | bytes 589832 | tf_op jit(solution)/shard_map/ppermute | solution.py:30
  120.7 28.3 %copy-start.3 = (bf16[32,768]{1,0:T(8,128)(2,1)S(1)}, bf16[32,768]{1,0:T(8,128)(2,1)}, u32[]{:S(2)}) copy-start(bf16[32,768]{1,0:T(8,128)(2,1)} %tok_ref.5) | copy-start | bytes 147460
  120.7 28.3 %all-to-all-start.1 = ((bf16[32,8,1152]{2,1,0:T(8,128)(2,1)}), bf16[32,8,1152]{2,1,0:T(8,128)(2,1)S(1)}, u32[]{:S(2)}, u32[]{:S(2)}) async-start(bf16[32,8,1152]{2,1,0:T(8,128)(2,1)} %bitcast.9), calls=%async_computation.1 | async-start | bytes 1179648 | tf_op jit(solution)/shard_map/all_to_all | solution.py:423
  (8 other events, 27.8 us)

commit v7 on v6

--- a/solution.py
+++ b/solution.py
@@ -23,6 +23,7 @@
 F32, BF16 = jnp.float32, jnp.bfloat16
 VMEM_LIMIT = 16 * 1024 * 1024
 WINDOW_FLOPS = 10**11
+FIRST_FLOPS = 10**10
 
 
 def shift(value, axis, by):
@@ -185,6 +186,12 @@
         out_ref[c * n : (c + 1) * n, :] = (jax.nn.silu(gate) * upward).astype(BF16)
 
 
+def repeat_kernel(in_ref, out_ref):
+    n = in_ref.shape[0] - 2 * TAIL
+    for i in range(out_ref.shape[0] // n):
+        out_ref[i * n : (i + 1) * n, :] = in_ref[:n, :]
+
+
 def down_part(at_ref, dz, n, nx, nz, pieces, own_ref, other_ref):
     units = pieces[0].shape[1]
     side = (at_ref[1] + dz) % nz
@@ -202,17 +209,28 @@
 
 
 def down_first_kernel(homes, nx, nz, at_ref, own_ref, other_ref, *refs):
-    pieces, out_ref = refs[:-1], refs[-1]
+    pieces, out_ref, rest_ref = refs[:-2], refs[-2], refs[-1]
+    units = pieces[0].shape[1]
+    for c, w_ref in enumerate((own_ref, other_ref)):
+        for x in range(nx):
+            t = x * nz + (at_ref[1] + 1) % nz
+            rest_ref[(c * nx + x) * units : (c * nx + x + 1) * units, :] = w_ref[
+                pl.ds(pl.multiple_of(t * units, units), units), :
+            ]
     out_ref[...] = down_part(at_ref, 0, homes * CAP, nx, nz, pieces, own_ref, other_ref)
 
 
-def down_last_kernel(homes, nx, nz, at_ref, own_ref, other_ref, first_ref, *refs):
-    pieces, out_ref = refs[:-1], refs[-1]
-    width = own_ref.shape[1]
+def down_last_kernel(homes, nx, first_ref, rest_ref, hid_ref, out_ref):
+    width = first_ref.shape[1]
     half = width // 2
-    n_main = homes * MAIN
-    total = down_part(at_ref, 1, homes * CAP, nx, nz, pieces, own_ref, other_ref)
-    part = (first_ref[...] + total).astype(BF16)
+    n, n_main = homes * CAP, homes * MAIN
+    depth = rest_ref.shape[0] // 2
+    total = first_ref[...]
+    for c in range(2):
+        starts = [(2 * x + c) * n for x in range(nx)]
+        wide = jnp.concatenate([hid_ref[at : at + n, :] for at in starts], 1)
+        total += dot(wide, rest_ref[c * depth : (c + 1) * depth, :])
+    part = total.astype(BF16)
     out_ref[:, :width] = part[:n_main]
     rest = part[n_main:]
     out_ref[:, width:] = (
@@ -397,27 +415,33 @@
     )
 
     hid_other = shift(hidden, "zhi", 1)
-    own_rows, other_rows = hidden[: 2 * n], hid_other[: 2 * n]
-    first = local_kernel(
+    own_rows = hidden[: 2 * n]
+    other_rows = local_kernel(
+        repeat_kernel, jax.ShapeDtypeStruct((nx * 2 * n, units), BF16), hid_other
+    )
+    other_rows = lax.all_to_all(
+        other_rows.reshape(nx, 2 * n, units), "x", 0, 0, tiled=True
+    ).reshape(nx * 2 * n, units)
+    first, w_rest = local_kernel(
         functools.partial(down_first_kernel, homes, nx, nz),
-        jax.ShapeDtypeStruct((n, width), F32),
+        [
+            jax.ShapeDtypeStruct((n, width), F32),
+            jax.ShapeDtypeStruct((2 * nx * units, width), BF16),
+        ],
         at,
         w_down,
         wd_other,
         *[shift(own_rows, "x", k) if k else own_rows for k in range(nx)],
+        flops=FIRST_FLOPS,
+        smem=1,
+    )
+    back = local_kernel(
+        functools.partial(down_last_kernel, homes, nx),
+        jax.ShapeDtypeStruct((homes * MAIN, span), BF16),
+        first,
+        w_rest,
+        other_rows,
         flops=2 * n * w_down.size,
-        smem=1,
-    )
-    back = local_kernel(
-        functools.partial(down_last_kernel, homes, nx, nz),
-        jax.ShapeDtypeStruct((homes * MAIN, span), BF16),
-        at,
-        w_down,
-        wd_other,
-        first,
-        *[shift(other_rows, "x", k) if k else other_rows for k in range(nx)],
-        flops=2 * n * w_down.size,
-        smem=1,
     )
     back, routes = lax.optimization_barrier((back, routes))
     returned = lax.all_to_all(

time: 152 us -> 151 us (level)
  starting transfers between devices: 83.2 us -> 78.4 us
  local copies, waits for them, and re-layouts: 3.49 us -> 7.36 us
    ppermute x18 -> x15, starting transfers between devices: 56.6 us -> 46.5 us  [shift(): lax.ppermute(value, axis, [(i, (i + by) % size) for i in range(size)])]
    all_to_all x0 -> x1, starting transfers between devices: none -> 5.77 us  [shards(): lax.all_to_all(other_rows.reshape(nx, 2 * n, units), 'x', 0, 0, tiled=True)]
    ppermute x18 -> x15, waiting for transfers between devices: 21.7 us -> 18.3 us  [shift(): lax.ppermute(value, axis, [(i, (i + by) % size) for i in range(size)])]
    all_to_all x0 -> x1, waiting for transfers between devices: none -> 2.41 us  [shards(): lax.all_to_all(other_rows.reshape(nx, 2 * n, units), 'x', 0, 0, tiled=True)]
    unnamed x24 -> x16, local copies, waits for them, and re-layouts: 1.98 us -> 4.38 us
    pallas_call x13 -> x14, Pallas kernels: 17.1 us -> 18.1 us  [local_kernel(): pl.pallas_call(body, out_shape=out, in_specs=[pl.BlockSpec(memory_space=s...]
  transfers between devices with their start and end apart: 20 -> 18, of which waited for: 7 -> 7; matrix products, arithmetic and copies ran while one was open for 1% -> 1% of each run, Pallas kernels for 10% -> 10%
where the time goes in v7:
time: 151 us; the launch traced here: 148 us
  starting transfers between devices  78.4 us (52%)
  waiting for transfers between devices  42.6 us (28%)
  Pallas kernels  18.1 us (12%)
  local copies, waits for them, and re-layouts  7.36 us (5%)
    ppermute x15, starting transfers between devices, shift(): lax.ppermute(value, axis, [(i, (i + by) % size) for i in range(size)])  46.5 us
    ppermute x15, waiting for transfers between devices, shift(): lax.ppermute(value, axis, [(i, (i + by) % size) for i in range(size)])  18.3 us
    all_to_all x1, waiting for transfers between devices, shards(): lax.all_to_all(back.reshape(homes, MAIN, span), HOMES, 0, 0, tiled=True)  18.3 us
    pallas_call x14, Pallas kernels, local_kernel(): pl.pallas_call(body, out_shape=out, in_specs=[pl.BlockSpec(memory_space=s...  18.1 us
    all_to_all x1, starting transfers between devices, shards(): lax.all_to_all(outgoing.reshape(nz * homes, MAIN, span + SIDE), DISPATCH,...  16.6 us
    all_to_all x1, starting transfers between devices, shards(): lax.all_to_all(back.reshape(homes, MAIN, span), HOMES, 0, 0, tiled=True)  9.54 us
    all_to_all x1, starting transfers between devices, shards(): lax.all_to_all(other_rows.reshape(nx, 2 * n, units), 'x', 0, 0, tiled=True)  5.77 us
    unnamed x16, local copies, waits for them, and re-layouts  4.38 us
  transfers between devices with their start and end apart: 18, of which 7 were waited for; matrix products, arithmetic and copies ran while one was open for 1% of the time, Pallas kernels for 10%

profile of v7, /device:TPU:6, one launch (start us, length us, event | category | flops | bytes accessed | tf_op | source)
XLA Modules:
  0.0 148.2 jit_solution(11027352097836674399)
XLA Ops:
  2.2 3.3 %collective-permute-start.1 = (bf16[1536,256]{1,0:T(8,128)(2,1)}, bf16[1536,256]{1,0:T(8,128)(2,1)S(1)}, u32[]{:S(2)}, u32[]{:S(2)}) collective-permute-start(bf16[1536,256]{1,0:T(8,128)(2,1)} %pad_maximum_fusion.3), channel_id=1, source_target_pairs={{0,4},{2,6},{4,0},{6,2},{1,5},{3,7},{5,1},{7,3},{8,12},{10,14},{12... | collective-permute-start | bytes 2359304 | tf_op jit(solution)/shard_map/ppermute | solution.py:31
  7.0 16.6 %all-to-all-start = ((bf16[64,8,1280]{2,1,0:T(8,128)(2,1)}), bf16[64,8,1280]{2,1,0:T(8,128)(2,1)S(1)}, u32[]{:S(2)}, u32[]{:S(2)}) async-start(bf16[64,8,1280]{2,1,0:T(8,128)(2,1)} %bitcast.3), calls=%async_computation | async-start | bytes 2621440 | tf_op jit(solution)/shard_map/all_to_all | solution.py:352
  28.9 5.1 %collective-permute-start.2 = (bf16[1536,256]{1,0:T(8,128)(2,1)S(1)}, bf16[1536,256]{1,0:T(8,128)(2,1)}, u32[]{:S(2)}, u32[]{:S(2)}) collective-permute-start(bf16[1536,256]{1,0:T(8,128)(2,1)S(1)} %get-tuple-element.27), channel_id=1, source_target_pairs={{0,2},{2,4},{4,6},{6,0},{1,3},{3,5},{5,7},{7,1},{8,10},{10,12},{12... | collective-permute-start | bytes 2359304 | tf_op jit(solution)/shard_map/ppermute | solution.py:31
  36.0 2.4 %collective-permute-start.8 = (bf16[1536,256]{1,0:T(8,128)(2,1)S(1)}, bf16[1536,256]{1,0:T(8,128)(2,1)}, u32[]{:S(2)}, u32[]{:S(2)}) collective-permute-start(bf16[1536,256]{1,0:T(8,128)(2,1)S(1)} %get-tuple-element.29.own_ref), channel_id=1, source_target_pairs={{0,8},{8,0},{1,9},{9,1},{2,10},{10,2},{3,11},{11,3},{4,12},{12,4},... | collective-permute-start | bytes 2359304 | tf_op jit(solution)/shard_map/ppermute | solution.py:31
  38.4 10.5 %collective-permute-done.5.own_ref = bf16[1536,256]{1,0:T(8,128)(2,1)} collective-permute-done((bf16[1536,256]{1,0:T(8,128)(2,1)S(1)}, bf16[1536,256]{1,0:T(8,128)(2,1)}, u32[]{:S(2)}, u32[]{:S(2)}) %collective-permute-start.5) | collective-permute-done | bytes 786464 | tf_op jit(solution)/shard_map/ppermute | solution.py:31
  50.8 2.4 %collective-permute-start.3 = (bf16[1536,256]{1,0:T(8,128)(2,1)}, bf16[1536,256]{1,0:T(8,128)(2,1)}, u32[]{:S(2)}, u32[]{:S(2)}) collective-permute-start(bf16[1536,256]{1,0:T(8,128)(2,1)} %collective-permute-done.2.own_ref), channel_id=1, source_target_pairs={{0,8},{8,0},{1,9},{9,1},{2,10},{10,2},{3,11},{11,3},{4,12},{12,4},... | collective-permute-start | bytes 2359304 | tf_op jit(solution)/shard_map/ppermute | solution.py:31
  55.2 3.6 %all-to-all-done = bf16[64,8,1280]{2,1,0:T(8,128)(2,1)S(1)} async-done(((bf16[64,8,1280]{2,1,0:T(8,128)(2,1)}), bf16[64,8,1280]{2,1,0:T(8,128)(2,1)S(1)}, u32[]{:S(2)}, u32[]{:S(2)}) %all-to-all-start) | async-done | bytes 1310752 | tf_op jit(solution)/shard_map/all_to_all | solution.py:352
  61.0 4.0 %collective-permute-start.9 = (bf16[800,256]{1,0:T(8,128)(2,1)S(1)}, bf16[800,256]{1,0:T(8,128)(2,1)S(1)}, u32[]{:S(2)}, u32[]{:S(2)}) collective-permute-start(bf16[800,256]{1,0:T(8,128)(2,1)S(1)} %shard_map.79), channel_id=1, source_target_pairs={{0,4},{2,6},{4,0},{6,2},{1,5},{3,7},{5,1},{7,3},{8,12},{10,14},{12... | collective-permute-start | bytes 1228808 | tf_op jit(solution)/shard_map/ppermute | solution.py:31
  65.1 2.1 %shard_map.78 = bf16[800,256]{1,0:T(8,128)(2,1)S(1)} custom-call(bf16[384,1536]{1,0:T(8,128)(2,1)S(1)} %get-tuple-element.21.rows_ref, bf16[16,256]{1,0:T(8,128)(2,1)S(1)} %get-tuple-element.22.tail_ref, bf16[16,256]{1,0:T(8,128)(2,1)S(1)} %get-tuple-element.26.router_ref, bf16[1536,256]{1,0:T(8,128)(2,1)} %collective-permute-done.5.own_ref, ...), custom_call_target="tpu_custom_call" | custom-call | flops 603979776 | bytes 3178496 | tf_op jit(solution)/shard_map/pallas_call | solution.py:45
  67.2 2.4 %collective-permute-start.7 = (bf16[800,256]{1,0:T(8,128)(2,1)S(1)}, bf16[800,256]{1,0:T(8,128)(2,1)S(1)}, u32[]{:S(2)}, u32[]{:S(2)}) collective-permute-start(bf16[800,256]{1,0:T(8,128)(2,1)S(1)} %shard_map.78), channel_id=1, source_target_pairs={{0,2},{2,4},{4,6},{6,0},{1,3},{3,5},{5,7},{7,1},{8,10},{10,12},{12... | collective-permute-start | bytes 1228808 | tf_op jit(solution)/shard_map/ppermute | solution.py:31
  69.6 2.1 %shard_map.77 = bf16[800,256]{1,0:T(8,128)(2,1)S(1)} custom-call(bf16[384,1536]{1,0:T(8,128)(2,1)S(1)} %get-tuple-element.21.rows_ref, bf16[16,256]{1,0:T(8,128)(2,1)S(1)} %get-tuple-element.22.tail_ref, bf16[16,256]{1,0:T(8,128)(2,1)S(1)} %get-tuple-element.26.router_ref, bf16[1536,256]{1,0:T(8,128)(2,1)} %collective-permute-done.2.own_ref, ...), custom_call_target="tpu_custom_call" | custom-call | flops 603979776 | bytes 3178496 | tf_op jit(solution)/shard_map/pallas_call | solution.py:45
  71.8 3.5 %collective-permute-start.4 = (bf16[800,256]{1,0:T(8,128)(2,1)S(1)}, bf16[800,256]{1,0:T(8,128)(2,1)S(1)}, u32[]{:S(2)}, u32[]{:S(2)}) collective-permute-start(bf16[800,256]{1,0:T(8,128)(2,1)S(1)} %shard_map.77), channel_id=1, source_target_pairs={{0,6},{2,0},{4,2},{6,4},{1,7},{3,1},{5,3},{7,5},{8,14},{10,8},{12,... | collective-permute-start | bytes 1228808 | tf_op jit(solution)/shard_map/ppermute | solution.py:31
  77.2 4.1 %collective-permute-done.7.refs_1_ = bf16[800,256]{1,0:T(8,128)(2,1)S(1)} collective-permute-done((bf16[800,256]{1,0:T(8,128)(2,1)S(1)}, bf16[800,256]{1,0:T(8,128)(2,1)S(1)}, u32[]{:S(2)}, u32[]{:S(2)}) %collective-permute-start.7) | collective-permute-done | bytes 409632 | tf_op jit(solution)/shard_map/ppermute | solution.py:31
  83.2 7.2 %collective-permute-start.14 = (bf16[800,128]{1,0:T(8,128)(2,1)S(1)}, bf16[800,128]{1,0:T(8,128)(2,1)S(1)}, u32[]{:S(2)}, u32[]{:S(2)}) collective-permute-start(bf16[800,128]{1,0:T(8,128)(2,1)S(1)} %shard_map.81.own_ref), channel_id=1, source_target_pairs={{0,1},{1,0},{2,3},{3,2},{4,5},{5,4},{6,7},{7,6},{8,9},{9,8},{10,11... | collective-permute-start | bytes 614408 | tf_op jit(solution)/shard_map/ppermute | solution.py:31
  90.4 3.1 %collective-permute-start.11 = (bf16[768,128]{1,0:T(8,128)(2,1)S(1)}, bf16[768,128]{1,0:T(8,128)(2,1)S(1)}, u32[]{:S(2)}, u32[]{:S(2)}) collective-permute-start(bf16[768,128]{1,0:T(8,128)(2,1)S(1)} %slice.4.refs_0_), channel_id=1, source_target_pairs={{0,2},{2,4},{4,6},{6,0},{1,3},{3,5},{5,7},{7,1},{8,10},{10,12},{12... | collective-permute-start | bytes 589832 | tf_op jit(solution)/shard_map/ppermute | solution.py:31
  93.5 2.4 %collective-permute-start.12 = (bf16[768,128]{1,0:T(8,128)(2,1)S(1)}, bf16[768,128]{1,0:T(8,128)(2,1)S(1)}, u32[]{:S(2)}, u32[]{:S(2)}) collective-permute-start(bf16[768,128]{1,0:T(8,128)(2,1)S(1)} %slice.4.refs_0_), channel_id=1, source_target_pairs={{0,4},{2,6},{4,0},{6,2},{1,5},{3,7},{5,1},{7,3},{8,12},{10,14},{12... | collective-permute-start | bytes 589832 | tf_op jit(solution)/shard_map/ppermute | solution.py:31
  96.0 3.0 %collective-permute-start.13 = (bf16[768,128]{1,0:T(8,128)(2,1)S(1)}, bf16[768,128]{1,0:T(8,128)(2,1)S(1)}, u32[]{:S(2)}, u32[]{:S(2)}) collective-permute-start(bf16[768,128]{1,0:T(8,128)(2,1)S(1)} %slice.4.refs_0_), channel_id=1, source_target_pairs={{0,6},{2,0},{4,2},{6,4},{1,7},{3,1},{5,3},{7,5},{8,14},{10,8},{12,... | collective-permute-start | bytes 589832 | tf_op jit(solution)/shard_map/ppermute | solution.py:31
  100.0 5.8 %all-to-all-start.1 = ((bf16[4,768,128]{2,1,0:T(8,128)(2,1)}), bf16[4,768,128]{2,1,0:T(8,128)(2,1)S(1)}, u32[]{:S(2)}, u32[]{:S(2)}) async-start(bf16[4,768,128]{2,1,0:T(8,128)(2,1)} %bitcast.6), calls=%async_computation.1 | async-start | bytes 1572864 | tf_op jit(solution)/shard_map/all_to_all | solution.py:422
  105.8 2.2 %collective-permute-done.13.refs_3_ = bf16[768,128]{1,0:T(8,128)(2,1)S(1)} collective-permute-done((bf16[768,128]{1,0:T(8,128)(2,1)S(1)}, bf16[768,128]{1,0:T(8,128)(2,1)S(1)}, u32[]{:S(2)}, u32[]{:S(2)}) %collective-permute-start.13) | collective-permute-done | bytes 196640 | tf_op jit(solution)/shard_map/ppermute | solution.py:31
  109.6 2.8 %shard_map.82 = (f32[384,768]{1,0:T(8,128)S(1)}, bf16[1024,768]{1,0:T(8,128)(2,1)S(1)}) custom-call(s32[2]{0:T(128)S(1)} %pad_add_fusion._.at_ref, bf16[1024,768]{1,0:T(8,128)(2,1)} %own_ref.1, bf16[1024,768]{1,0:T(8,128)(2,1)} %collective-permute-done.other_ref, bf16[768,128]{1,0:T(8,128)(2,1)S(1)} %slice.4.refs_0_, ...), custom_call_target="tpu_custom_call" | custom-call | flops 10000000000 | bytes 6684680 | tf_op jit(solution)/shard_map/pallas_call | solution.py:45
  113.4 2.4 %all-to-all-done.1 = bf16[4,768,128]{2,1,0:T(8,128)(2,1)S(1)} async-done(((bf16[4,768,128]{2,1,0:T(8,128)(2,1)}), bf16[4,768,128]{2,1,0:T(8,128)(2,1)S(1)}, u32[]{:S(2)}, u32[]{:S(2)}) %all-to-all-start.1) | async-done | bytes 786464 | tf_op jit(solution)/shard_map/all_to_all | solution.py:422
  117.1 2.0 %shard_map.84 = bf16[256,1152]{1,0:T(8,128)(2,1)} custom-call(f32[384,768]{1,0:T(8,128)S(1)} %copy-done.1, bf16[1024,768]{1,0:T(8,128)(2,1)S(1)} %get-tuple-element.32.rest_ref, bf16[3072,128]{1,0:T(8,128)(2,1)S(1)} %bitcast.12), custom_call_target="tpu_custom_call" | custom-call | flops 603979776 | bytes 4128768 | tf_op jit(solution)/shard_map/pallas_call | solution.py:45
  119.1 9.5 %all-to-all-start.2 = ((bf16[32,8,1152]{2,1,0:T(8,128)(2,1)}), bf16[32,8,1152]{2,1,0:T(8,128)(2,1)S(1)}, u32[]{:S(2)}, u32[]{:S(2)}) async-start(bf16[32,8,1152]{2,1,0:T(8,128)(2,1)} %bitcast.9), calls=%async_computation.2 | async-start | bytes 1179648 | tf_op jit(solution)/shard_map/all_to_all | solution.py:447
  128.9 18.3 %all-to-all-done.2 = bf16[32,8,1152]{2,1,0:T(8,128)(2,1)S(1)} async-done(((bf16[32,8,1152]{2,1,0:T(8,128)(2,1)}), bf16[32,8,1152]{2,1,0:T(8,128)(2,1)S(1)}, u32[]{:S(2)}, u32[]{:S(2)}) %all-to-all-start.2) | async-done | bytes 589856 | tf_op jit(solution)/shard_map/all_to_all | solution.py:447
  (51 shorter events, 26.9 us)
Async XLA Ops:
  0.0 5.5 %copy-start.7 = (f32[768]{0:T(1024)S(1)}, f32[768]{0:T(1024)}, u32[]{:S(2)}) copy-start(f32[768]{0:T(1024)} %param.8) | copy-start | bytes 9220
  0.0 5.6 %copy-start.2 = (bf16[32,768]{1,0:T(8,128)(2,1)S(1)}, bf16[32,768]{1,0:T(8,128)(2,1)}, u32[]{:S(2)}) copy-start(bf16[32,768]{1,0:T(8,128)(2,1)} %tok_ref.5) | copy-start | bytes 147460
  0.0 5.6 %copy-start.3 = (s32[32,2]{0,1:T(2,128)S(1)}, s32[32,2]{0,1:T(2,128)}, u32[]{:S(2)}) copy-start(s32[32,2]{0,1:T(2,128)} %param.10) | copy-start | bytes 772
  2.2 33.7 %collective-permute-start.1 = (bf16[1536,256]{1,0:T(8,128)(2,1)}, bf16[1536,256]{1,0:T(8,128)(2,1)S(1)}, u32[]{:S(2)}, u32[]{:S(2)}) collective-permute-start(bf16[1536,256]{1,0:T(8,128)(2,1)} %pad_maximum_fusion.3), channel_id=1, source_target_pairs={{0,4},{2,6},{4,0},{6,2},{1,5},{3,7},{5,1},{7,3},{8,12},{10,14},{12... | collective-permute-start | bytes 2359304 | tf_op jit(solution)/shard_map/ppermute | solution.py:31
  7.0 51.7 %all-to-all-start = ((bf16[64,8,1280]{2,1,0:T(8,128)(2,1)}), bf16[64,8,1280]{2,1,0:T(8,128)(2,1)S(1)}, u32[]{:S(2)}, u32[]{:S(2)}) async-start(bf16[64,8,1280]{2,1,0:T(8,128)(2,1)} %bitcast.3), calls=%async_computation | async-start | bytes 2621440 | tf_op jit(solution)/shard_map/all_to_all | solution.py:352
  27.0 21.9 %collective-permute-start.5 = (bf16[1536,256]{1,0:T(8,128)(2,1)S(1)}, bf16[1536,256]{1,0:T(8,128)(2,1)}, u32[]{:S(2)}, u32[]{:S(2)}) collective-permute-start(bf16[1536,256]{1,0:T(8,128)(2,1)S(1)} %get-tuple-element.28), channel_id=1, source_target_pairs={{0,6},{2,0},{4,2},{6,4},{1,7},{3,1},{5,3},{7,5},{8,14},{10,8},{12,... | collective-permute-start | bytes 2359304 | tf_op jit(solution)/shard_map/ppermute | solution.py:31
  28.9 21.9 %collective-permute-start.2 = (bf16[1536,256]{1,0:T(8,128)(2,1)S(1)}, bf16[1536,256]{1,0:T(8,128)(2,1)}, u32[]{:S(2)}, u32[]{:S(2)}) collective-permute-start(bf16[1536,256]{1,0:T(8,128)(2,1)S(1)} %get-tuple-element.27), channel_id=1, source_target_pairs={{0,2},{2,4},{4,6},{6,0},{1,3},{3,5},{5,7},{7,1},{8,10},{10,12},{12... | collective-permute-start | bytes 2359304 | tf_op jit(solution)/shard_map/ppermute | solution.py:31
  34.0 71.8 %collective-permute-start = (bf16[1024,768]{1,0:T(8,128)(2,1)}, bf16[1024,768]{1,0:T(8,128)(2,1)}, u32[]{:S(2)}, u32[]{:S(2)}) collective-permute-start(bf16[1024,768]{1,0:T(8,128)(2,1)} %own_ref.1), channel_id=1, source_target_pairs={{0,8},{8,0},{1,9},{9,1},{2,10},{10,2},{3,11},{11,3},{4,12},{12,4},... | collective-permute-start | bytes 4718600 | tf_op jit(solution)/shard_map/ppermute | solution.py:31
  36.0 23.1 %collective-permute-start.8 = (bf16[1536,256]{1,0:T(8,128)(2,1)S(1)}, bf16[1536,256]{1,0:T(8,128)(2,1)}, u32[]{:S(2)}, u32[]{:S(2)}) collective-permute-start(bf16[1536,256]{1,0:T(8,128)(2,1)S(1)} %get-tuple-element.29.own_ref), channel_id=1, source_target_pairs={{0,8},{8,0},{1,9},{9,1},{2,10},{10,2},{3,11},{11,3},{4,12},{12,4},... | collective-permute-start | bytes 2359304 | tf_op jit(solution)/shard_map/ppermute | solution.py:31
  48.9 16.2 %collective-permute-start.6 = (bf16[1536,256]{1,0:T(8,128)(2,1)}, bf16[1536,256]{1,0:T(8,128)(2,1)}, u32[]{:S(2)}, u32[]{:S(2)}) collective-permute-start(bf16[1536,256]{1,0:T(8,128)(2,1)} %collective-permute-done.5.own_ref), channel_id=1, source_target_pairs={{0,8},{8,0},{1,9},{9,1},{2,10},{10,2},{3,11},{11,3},{4,12},{12,4},... | collective-permute-start | bytes 2359304 | tf_op jit(solution)/shard_map/ppermute | solution.py:31
  50.8 18.8 %collective-permute-start.3 = (bf16[1536,256]{1,0:T(8,128)(2,1)}, bf16[1536,256]{1,0:T(8,128)(2,1)}, u32[]{:S(2)}, u32[]{:S(2)}) collective-permute-start(bf16[1536,256]{1,0:T(8,128)(2,1)} %collective-permute-done.2.own_ref), channel_id=1, source_target_pairs={{0,8},{8,0},{1,9},{9,1},{2,10},{10,2},{3,11},{11,3},{4,12},{12,4},... | collective-permute-start | bytes 2359304 | tf_op jit(solution)/shard_map/ppermute | solution.py:31
  53.2 22.0 %collective-permute-start.10 = (bf16[1536,256]{1,0:T(8,128)(2,1)S(1)}, bf16[1536,256]{1,0:T(8,128)(2,1)}, u32[]{:S(2)}, u32[]{:S(2)}) collective-permute-start(bf16[1536,256]{1,0:T(8,128)(2,1)S(1)} %get-tuple-element.30.own_ref), channel_id=1, source_target_pairs={{0,8},{8,0},{1,9},{9,1},{2,10},{10,2},{3,11},{11,3},{4,12},{12,4},... | collective-permute-start | bytes 2359304 | tf_op jit(solution)/shard_map/ppermute | solution.py:31
  61.0 16.2 %collective-permute-start.9 = (bf16[800,256]{1,0:T(8,128)(2,1)S(1)}, bf16[800,256]{1,0:T(8,128)(2,1)S(1)}, u32[]{:S(2)}, u32[]{:S(2)}) collective-permute-start(bf16[800,256]{1,0:T(8,128)(2,1)S(1)} %shard_map.79), channel_id=1, source_target_pairs={{0,4},{2,6},{4,0},{6,2},{1,5},{3,7},{5,1},{7,3},{8,12},{10,14},{12... | collective-permute-start | bytes 1228808 | tf_op jit(solution)/shard_map/ppermute | solution.py:31
  67.2 14.1 %collective-permute-start.7 = (bf16[800,256]{1,0:T(8,128)(2,1)S(1)}, bf16[800,256]{1,0:T(8,128)(2,1)S(1)}, u32[]{:S(2)}, u32[]{:S(2)}) collective-permute-start(bf16[800,256]{1,0:T(8,128)(2,1)S(1)} %shard_map.78), channel_id=1, source_target_pairs={{0,2},{2,4},{4,6},{6,0},{1,3},{3,5},{5,7},{7,1},{8,10},{10,12},{12... | collective-permute-start | bytes 1228808 | tf_op jit(solution)/shard_map/ppermute | solution.py:31
  71.8 11.1 %collective-permute-start.4 = (bf16[800,256]{1,0:T(8,128)(2,1)S(1)}, bf16[800,256]{1,0:T(8,128)(2,1)S(1)}, u32[]{:S(2)}, u32[]{:S(2)}) collective-permute-start(bf16[800,256]{1,0:T(8,128)(2,1)S(1)} %shard_map.77), channel_id=1, source_target_pairs={{0,6},{2,0},{4,2},{6,4},{1,7},{3,1},{5,3},{7,5},{8,14},{10,8},{12,... | collective-permute-start | bytes 1228808 | tf_op jit(solution)/shard_map/ppermute | solution.py:31
  83.2 15.8 %collective-permute-start.14 = (bf16[800,128]{1,0:T(8,128)(2,1)S(1)}, bf16[800,128]{1,0:T(8,128)(2,1)S(1)}, u32[]{:S(2)}, u32[]{:S(2)}) collective-permute-start(bf16[800,128]{1,0:T(8,128)(2,1)S(1)} %shard_map.81.own_ref), channel_id=1, source_target_pairs={{0,1},{1,0},{2,3},{3,2},{4,5},{5,4},{6,7},{7,6},{8,9},{9,8},{10,11... | collective-permute-start | bytes 614408 | tf_op jit(solution)/shard_map/ppermute | solution.py:31
  90.4 15.4 %collective-permute-start.11 = (bf16[768,128]{1,0:T(8,128)(2,1)S(1)}, bf16[768,128]{1,0:T(8,128)(2,1)S(1)}, u32[]{:S(2)}, u32[]{:S(2)}) collective-permute-start(bf16[768,128]{1,0:T(8,128)(2,1)S(1)} %slice.4.refs_0_), channel_id=1, source_target_pairs={{0,2},{2,4},{4,6},{6,0},{1,3},{3,5},{5,7},{7,1},{8,10},{10,12},{12... | collective-permute-start | bytes 589832 | tf_op jit(solution)/shard_map/ppermute | solution.py:31
  93.5 12.3 %collective-permute-start.12 = (bf16[768,128]{1,0:T(8,128)(2,1)S(1)}, bf16[768,128]{1,0:T(8,128)(2,1)S(1)}, u32[]{:S(2)}, u32[]{:S(2)}) collective-permute-start(bf16[768,128]{1,0:T(8,128)(2,1)S(1)} %slice.4.refs_0_), channel_id=1, source_target_pairs={{0,4},{2,6},{4,0},{6,2},{1,5},{3,7},{5,1},{7,3},{8,12},{10,14},{12... | collective-permute-start | bytes 589832 | tf_op jit(solution)/shard_map/ppermute | solution.py:31
  96.0 12.0 %collective-permute-start.13 = (bf16[768,128]{1,0:T(8,128)(2,1)S(1)}, bf16[768,128]{1,0:T(8,128)(2,1)S(1)}, u32[]{:S(2)}, u32[]{:S(2)}) collective-permute-start(bf16[768,128]{1,0:T(8,128)(2,1)S(1)} %slice.4.refs_0_), channel_id=1, source_target_pairs={{0,6},{2,0},{4,2},{6,4},{1,7},{3,1},{5,3},{7,5},{8,14},{10,8},{12,... | collective-permute-start | bytes 589832 | tf_op jit(solution)/shard_map/ppermute | solution.py:31
  100.0 15.8 %all-to-all-start.1 = ((bf16[4,768,128]{2,1,0:T(8,128)(2,1)}), bf16[4,768,128]{2,1,0:T(8,128)(2,1)S(1)}, u32[]{:S(2)}, u32[]{:S(2)}) async-start(bf16[4,768,128]{2,1,0:T(8,128)(2,1)} %bitcast.6), calls=%async_computation.1 | async-start | bytes 1572864 | tf_op jit(solution)/shard_map/all_to_all | solution.py:422
  108.7 0.9 copy-start.5
  112.4 1.0 copy-start
  115.8 1.3 copy-start.1
  119.1 28.1 %all-to-all-start.2 = ((bf16[32,8,1152]{2,1,0:T(8,128)(2,1)}), bf16[32,8,1152]{2,1,0:T(8,128)(2,1)S(1)}, u32[]{:S(2)}, u32[]{:S(2)}) async-start(bf16[32,8,1152]{2,1,0:T(8,128)(2,1)} %bitcast.9), calls=%async_computation.2 | async-start | bytes 1179648 | tf_op jit(solution)/shard_map/all_to_all | solution.py:447
  (2 other events, 1.4 us)

commit v8 on v7

--- a/solution.py
+++ b/solution.py
@@ -220,17 +220,20 @@
     out_ref[...] = down_part(at_ref, 0, homes * CAP, nx, nz, pieces, own_ref, other_ref)
 
 
-def down_last_kernel(homes, nx, first_ref, rest_ref, hid_ref, out_ref):
+def down_last_kernel(homes, nx, rest_ref, hid_ref, first_ref, out_ref, held_ref, sem):
+    copy = pltpu.make_async_copy(first_ref, held_ref, sem)
+    copy.start()
     width = first_ref.shape[1]
     half = width // 2
     n, n_main = homes * CAP, homes * MAIN
     depth = rest_ref.shape[0] // 2
-    total = first_ref[...]
+    total = 0.0
     for c in range(2):
         starts = [(2 * x + c) * n for x in range(nx)]
         wide = jnp.concatenate([hid_ref[at : at + n, :] for at in starts], 1)
         total += dot(wide, rest_ref[c * depth : (c + 1) * depth, :])
-    part = total.astype(BF16)
+    copy.wait()
+    part = (total + held_ref[...]).astype(BF16)
     out_ref[:, :width] = part[:n_main]
     rest = part[n_main:]
     out_ref[:, width:] = (
@@ -438,9 +441,11 @@
     back = local_kernel(
         functools.partial(down_last_kernel, homes, nx),
         jax.ShapeDtypeStruct((homes * MAIN, span), BF16),
-        first,
         w_rest,
         other_rows,
+        first,
+        far=1,
+        scratch=[pltpu.VMEM((n, width), F32), pltpu.SemaphoreType.DMA],
         flops=2 * n * w_down.size,
     )
     back, routes = lax.optimization_barrier((back, routes))

time: 151 us -> 151 us (level)
  no operation moved by 1% of the time
where the time goes in v8:
time: 151 us; the launch traced here: 149 us
  starting transfers between devices  78.4 us (52%)
  waiting for transfers between devices  42.6 us (28%)
  Pallas kernels  18.3 us (12%)
  local copies, waits for them, and re-layouts  7.36 us (5%)
    ppermute x15, starting transfers between devices, shift(): lax.ppermute(value, axis, [(i, (i + by) % size) for i in range(size)])  46.5 us
    ppermute x15, waiting for transfers between devices, shift(): lax.ppermute(value, axis, [(i, (i + by) % size) for i in range(size)])  18.3 us
    pallas_call x14, Pallas kernels, local_kernel(): pl.pallas_call(body, out_shape=out, in_specs=[pl.BlockSpec(memory_space=s...  18.3 us
    all_to_all x1, waiting for transfers between devices, shards(): lax.all_to_all(back.reshape(homes, MAIN, span), HOMES, 0, 0, tiled=True)  18.3 us
    all_to_all x1, starting transfers between devices, shards(): lax.all_to_all(outgoing.reshape(nz * homes, MAIN, span + SIDE), DISPATCH,...  16.6 us
    all_to_all x1, starting transfers between devices, shards(): lax.all_to_all(back.reshape(homes, MAIN, span), HOMES, 0, 0, tiled=True)  9.56 us
    all_to_all x1, starting transfers between devices, shards(): lax.all_to_all(other_rows.reshape(nx, 2 * n, units), 'x', 0, 0, tiled=True)  5.77 us
    unnamed x16, local copies, waits for them, and re-layouts  4.38 us
  transfers between devices with their start and end apart: 18, of which 7 were waited for; matrix products, arithmetic and copies ran while one was open for 1% of the time, Pallas kernels for 10%

profile of v8, /device:TPU:6, one launch (start us, length us, event | category | flops | bytes accessed | tf_op | source)
XLA Modules:
  0.0 148.5 jit_solution(11966539937725849210)
XLA Ops:
  2.2 3.3 %collective-permute-start.1 = (bf16[1536,256]{1,0:T(8,128)(2,1)}, bf16[1536,256]{1,0:T(8,128)(2,1)S(1)}, u32[]{:S(2)}, u32[]{:S(2)}) collective-permute-start(bf16[1536,256]{1,0:T(8,128)(2,1)} %pad_maximum_fusion.3), channel_id=1, source_target_pairs={{0,4},{2,6},{4,0},{6,2},{1,5},{3,7},{5,1},{7,3},{8,12},{10,14},{12... | collective-permute-start | bytes 2359304 | tf_op jit(solution)/shard_map/ppermute | solution.py:31
  7.0 16.6 %all-to-all-start = ((bf16[64,8,1280]{2,1,0:T(8,128)(2,1)}), bf16[64,8,1280]{2,1,0:T(8,128)(2,1)S(1)}, u32[]{:S(2)}, u32[]{:S(2)}) async-start(bf16[64,8,1280]{2,1,0:T(8,128)(2,1)} %bitcast.3), calls=%async_computation | async-start | bytes 2621440 | tf_op jit(solution)/shard_map/all_to_all | solution.py:355
  28.9 5.1 %collective-permute-start.2 = (bf16[1536,256]{1,0:T(8,128)(2,1)S(1)}, bf16[1536,256]{1,0:T(8,128)(2,1)}, u32[]{:S(2)}, u32[]{:S(2)}) collective-permute-start(bf16[1536,256]{1,0:T(8,128)(2,1)S(1)} %get-tuple-element.27), channel_id=1, source_target_pairs={{0,2},{2,4},{4,6},{6,0},{1,3},{3,5},{5,7},{7,1},{8,10},{10,12},{12... | collective-permute-start | bytes 2359304 | tf_op jit(solution)/shard_map/ppermute | solution.py:31
  36.0 2.4 %collective-permute-start.8 = (bf16[1536,256]{1,0:T(8,128)(2,1)S(1)}, bf16[1536,256]{1,0:T(8,128)(2,1)}, u32[]{:S(2)}, u32[]{:S(2)}) collective-permute-start(bf16[1536,256]{1,0:T(8,128)(2,1)S(1)} %get-tuple-element.29.own_ref), channel_id=1, source_target_pairs={{0,8},{8,0},{1,9},{9,1},{2,10},{10,2},{3,11},{11,3},{4,12},{12,4},... | collective-permute-start | bytes 2359304 | tf_op jit(solution)/shard_map/ppermute | solution.py:31
  38.4 10.5 %collective-permute-done.5.own_ref = bf16[1536,256]{1,0:T(8,128)(2,1)} collective-permute-done((bf16[1536,256]{1,0:T(8,128)(2,1)S(1)}, bf16[1536,256]{1,0:T(8,128)(2,1)}, u32[]{:S(2)}, u32[]{:S(2)}) %collective-permute-start.5) | collective-permute-done | bytes 786464 | tf_op jit(solution)/shard_map/ppermute | solution.py:31
  50.8 2.4 %collective-permute-start.3 = (bf16[1536,256]{1,0:T(8,128)(2,1)}, bf16[1536,256]{1,0:T(8,128)(2,1)}, u32[]{:S(2)}, u32[]{:S(2)}) collective-permute-start(bf16[1536,256]{1,0:T(8,128)(2,1)} %collective-permute-done.2.own_ref), channel_id=1, source_target_pairs={{0,8},{8,0},{1,9},{9,1},{2,10},{10,2},{3,11},{11,3},{4,12},{12,4},... | collective-permute-start | bytes 2359304 | tf_op jit(solution)/shard_map/ppermute | solution.py:31
  55.2 3.6 %all-to-all-done = bf16[64,8,1280]{2,1,0:T(8,128)(2,1)S(1)} async-done(((bf16[64,8,1280]{2,1,0:T(8,128)(2,1)}), bf16[64,8,1280]{2,1,0:T(8,128)(2,1)S(1)}, u32[]{:S(2)}, u32[]{:S(2)}) %all-to-all-start) | async-done | bytes 1310752 | tf_op jit(solution)/shard_map/all_to_all | solution.py:355
  61.0 4.0 %collective-permute-start.9 = (bf16[800,256]{1,0:T(8,128)(2,1)S(1)}, bf16[800,256]{1,0:T(8,128)(2,1)S(1)}, u32[]{:S(2)}, u32[]{:S(2)}) collective-permute-start(bf16[800,256]{1,0:T(8,128)(2,1)S(1)} %shard_map.79), channel_id=1, source_target_pairs={{0,4},{2,6},{4,0},{6,2},{1,5},{3,7},{5,1},{7,3},{8,12},{10,14},{12... | collective-permute-start | bytes 1228808 | tf_op jit(solution)/shard_map/ppermute | solution.py:31
  65.1 2.1 %shard_map.78 = bf16[800,256]{1,0:T(8,128)(2,1)S(1)} custom-call(bf16[384,1536]{1,0:T(8,128)(2,1)S(1)} %get-tuple-element.21.rows_ref, bf16[16,256]{1,0:T(8,128)(2,1)S(1)} %get-tuple-element.22.tail_ref, bf16[16,256]{1,0:T(8,128)(2,1)S(1)} %get-tuple-element.26.router_ref, bf16[1536,256]{1,0:T(8,128)(2,1)} %collective-permute-done.5.own_ref, ...), custom_call_target="tpu_custom_call" | custom-call | flops 603979776 | bytes 3178496 | tf_op jit(solution)/shard_map/pallas_call | solution.py:45
  67.2 2.4 %collective-permute-start.7 = (bf16[800,256]{1,0:T(8,128)(2,1)S(1)}, bf16[800,256]{1,0:T(8,128)(2,1)S(1)}, u32[]{:S(2)}, u32[]{:S(2)}) collective-permute-start(bf16[800,256]{1,0:T(8,128)(2,1)S(1)} %shard_map.78), channel_id=1, source_target_pairs={{0,2},{2,4},{4,6},{6,0},{1,3},{3,5},{5,7},{7,1},{8,10},{10,12},{12... | collective-permute-start | bytes 1228808 | tf_op jit(solution)/shard_map/ppermute | solution.py:31
  69.6 2.1 %shard_map.77 = bf16[800,256]{1,0:T(8,128)(2,1)S(1)} custom-call(bf16[384,1536]{1,0:T(8,128)(2,1)S(1)} %get-tuple-element.21.rows_ref, bf16[16,256]{1,0:T(8,128)(2,1)S(1)} %get-tuple-element.22.tail_ref, bf16[16,256]{1,0:T(8,128)(2,1)S(1)} %get-tuple-element.26.router_ref, bf16[1536,256]{1,0:T(8,128)(2,1)} %collective-permute-done.2.own_ref, ...), custom_call_target="tpu_custom_call" | custom-call | flops 603979776 | bytes 3178496 | tf_op jit(solution)/shard_map/pallas_call | solution.py:45
  71.8 3.5 %collective-permute-start.4 = (bf16[800,256]{1,0:T(8,128)(2,1)S(1)}, bf16[800,256]{1,0:T(8,128)(2,1)S(1)}, u32[]{:S(2)}, u32[]{:S(2)}) collective-permute-start(bf16[800,256]{1,0:T(8,128)(2,1)S(1)} %shard_map.77), channel_id=1, source_target_pairs={{0,6},{2,0},{4,2},{6,4},{1,7},{3,1},{5,3},{7,5},{8,14},{10,8},{12,... | collective-permute-start | bytes 1228808 | tf_op jit(solution)/shard_map/ppermute | solution.py:31
  77.2 4.1 %collective-permute-done.7.refs_1_ = bf16[800,256]{1,0:T(8,128)(2,1)S(1)} collective-permute-done((bf16[800,256]{1,0:T(8,128)(2,1)S(1)}, bf16[800,256]{1,0:T(8,128)(2,1)S(1)}, u32[]{:S(2)}, u32[]{:S(2)}) %collective-permute-start.7) | collective-permute-done | bytes 409632 | tf_op jit(solution)/shard_map/ppermute | solution.py:31
  83.2 7.2 %collective-permute-start.14 = (bf16[800,128]{1,0:T(8,128)(2,1)S(1)}, bf16[800,128]{1,0:T(8,128)(2,1)S(1)}, u32[]{:S(2)}, u32[]{:S(2)}) collective-permute-start(bf16[800,128]{1,0:T(8,128)(2,1)S(1)} %shard_map.81.own_ref), channel_id=1, source_target_pairs={{0,1},{1,0},{2,3},{3,2},{4,5},{5,4},{6,7},{7,6},{8,9},{9,8},{10,11... | collective-permute-start | bytes 614408 | tf_op jit(solution)/shard_map/ppermute | solution.py:31
  90.4 3.1 %collective-permute-start.11 = (bf16[768,128]{1,0:T(8,128)(2,1)S(1)}, bf16[768,128]{1,0:T(8,128)(2,1)S(1)}, u32[]{:S(2)}, u32[]{:S(2)}) collective-permute-start(bf16[768,128]{1,0:T(8,128)(2,1)S(1)} %slice.4.refs_0_), channel_id=1, source_target_pairs={{0,2},{2,4},{4,6},{6,0},{1,3},{3,5},{5,7},{7,1},{8,10},{10,12},{12... | collective-permute-start | bytes 589832 | tf_op jit(solution)/shard_map/ppermute | solution.py:31
  93.5 2.4 %collective-permute-start.12 = (bf16[768,128]{1,0:T(8,128)(2,1)S(1)}, bf16[768,128]{1,0:T(8,128)(2,1)S(1)}, u32[]{:S(2)}, u32[]{:S(2)}) collective-permute-start(bf16[768,128]{1,0:T(8,128)(2,1)S(1)} %slice.4.refs_0_), channel_id=1, source_target_pairs={{0,4},{2,6},{4,0},{6,2},{1,5},{3,7},{5,1},{7,3},{8,12},{10,14},{12... | collective-permute-start | bytes 589832 | tf_op jit(solution)/shard_map/ppermute | solution.py:31
  96.0 3.0 %collective-permute-start.13 = (bf16[768,128]{1,0:T(8,128)(2,1)S(1)}, bf16[768,128]{1,0:T(8,128)(2,1)S(1)}, u32[]{:S(2)}, u32[]{:S(2)}) collective-permute-start(bf16[768,128]{1,0:T(8,128)(2,1)S(1)} %slice.4.refs_0_), channel_id=1, source_target_pairs={{0,6},{2,0},{4,2},{6,4},{1,7},{3,1},{5,3},{7,5},{8,14},{10,8},{12,... | collective-permute-start | bytes 589832 | tf_op jit(solution)/shard_map/ppermute | solution.py:31
  100.0 5.8 %all-to-all-start.1 = ((bf16[4,768,128]{2,1,0:T(8,128)(2,1)}), bf16[4,768,128]{2,1,0:T(8,128)(2,1)S(1)}, u32[]{:S(2)}, u32[]{:S(2)}) async-start(bf16[4,768,128]{2,1,0:T(8,128)(2,1)} %bitcast.6), calls=%async_computation.1 | async-start | bytes 1572864 | tf_op jit(solution)/shard_map/all_to_all | solution.py:425
  105.8 2.2 %collective-permute-done.13.refs_3_ = bf16[768,128]{1,0:T(8,128)(2,1)S(1)} collective-permute-done((bf16[768,128]{1,0:T(8,128)(2,1)S(1)}, bf16[768,128]{1,0:T(8,128)(2,1)S(1)}, u32[]{:S(2)}, u32[]{:S(2)}) %collective-permute-start.13) | collective-permute-done | bytes 196640 | tf_op jit(solution)/shard_map/ppermute | solution.py:31
  109.6 2.8 %shard_map.82 = (f32[384,768]{1,0:T(8,128)S(1)}, bf16[1024,768]{1,0:T(8,128)(2,1)S(1)}) custom-call(s32[2]{0:T(128)S(1)} %pad_add_fusion._.at_ref, bf16[1024,768]{1,0:T(8,128)(2,1)} %own_ref.1, bf16[1024,768]{1,0:T(8,128)(2,1)} %collective-permute-done.other_ref, bf16[768,128]{1,0:T(8,128)(2,1)S(1)} %slice.4.refs_0_, ...), custom_call_target="tpu_custom_call" | custom-call | flops 10000000000 | bytes 6684680 | tf_op jit(solution)/shard_map/pallas_call | solution.py:45
  113.4 2.4 %all-to-all-done.1 = bf16[4,768,128]{2,1,0:T(8,128)(2,1)S(1)} async-done(((bf16[4,768,128]{2,1,0:T(8,128)(2,1)}), bf16[4,768,128]{2,1,0:T(8,128)(2,1)S(1)}, u32[]{:S(2)}, u32[]{:S(2)}) %all-to-all-start.1) | async-done | bytes 786464 | tf_op jit(solution)/shard_map/all_to_all | solution.py:425
  117.1 2.3 %shard_map.84 = bf16[256,1152]{1,0:T(8,128)(2,1)} custom-call(bf16[1024,768]{1,0:T(8,128)(2,1)S(1)} %get-tuple-element.31.rest_ref, bf16[3072,128]{1,0:T(8,128)(2,1)S(1)} %bitcast.12, f32[384,768]{1,0:T(8,128)S(1)} %copy-done.1), custom_call_target="tpu_custom_call" | custom-call | flops 603979776 | bytes 4128768 | tf_op jit(solution)/shard_map/pallas_call | solution.py:45
  119.4 9.6 %all-to-all-start.2 = ((bf16[32,8,1152]{2,1,0:T(8,128)(2,1)}), bf16[32,8,1152]{2,1,0:T(8,128)(2,1)S(1)}, u32[]{:S(2)}, u32[]{:S(2)}) async-start(bf16[32,8,1152]{2,1,0:T(8,128)(2,1)} %bitcast.9), calls=%async_computation.2 | async-start | bytes 1179648 | tf_op jit(solution)/shard_map/all_to_all | solution.py:452
  129.2 18.3 %all-to-all-done.2 = bf16[32,8,1152]{2,1,0:T(8,128)(2,1)S(1)} async-done(((bf16[32,8,1152]{2,1,0:T(8,128)(2,1)}), bf16[32,8,1152]{2,1,0:T(8,128)(2,1)S(1)}, u32[]{:S(2)}, u32[]{:S(2)}) %all-to-all-start.2) | async-done | bytes 589856 | tf_op jit(solution)/shard_map/all_to_all | solution.py:452
  (51 shorter events, 26.9 us)
Async XLA Ops:
  0.0 5.5 %copy-start.7 = (f32[768]{0:T(1024)S(1)}, f32[768]{0:T(1024)}, u32[]{:S(2)}) copy-start(f32[768]{0:T(1024)} %param.8) | copy-start | bytes 9220
  0.0 5.6 %copy-start.2 = (bf16[32,768]{1,0:T(8,128)(2,1)S(1)}, bf16[32,768]{1,0:T(8,128)(2,1)}, u32[]{:S(2)}) copy-start(bf16[32,768]{1,0:T(8,128)(2,1)} %tok_ref.5) | copy-start | bytes 147460
  0.0 5.6 %copy-start.3 = (s32[32,2]{0,1:T(2,128)S(1)}, s32[32,2]{0,1:T(2,128)}, u32[]{:S(2)}) copy-start(s32[32,2]{0,1:T(2,128)} %param.10) | copy-start | bytes 772
  2.2 33.7 %collective-permute-start.1 = (bf16[1536,256]{1,0:T(8,128)(2,1)}, bf16[1536,256]{1,0:T(8,128)(2,1)S(1)}, u32[]{:S(2)}, u32[]{:S(2)}) collective-permute-start(bf16[1536,256]{1,0:T(8,128)(2,1)} %pad_maximum_fusion.3), channel_id=1, source_target_pairs={{0,4},{2,6},{4,0},{6,2},{1,5},{3,7},{5,1},{7,3},{8,12},{10,14},{12... | collective-permute-start | bytes 2359304 | tf_op jit(solution)/shard_map/ppermute | solution.py:31
  7.0 51.7 %all-to-all-start = ((bf16[64,8,1280]{2,1,0:T(8,128)(2,1)}), bf16[64,8,1280]{2,1,0:T(8,128)(2,1)S(1)}, u32[]{:S(2)}, u32[]{:S(2)}) async-start(bf16[64,8,1280]{2,1,0:T(8,128)(2,1)} %bitcast.3), calls=%async_computation | async-start | bytes 2621440 | tf_op jit(solution)/shard_map/all_to_all | solution.py:355
  27.0 21.9 %collective-permute-start.5 = (bf16[1536,256]{1,0:T(8,128)(2,1)S(1)}, bf16[1536,256]{1,0:T(8,128)(2,1)}, u32[]{:S(2)}, u32[]{:S(2)}) collective-permute-start(bf16[1536,256]{1,0:T(8,128)(2,1)S(1)} %get-tuple-element.28), channel_id=1, source_target_pairs={{0,6},{2,0},{4,2},{6,4},{1,7},{3,1},{5,3},{7,5},{8,14},{10,8},{12,... | collective-permute-start | bytes 2359304 | tf_op jit(solution)/shard_map/ppermute | solution.py:31
  28.9 21.9 %collective-permute-start.2 = (bf16[1536,256]{1,0:T(8,128)(2,1)S(1)}, bf16[1536,256]{1,0:T(8,128)(2,1)}, u32[]{:S(2)}, u32[]{:S(2)}) collective-permute-start(bf16[1536,256]{1,0:T(8,128)(2,1)S(1)} %get-tuple-element.27), channel_id=1, source_target_pairs={{0,2},{2,4},{4,6},{6,0},{1,3},{3,5},{5,7},{7,1},{8,10},{10,12},{12... | collective-permute-start | bytes 2359304 | tf_op jit(solution)/shard_map/ppermute | solution.py:31
  34.0 71.8 %collective-permute-start = (bf16[1024,768]{1,0:T(8,128)(2,1)}, bf16[1024,768]{1,0:T(8,128)(2,1)}, u32[]{:S(2)}, u32[]{:S(2)}) collective-permute-start(bf16[1024,768]{1,0:T(8,128)(2,1)} %own_ref.1), channel_id=1, source_target_pairs={{0,8},{8,0},{1,9},{9,1},{2,10},{10,2},{3,11},{11,3},{4,12},{12,4},... | collective-permute-start | bytes 4718600 | tf_op jit(solution)/shard_map/ppermute | solution.py:31
  36.0 23.1 %collective-permute-start.8 = (bf16[1536,256]{1,0:T(8,128)(2,1)S(1)}, bf16[1536,256]{1,0:T(8,128)(2,1)}, u32[]{:S(2)}, u32[]{:S(2)}) collective-permute-start(bf16[1536,256]{1,0:T(8,128)(2,1)S(1)} %get-tuple-element.29.own_ref), channel_id=1, source_target_pairs={{0,8},{8,0},{1,9},{9,1},{2,10},{10,2},{3,11},{11,3},{4,12},{12,4},... | collective-permute-start | bytes 2359304 | tf_op jit(solution)/shard_map/ppermute | solution.py:31
  48.9 16.2 %collective-permute-start.6 = (bf16[1536,256]{1,0:T(8,128)(2,1)}, bf16[1536,256]{1,0:T(8,128)(2,1)}, u32[]{:S(2)}, u32[]{:S(2)}) collective-permute-start(bf16[1536,256]{1,0:T(8,128)(2,1)} %collective-permute-done.5.own_ref), channel_id=1, source_target_pairs={{0,8},{8,0},{1,9},{9,1},{2,10},{10,2},{3,11},{11,3},{4,12},{12,4},... | collective-permute-start | bytes 2359304 | tf_op jit(solution)/shard_map/ppermute | solution.py:31
  50.8 18.8 %collective-permute-start.3 = (bf16[1536,256]{1,0:T(8,128)(2,1)}, bf16[1536,256]{1,0:T(8,128)(2,1)}, u32[]{:S(2)}, u32[]{:S(2)}) collective-permute-start(bf16[1536,256]{1,0:T(8,128)(2,1)} %collective-permute-done.2.own_ref), channel_id=1, source_target_pairs={{0,8},{8,0},{1,9},{9,1},{2,10},{10,2},{3,11},{11,3},{4,12},{12,4},... | collective-permute-start | bytes 2359304 | tf_op jit(solution)/shard_map/ppermute | solution.py:31
  53.2 22.0 %collective-permute-start.10 = (bf16[1536,256]{1,0:T(8,128)(2,1)S(1)}, bf16[1536,256]{1,0:T(8,128)(2,1)}, u32[]{:S(2)}, u32[]{:S(2)}) collective-permute-start(bf16[1536,256]{1,0:T(8,128)(2,1)S(1)} %get-tuple-element.30.own_ref), channel_id=1, source_target_pairs={{0,8},{8,0},{1,9},{9,1},{2,10},{10,2},{3,11},{11,3},{4,12},{12,4},... | collective-permute-start | bytes 2359304 | tf_op jit(solution)/shard_map/ppermute | solution.py:31
  61.0 16.2 %collective-permute-start.9 = (bf16[800,256]{1,0:T(8,128)(2,1)S(1)}, bf16[800,256]{1,0:T(8,128)(2,1)S(1)}, u32[]{:S(2)}, u32[]{:S(2)}) collective-permute-start(bf16[800,256]{1,0:T(8,128)(2,1)S(1)} %shard_map.79), channel_id=1, source_target_pairs={{0,4},{2,6},{4,0},{6,2},{1,5},{3,7},{5,1},{7,3},{8,12},{10,14},{12... | collective-permute-start | bytes 1228808 | tf_op jit(solution)/shard_map/ppermute | solution.py:31
  67.2 14.1 %collective-permute-start.7 = (bf16[800,256]{1,0:T(8,128)(2,1)S(1)}, bf16[800,256]{1,0:T(8,128)(2,1)S(1)}, u32[]{:S(2)}, u32[]{:S(2)}) collective-permute-start(bf16[800,256]{1,0:T(8,128)(2,1)S(1)} %shard_map.78), channel_id=1, source_target_pairs={{0,2},{2,4},{4,6},{6,0},{1,3},{3,5},{5,7},{7,1},{8,10},{10,12},{12... | collective-permute-start | bytes 1228808 | tf_op jit(solution)/shard_map/ppermute | solution.py:31
  71.8 11.1 %collective-permute-start.4 = (bf16[800,256]{1,0:T(8,128)(2,1)S(1)}, bf16[800,256]{1,0:T(8,128)(2,1)S(1)}, u32[]{:S(2)}, u32[]{:S(2)}) collective-permute-start(bf16[800,256]{1,0:T(8,128)(2,1)S(1)} %shard_map.77), channel_id=1, source_target_pairs={{0,6},{2,0},{4,2},{6,4},{1,7},{3,1},{5,3},{7,5},{8,14},{10,8},{12,... | collective-permute-start | bytes 1228808 | tf_op jit(solution)/shard_map/ppermute | solution.py:31
  83.2 15.8 %collective-permute-start.14 = (bf16[800,128]{1,0:T(8,128)(2,1)S(1)}, bf16[800,128]{1,0:T(8,128)(2,1)S(1)}, u32[]{:S(2)}, u32[]{:S(2)}) collective-permute-start(bf16[800,128]{1,0:T(8,128)(2,1)S(1)} %shard_map.81.own_ref), channel_id=1, source_target_pairs={{0,1},{1,0},{2,3},{3,2},{4,5},{5,4},{6,7},{7,6},{8,9},{9,8},{10,11... | collective-permute-start | bytes 614408 | tf_op jit(solution)/shard_map/ppermute | solution.py:31
  90.4 15.4 %collective-permute-start.11 = (bf16[768,128]{1,0:T(8,128)(2,1)S(1)}, bf16[768,128]{1,0:T(8,128)(2,1)S(1)}, u32[]{:S(2)}, u32[]{:S(2)}) collective-permute-start(bf16[768,128]{1,0:T(8,128)(2,1)S(1)} %slice.4.refs_0_), channel_id=1, source_target_pairs={{0,2},{2,4},{4,6},{6,0},{1,3},{3,5},{5,7},{7,1},{8,10},{10,12},{12... | collective-permute-start | bytes 589832 | tf_op jit(solution)/shard_map/ppermute | solution.py:31
  93.5 12.3 %collective-permute-start.12 = (bf16[768,128]{1,0:T(8,128)(2,1)S(1)}, bf16[768,128]{1,0:T(8,128)(2,1)S(1)}, u32[]{:S(2)}, u32[]{:S(2)}) collective-permute-start(bf16[768,128]{1,0:T(8,128)(2,1)S(1)} %slice.4.refs_0_), channel_id=1, source_target_pairs={{0,4},{2,6},{4,0},{6,2},{1,5},{3,7},{5,1},{7,3},{8,12},{10,14},{12... | collective-permute-start | bytes 589832 | tf_op jit(solution)/shard_map/ppermute | solution.py:31
  96.0 12.0 %collective-permute-start.13 = (bf16[768,128]{1,0:T(8,128)(2,1)S(1)}, bf16[768,128]{1,0:T(8,128)(2,1)S(1)}, u32[]{:S(2)}, u32[]{:S(2)}) collective-permute-start(bf16[768,128]{1,0:T(8,128)(2,1)S(1)} %slice.4.refs_0_), channel_id=1, source_target_pairs={{0,6},{2,0},{4,2},{6,4},{1,7},{3,1},{5,3},{7,5},{8,14},{10,8},{12,... | collective-permute-start | bytes 589832 | tf_op jit(solution)/shard_map/ppermute | solution.py:31
  100.0 15.8 %all-to-all-start.1 = ((bf16[4,768,128]{2,1,0:T(8,128)(2,1)}), bf16[4,768,128]{2,1,0:T(8,128)(2,1)S(1)}, u32[]{:S(2)}, u32[]{:S(2)}) async-start(bf16[4,768,128]{2,1,0:T(8,128)(2,1)} %bitcast.6), calls=%async_computation.1 | async-start | bytes 1572864 | tf_op jit(solution)/shard_map/all_to_all | solution.py:425
  108.7 0.9 copy-start.5
  112.4 1.0 copy-start
  115.8 1.3 copy-start.1
  119.4 28.1 %all-to-all-start.2 = ((bf16[32,8,1152]{2,1,0:T(8,128)(2,1)}), bf16[32,8,1152]{2,1,0:T(8,128)(2,1)S(1)}, u32[]{:S(2)}, u32[]{:S(2)}) async-start(bf16[32,8,1152]{2,1,0:T(8,128)(2,1)} %bitcast.9), calls=%async_computation.2 | async-start | bytes 1179648 | tf_op jit(solution)/shard_map/all_to_all | solution.py:452
  (2 other events, 1.4 us)

commit v9 on v7

--- a/solution.py
+++ b/solution.py
@@ -217,7 +217,8 @@
             rest_ref[(c * nx + x) * units : (c * nx + x + 1) * units, :] = w_ref[
                 pl.ds(pl.multiple_of(t * units, units), units), :
             ]
-    out_ref[...] = down_part(at_ref, 0, homes * CAP, nx, nz, pieces, own_ref, other_ref)
+    total = down_part(at_ref, 0, homes * CAP, nx, nz, pieces, own_ref, other_ref)
+    out_ref[...] = total.astype(BF16)
 
 
 def down_last_kernel(homes, nx, first_ref, rest_ref, hid_ref, out_ref):
@@ -225,7 +226,7 @@
     half = width // 2
     n, n_main = homes * CAP, homes * MAIN
     depth = rest_ref.shape[0] // 2
-    total = first_ref[...]
+    total = first_ref[...].astype(F32)
     for c in range(2):
         starts = [(2 * x + c) * n for x in range(nx)]
         wide = jnp.concatenate([hid_ref[at : at + n, :] for at in starts], 1)
@@ -425,7 +426,7 @@
     first, w_rest = local_kernel(
         functools.partial(down_first_kernel, homes, nx, nz),
         [
-            jax.ShapeDtypeStruct((n, width), F32),
+            jax.ShapeDtypeStruct((n, width), BF16),
             jax.ShapeDtypeStruct((2 * nx * units, width), BF16),
         ],
         at,

time: 151 us -> 149 us (0.987)
  waiting for transfers between devices: 42.6 us -> 39.5 us
  local copies, waits for them, and re-layouts: 7.36 us -> 9.18 us
    unnamed x16 -> x24, local copies, waits for them, and re-layouts: 4.38 us -> 6.2 us
    all_to_all x1, waiting for transfers between devices: 2.41 us -> 0.67 us  [shards(): lax.all_to_all(other_rows.reshape(nx, 2 * n, units), 'x', 0, 0, tiled=True)]
where the time goes in v9:
time: 149 us; the launch traced here: 147 us
  starting transfers between devices  78.4 us (53%)
  waiting for transfers between devices  39.5 us (27%)
  Pallas kernels  18 us (12%)
  local copies, waits for them, and re-layouts  9.18 us (6%)
    ppermute x15, starting transfers between devices, shift(): lax.ppermute(value, axis, [(i, (i + by) % size) for i in range(size)])  46.5 us
    all_to_all x1, waiting for transfers between devices, shards(): lax.all_to_all(back.reshape(homes, MAIN, span), HOMES, 0, 0, tiled=True)  18.3 us
    pallas_call x14, Pallas kernels, local_kernel(): pl.pallas_call(body, out_shape=out, in_specs=[pl.BlockSpec(memory_space=s...  18 us
    ppermute x15, waiting for transfers between devices, shift(): lax.ppermute(value, axis, [(i, (i + by) % size) for i in range(size)])  17 us
    all_to_all x1, starting transfers between devices, shards(): lax.all_to_all(outgoing.reshape(nz * homes, MAIN, span + SIDE), DISPATCH,...  16.6 us
    all_to_all x1, starting transfers between devices, shards(): lax.all_to_all(back.reshape(homes, MAIN, span), HOMES, 0, 0, tiled=True)  9.51 us
    unnamed x24, local copies, waits for them, and re-layouts  6.2 us
    all_to_all x1, starting transfers between devices, shards(): lax.all_to_all(other_rows.reshape(nx, 2 * n, units), 'x', 0, 0, tiled=True)  5.77 us
  transfers between devices with their start and end apart: 18, of which 7 were waited for; matrix products, arithmetic and copies ran while one was open for 1% of the time, Pallas kernels for 10%

profile of v9, /device:TPU:6, one launch (start us, length us, event | category | flops | bytes accessed | tf_op | source)
XLA Modules:
  0.0 146.9 jit_solution(2692750070623629761)
XLA Ops:
  2.2 3.3 %collective-permute-start.1 = (bf16[1536,256]{1,0:T(8,128)(2,1)}, bf16[1536,256]{1,0:T(8,128)(2,1)S(1)}, u32[]{:S(2)}, u32[]{:S(2)}) collective-permute-start(bf16[1536,256]{1,0:T(8,128)(2,1)} %pad_maximum_fusion.3), channel_id=1, source_target_pairs={{0,4},{2,6},{4,0},{6,2},{1,5},{3,7},{5,1},{7,3},{8,12},{10,14},{12... | collective-permute-start | bytes 2359304 | tf_op jit(solution)/shard_map/ppermute | solution.py:31
  7.0 16.6 %all-to-all-start = ((bf16[64,8,1280]{2,1,0:T(8,128)(2,1)}), bf16[64,8,1280]{2,1,0:T(8,128)(2,1)S(1)}, u32[]{:S(2)}, u32[]{:S(2)}) async-start(bf16[64,8,1280]{2,1,0:T(8,128)(2,1)} %bitcast.3), calls=%async_computation | async-start | bytes 2621440 | tf_op jit(solution)/shard_map/all_to_all | solution.py:353
  26.9 1.9 %collective-permute-start.5 = (bf16[1536,256]{1,0:T(8,128)(2,1)S(1)}, bf16[1536,256]{1,0:T(8,128)(2,1)}, u32[]{:S(2)}, u32[]{:S(2)}) collective-permute-start(bf16[1536,256]{1,0:T(8,128)(2,1)S(1)} %get-tuple-element.28), channel_id=1, source_target_pairs={{0,6},{2,0},{4,2},{6,4},{1,7},{3,1},{5,3},{7,5},{8,14},{10,8},{12,... | collective-permute-start | bytes 2359304 | tf_op jit(solution)/shard_map/ppermute | solution.py:31
  28.9 5.1 %collective-permute-start.2 = (bf16[1536,256]{1,0:T(8,128)(2,1)S(1)}, bf16[1536,256]{1,0:T(8,128)(2,1)}, u32[]{:S(2)}, u32[]{:S(2)}) collective-permute-start(bf16[1536,256]{1,0:T(8,128)(2,1)S(1)} %get-tuple-element.27), channel_id=1, source_target_pairs={{0,2},{2,4},{4,6},{6,0},{1,3},{3,5},{5,7},{7,1},{8,10},{10,12},{12... | collective-permute-start | bytes 2359304 | tf_op jit(solution)/shard_map/ppermute | solution.py:31
  34.0 1.9 %collective-permute-start = (bf16[1024,768]{1,0:T(8,128)(2,1)}, bf16[1024,768]{1,0:T(8,128)(2,1)}, u32[]{:S(2)}, u32[]{:S(2)}) collective-permute-start(bf16[1024,768]{1,0:T(8,128)(2,1)} %own_ref.1), channel_id=1, source_target_pairs={{0,8},{8,0},{1,9},{9,1},{2,10},{10,2},{3,11},{11,3},{4,12},{12,4},... | collective-permute-start | bytes 4718600 | tf_op jit(solution)/shard_map/ppermute | solution.py:31
  36.0 2.4 %collective-permute-start.8 = (bf16[1536,256]{1,0:T(8,128)(2,1)S(1)}, bf16[1536,256]{1,0:T(8,128)(2,1)}, u32[]{:S(2)}, u32[]{:S(2)}) collective-permute-start(bf16[1536,256]{1,0:T(8,128)(2,1)S(1)} %get-tuple-element.29.own_ref), channel_id=1, source_target_pairs={{0,8},{8,0},{1,9},{9,1},{2,10},{10,2},{3,11},{11,3},{4,12},{12,4},... | collective-permute-start | bytes 2359304 | tf_op jit(solution)/shard_map/ppermute | solution.py:31
  38.4 10.5 %collective-permute-done.5.own_ref = bf16[1536,256]{1,0:T(8,128)(2,1)} collective-permute-done((bf16[1536,256]{1,0:T(8,128)(2,1)S(1)}, bf16[1536,256]{1,0:T(8,128)(2,1)}, u32[]{:S(2)}, u32[]{:S(2)}) %collective-permute-start.5) | collective-permute-done | bytes 786464 | tf_op jit(solution)/shard_map/ppermute | solution.py:31
  50.8 2.4 %collective-permute-start.3 = (bf16[1536,256]{1,0:T(8,128)(2,1)}, bf16[1536,256]{1,0:T(8,128)(2,1)}, u32[]{:S(2)}, u32[]{:S(2)}) collective-permute-start(bf16[1536,256]{1,0:T(8,128)(2,1)} %collective-permute-done.2.own_ref), channel_id=1, source_target_pairs={{0,8},{8,0},{1,9},{9,1},{2,10},{10,2},{3,11},{11,3},{4,12},{12,4},... | collective-permute-start | bytes 2359304 | tf_op jit(solution)/shard_map/ppermute | solution.py:31
  55.2 3.6 %all-to-all-done = bf16[64,8,1280]{2,1,0:T(8,128)(2,1)S(1)} async-done(((bf16[64,8,1280]{2,1,0:T(8,128)(2,1)}), bf16[64,8,1280]{2,1,0:T(8,128)(2,1)S(1)}, u32[]{:S(2)}, u32[]{:S(2)}) %all-to-all-start) | async-done | bytes 1310752 | tf_op jit(solution)/shard_map/all_to_all | solution.py:353
  61.0 4.0 %collective-permute-start.9 = (bf16[800,256]{1,0:T(8,128)(2,1)S(1)}, bf16[800,256]{1,0:T(8,128)(2,1)S(1)}, u32[]{:S(2)}, u32[]{:S(2)}) collective-permute-start(bf16[800,256]{1,0:T(8,128)(2,1)S(1)} %shard_map.79), channel_id=1, source_target_pairs={{0,4},{2,6},{4,0},{6,2},{1,5},{3,7},{5,1},{7,3},{8,12},{10,14},{12... | collective-permute-start | bytes 1228808 | tf_op jit(solution)/shard_map/ppermute | solution.py:31
  65.1 2.1 %shard_map.78 = bf16[800,256]{1,0:T(8,128)(2,1)S(1)} custom-call(bf16[384,1536]{1,0:T(8,128)(2,1)S(1)} %get-tuple-element.21.rows_ref, bf16[16,256]{1,0:T(8,128)(2,1)S(1)} %get-tuple-element.22.tail_ref, bf16[16,256]{1,0:T(8,128)(2,1)S(1)} %get-tuple-element.26.router_ref, bf16[1536,256]{1,0:T(8,128)(2,1)} %collective-permute-done.5.own_ref, ...), custom_call_target="tpu_custom_call" | custom-call | flops 603979776 | bytes 3178496 | tf_op jit(solution)/shard_map/pallas_call | solution.py:45
  67.2 2.4 %collective-permute-start.7 = (bf16[800,256]{1,0:T(8,128)(2,1)S(1)}, bf16[800,256]{1,0:T(8,128)(2,1)S(1)}, u32[]{:S(2)}, u32[]{:S(2)}) collective-permute-start(bf16[800,256]{1,0:T(8,128)(2,1)S(1)} %shard_map.78), channel_id=1, source_target_pairs={{0,2},{2,4},{4,6},{6,0},{1,3},{3,5},{5,7},{7,1},{8,10},{10,12},{12... | collective-permute-start | bytes 1228808 | tf_op jit(solution)/shard_map/ppermute | solution.py:31
  69.6 2.1 %shard_map.77 = bf16[800,256]{1,0:T(8,128)(2,1)S(1)} custom-call(bf16[384,1536]{1,0:T(8,128)(2,1)S(1)} %get-tuple-element.21.rows_ref, bf16[16,256]{1,0:T(8,128)(2,1)S(1)} %get-tuple-element.22.tail_ref, bf16[16,256]{1,0:T(8,128)(2,1)S(1)} %get-tuple-element.26.router_ref, bf16[1536,256]{1,0:T(8,128)(2,1)} %collective-permute-done.2.own_ref, ...), custom_call_target="tpu_custom_call" | custom-call | flops 603979776 | bytes 3178496 | tf_op jit(solution)/shard_map/pallas_call | solution.py:45
  71.8 3.5 %collective-permute-start.4 = (bf16[800,256]{1,0:T(8,128)(2,1)S(1)}, bf16[800,256]{1,0:T(8,128)(2,1)S(1)}, u32[]{:S(2)}, u32[]{:S(2)}) collective-permute-start(bf16[800,256]{1,0:T(8,128)(2,1)S(1)} %shard_map.77), channel_id=1, source_target_pairs={{0,6},{2,0},{4,2},{6,4},{1,7},{3,1},{5,3},{7,5},{8,14},{10,8},{12,... | collective-permute-start | bytes 1228808 | tf_op jit(solution)/shard_map/ppermute | solution.py:31
  77.2 4.1 %collective-permute-done.7.refs_1_ = bf16[800,256]{1,0:T(8,128)(2,1)S(1)} collective-permute-done((bf16[800,256]{1,0:T(8,128)(2,1)S(1)}, bf16[800,256]{1,0:T(8,128)(2,1)S(1)}, u32[]{:S(2)}, u32[]{:S(2)}) %collective-permute-start.7) | collective-permute-done | bytes 409632 | tf_op jit(solution)/shard_map/ppermute | solution.py:31
  83.2 7.2 %collective-permute-start.14 = (bf16[800,128]{1,0:T(8,128)(2,1)S(1)}, bf16[800,128]{1,0:T(8,128)(2,1)S(1)}, u32[]{:S(2)}, u32[]{:S(2)}) collective-permute-start(bf16[800,128]{1,0:T(8,128)(2,1)S(1)} %shard_map.81.own_ref), channel_id=1, source_target_pairs={{0,1},{1,0},{2,3},{3,2},{4,5},{5,4},{6,7},{7,6},{8,9},{9,8},{10,11... | collective-permute-start | bytes 614408 | tf_op jit(solution)/shard_map/ppermute | solution.py:31
  90.4 3.1 %collective-permute-start.11 = (bf16[768,128]{1,0:T(8,128)(2,1)S(1)}, bf16[768,128]{1,0:T(8,128)(2,1)S(1)}, u32[]{:S(2)}, u32[]{:S(2)}) collective-permute-start(bf16[768,128]{1,0:T(8,128)(2,1)S(1)} %slice.4.refs_0_), channel_id=1, source_target_pairs={{0,2},{2,4},{4,6},{6,0},{1,3},{3,5},{5,7},{7,1},{8,10},{10,12},{12... | collective-permute-start | bytes 589832 | tf_op jit(solution)/shard_map/ppermute | solution.py:31
  93.5 2.4 %collective-permute-start.12 = (bf16[768,128]{1,0:T(8,128)(2,1)S(1)}, bf16[768,128]{1,0:T(8,128)(2,1)S(1)}, u32[]{:S(2)}, u32[]{:S(2)}) collective-permute-start(bf16[768,128]{1,0:T(8,128)(2,1)S(1)} %slice.4.refs_0_), channel_id=1, source_target_pairs={{0,4},{2,6},{4,0},{6,2},{1,5},{3,7},{5,1},{7,3},{8,12},{10,14},{12... | collective-permute-start | bytes 589832 | tf_op jit(solution)/shard_map/ppermute | solution.py:31
  96.0 3.0 %collective-permute-start.13 = (bf16[768,128]{1,0:T(8,128)(2,1)S(1)}, bf16[768,128]{1,0:T(8,128)(2,1)S(1)}, u32[]{:S(2)}, u32[]{:S(2)}) collective-permute-start(bf16[768,128]{1,0:T(8,128)(2,1)S(1)} %slice.4.refs_0_), channel_id=1, source_target_pairs={{0,6},{2,0},{4,2},{6,4},{1,7},{3,1},{5,3},{7,5},{8,14},{10,8},{12,... | collective-permute-start | bytes 589832 | tf_op jit(solution)/shard_map/ppermute | solution.py:31
  100.0 5.8 %all-to-all-start.1 = ((bf16[4,768,128]{2,1,0:T(8,128)(2,1)}), bf16[4,768,128]{2,1,0:T(8,128)(2,1)S(1)}, u32[]{:S(2)}, u32[]{:S(2)}) async-start(bf16[4,768,128]{2,1,0:T(8,128)(2,1)} %bitcast.6), calls=%async_computation.1 | async-start | bytes 1572864 | tf_op jit(solution)/shard_map/all_to_all | solution.py:423
  112.3 2.8 %shard_map.82 = (bf16[384,768]{1,0:T(8,128)(2,1)S(1)}, bf16[1024,768]{1,0:T(8,128)(2,1)S(1)}) custom-call(s32[2]{0:T(128)S(1)} %pad_add_fusion._.at_ref, bf16[1024,768]{1,0:T(8,128)(2,1)} %own_ref.1, bf16[1024,768]{1,0:T(8,128)(2,1)} %collective-permute-done.other_ref, bf16[768,128]{1,0:T(8,128)(2,1)S(1)} %copy-done.2, bf16[768,128]{1,0:T(8,128)(2,1)S(1)} %copy-done.5, ...), custom_call_target="tpu_custom_call" | custom-call | flops 10000000000 | bytes 6094856 | tf_op jit(solution)/shard_map/pallas_call | solution.py:45
  115.8 2.0 %shard_map.84 = bf16[256,1152]{1,0:T(8,128)(2,1)} custom-call(bf16[384,768]{1,0:T(8,128)(2,1)S(1)} %get-tuple-element.31.first_ref, bf16[1024,768]{1,0:T(8,128)(2,1)S(1)} %get-tuple-element.32.rest_ref, bf16[3072,128]{1,0:T(8,128)(2,1)S(1)} %bitcast.12), custom_call_target="tpu_custom_call" | custom-call | flops 603979776 | bytes 3538944 | tf_op jit(solution)/shard_map/pallas_call | solution.py:45
  117.8 9.5 %all-to-all-start.2 = ((bf16[32,8,1152]{2,1,0:T(8,128)(2,1)}), bf16[32,8,1152]{2,1,0:T(8,128)(2,1)S(1)}, u32[]{:S(2)}, u32[]{:S(2)}) async-start(bf16[32,8,1152]{2,1,0:T(8,128)(2,1)} %bitcast.9), calls=%async_computation.2 | async-start | bytes 1179648 | tf_op jit(solution)/shard_map/all_to_all | solution.py:448
  127.6 18.3 %all-to-all-done.2 = bf16[32,8,1152]{2,1,0:T(8,128)(2,1)S(1)} async-done(((bf16[32,8,1152]{2,1,0:T(8,128)(2,1)}), bf16[32,8,1152]{2,1,0:T(8,128)(2,1)S(1)}, u32[]{:S(2)}, u32[]{:S(2)}) %all-to-all-start.2) | async-done | bytes 589856 | tf_op jit(solution)/shard_map/all_to_all | solution.py:448
  (59 shorter events, 26.4 us)
Async XLA Ops:
  0.0 5.5 %copy-start.11 = (f32[768]{0:T(1024)S(1)}, f32[768]{0:T(1024)}, u32[]{:S(2)}) copy-start(f32[768]{0:T(1024)} %param.8) | copy-start | bytes 9220
  0.0 5.5 %copy-start = (bf16[32,768]{1,0:T(8,128)(2,1)S(1)}, bf16[32,768]{1,0:T(8,128)(2,1)}, u32[]{:S(2)}) copy-start(bf16[32,768]{1,0:T(8,128)(2,1)} %tok_ref.5) | copy-start | bytes 147460
  0.0 5.5 %copy-start.3 = (s32[32,2]{0,1:T(2,128)S(1)}, s32[32,2]{0,1:T(2,128)}, u32[]{:S(2)}) copy-start(s32[32,2]{0,1:T(2,128)} %param.10) | copy-start | bytes 772
  2.2 33.7 %collective-permute-start.1 = (bf16[1536,256]{1,0:T(8,128)(2,1)}, bf16[1536,256]{1,0:T(8,128)(2,1)S(1)}, u32[]{:S(2)}, u32[]{:S(2)}) collective-permute-start(bf16[1536,256]{1,0:T(8,128)(2,1)} %pad_maximum_fusion.3), channel_id=1, source_target_pairs={{0,4},{2,6},{4,0},{6,2},{1,5},{3,7},{5,1},{7,3},{8,12},{10,14},{12... | collective-permute-start | bytes 2359304 | tf_op jit(solution)/shard_map/ppermute | solution.py:31
  7.0 51.7 %all-to-all-start = ((bf16[64,8,1280]{2,1,0:T(8,128)(2,1)}), bf16[64,8,1280]{2,1,0:T(8,128)(2,1)S(1)}, u32[]{:S(2)}, u32[]{:S(2)}) async-start(bf16[64,8,1280]{2,1,0:T(8,128)(2,1)} %bitcast.3), calls=%async_computation | async-start | bytes 2621440 | tf_op jit(solution)/shard_map/all_to_all | solution.py:353
  26.9 21.9 %collective-permute-start.5 = (bf16[1536,256]{1,0:T(8,128)(2,1)S(1)}, bf16[1536,256]{1,0:T(8,128)(2,1)}, u32[]{:S(2)}, u32[]{:S(2)}) collective-permute-start(bf16[1536,256]{1,0:T(8,128)(2,1)S(1)} %get-tuple-element.28), channel_id=1, source_target_pairs={{0,6},{2,0},{4,2},{6,4},{1,7},{3,1},{5,3},{7,5},{8,14},{10,8},{12,... | collective-permute-start | bytes 2359304 | tf_op jit(solution)/shard_map/ppermute | solution.py:31
  28.9 21.9 %collective-permute-start.2 = (bf16[1536,256]{1,0:T(8,128)(2,1)S(1)}, bf16[1536,256]{1,0:T(8,128)(2,1)}, u32[]{:S(2)}, u32[]{:S(2)}) collective-permute-start(bf16[1536,256]{1,0:T(8,128)(2,1)S(1)} %get-tuple-element.27), channel_id=1, source_target_pairs={{0,2},{2,4},{4,6},{6,0},{1,3},{3,5},{5,7},{7,1},{8,10},{10,12},{12... | collective-permute-start | bytes 2359304 | tf_op jit(solution)/shard_map/ppermute | solution.py:31
  34.0 71.7 %collective-permute-start = (bf16[1024,768]{1,0:T(8,128)(2,1)}, bf16[1024,768]{1,0:T(8,128)(2,1)}, u32[]{:S(2)}, u32[]{:S(2)}) collective-permute-start(bf16[1024,768]{1,0:T(8,128)(2,1)} %own_ref.1), channel_id=1, source_target_pairs={{0,8},{8,0},{1,9},{9,1},{2,10},{10,2},{3,11},{11,3},{4,12},{12,4},... | collective-permute-start | bytes 4718600 | tf_op jit(solution)/shard_map/ppermute | solution.py:31
  36.0 23.1 %collective-permute-start.8 = (bf16[1536,256]{1,0:T(8,128)(2,1)S(1)}, bf16[1536,256]{1,0:T(8,128)(2,1)}, u32[]{:S(2)}, u32[]{:S(2)}) collective-permute-start(bf16[1536,256]{1,0:T(8,128)(2,1)S(1)} %get-tuple-element.29.own_ref), channel_id=1, source_target_pairs={{0,8},{8,0},{1,9},{9,1},{2,10},{10,2},{3,11},{11,3},{4,12},{12,4},... | collective-permute-start | bytes 2359304 | tf_op jit(solution)/shard_map/ppermute | solution.py:31
  48.9 16.2 %collective-permute-start.6 = (bf16[1536,256]{1,0:T(8,128)(2,1)}, bf16[1536,256]{1,0:T(8,128)(2,1)}, u32[]{:S(2)}, u32[]{:S(2)}) collective-permute-start(bf16[1536,256]{1,0:T(8,128)(2,1)} %collective-permute-done.5.own_ref), channel_id=1, source_target_pairs={{0,8},{8,0},{1,9},{9,1},{2,10},{10,2},{3,11},{11,3},{4,12},{12,4},... | collective-permute-start | bytes 2359304 | tf_op jit(solution)/shard_map/ppermute | solution.py:31
  50.8 18.8 %collective-permute-start.3 = (bf16[1536,256]{1,0:T(8,128)(2,1)}, bf16[1536,256]{1,0:T(8,128)(2,1)}, u32[]{:S(2)}, u32[]{:S(2)}) collective-permute-start(bf16[1536,256]{1,0:T(8,128)(2,1)} %collective-permute-done.2.own_ref), channel_id=1, source_target_pairs={{0,8},{8,0},{1,9},{9,1},{2,10},{10,2},{3,11},{11,3},{4,12},{12,4},... | collective-permute-start | bytes 2359304 | tf_op jit(solution)/shard_map/ppermute | solution.py:31
  53.2 22.0 %collective-permute-start.10 = (bf16[1536,256]{1,0:T(8,128)(2,1)S(1)}, bf16[1536,256]{1,0:T(8,128)(2,1)}, u32[]{:S(2)}, u32[]{:S(2)}) collective-permute-start(bf16[1536,256]{1,0:T(8,128)(2,1)S(1)} %get-tuple-element.30.own_ref), channel_id=1, source_target_pairs={{0,8},{8,0},{1,9},{9,1},{2,10},{10,2},{3,11},{11,3},{4,12},{12,4},... | collective-permute-start | bytes 2359304 | tf_op jit(solution)/shard_map/ppermute | solution.py:31
  61.0 16.2 %collective-permute-start.9 = (bf16[800,256]{1,0:T(8,128)(2,1)S(1)}, bf16[800,256]{1,0:T(8,128)(2,1)S(1)}, u32[]{:S(2)}, u32[]{:S(2)}) collective-permute-start(bf16[800,256]{1,0:T(8,128)(2,1)S(1)} %shard_map.79), channel_id=1, source_target_pairs={{0,4},{2,6},{4,0},{6,2},{1,5},{3,7},{5,1},{7,3},{8,12},{10,14},{12... | collective-permute-start | bytes 1228808 | tf_op jit(solution)/shard_map/ppermute | solution.py:31
  67.2 14.1 %collective-permute-start.7 = (bf16[800,256]{1,0:T(8,128)(2,1)S(1)}, bf16[800,256]{1,0:T(8,128)(2,1)S(1)}, u32[]{:S(2)}, u32[]{:S(2)}) collective-permute-start(bf16[800,256]{1,0:T(8,128)(2,1)S(1)} %shard_map.78), channel_id=1, source_target_pairs={{0,2},{2,4},{4,6},{6,0},{1,3},{3,5},{5,7},{7,1},{8,10},{10,12},{12... | collective-permute-start | bytes 1228808 | tf_op jit(solution)/shard_map/ppermute | solution.py:31
  71.8 11.1 %collective-permute-start.4 = (bf16[800,256]{1,0:T(8,128)(2,1)S(1)}, bf16[800,256]{1,0:T(8,128)(2,1)S(1)}, u32[]{:S(2)}, u32[]{:S(2)}) collective-permute-start(bf16[800,256]{1,0:T(8,128)(2,1)S(1)} %shard_map.77), channel_id=1, source_target_pairs={{0,6},{2,0},{4,2},{6,4},{1,7},{3,1},{5,3},{7,5},{8,14},{10,8},{12,... | collective-permute-start | bytes 1228808 | tf_op jit(solution)/shard_map/ppermute | solution.py:31
  83.2 15.8 %collective-permute-start.14 = (bf16[800,128]{1,0:T(8,128)(2,1)S(1)}, bf16[800,128]{1,0:T(8,128)(2,1)S(1)}, u32[]{:S(2)}, u32[]{:S(2)}) collective-permute-start(bf16[800,128]{1,0:T(8,128)(2,1)S(1)} %shard_map.81.own_ref), channel_id=1, source_target_pairs={{0,1},{1,0},{2,3},{3,2},{4,5},{5,4},{6,7},{7,6},{8,9},{9,8},{10,11... | collective-permute-start | bytes 614408 | tf_op jit(solution)/shard_map/ppermute | solution.py:31
  90.4 16.0 %copy-start.1 = (bf16[768,128]{1,0:T(8,128)(2,1)}, bf16[768,128]{1,0:T(8,128)(2,1)S(1)}, u32[]{:S(2)}) copy-start(bf16[768,128]{1,0:T(8,128)(2,1)S(1)} %slice.4.refs_0_) | copy-start | bytes 589828
  90.4 15.3 %collective-permute-start.11 = (bf16[768,128]{1,0:T(8,128)(2,1)S(1)}, bf16[768,128]{1,0:T(8,128)(2,1)S(1)}, u32[]{:S(2)}, u32[]{:S(2)}) collective-permute-start(bf16[768,128]{1,0:T(8,128)(2,1)S(1)} %slice.4.refs_0_), channel_id=1, source_target_pairs={{0,2},{2,4},{4,6},{6,0},{1,3},{3,5},{5,7},{7,1},{8,10},{10,12},{12... | collective-permute-start | bytes 589832 | tf_op jit(solution)/shard_map/ppermute | solution.py:31
  93.5 12.9 %collective-permute-start.12 = (bf16[768,128]{1,0:T(8,128)(2,1)S(1)}, bf16[768,128]{1,0:T(8,128)(2,1)S(1)}, u32[]{:S(2)}, u32[]{:S(2)}) collective-permute-start(bf16[768,128]{1,0:T(8,128)(2,1)S(1)} %slice.4.refs_0_), channel_id=1, source_target_pairs={{0,4},{2,6},{4,0},{6,2},{1,5},{3,7},{5,1},{7,3},{8,12},{10,14},{12... | collective-permute-start | bytes 589832 | tf_op jit(solution)/shard_map/ppermute | solution.py:31
  96.0 12.0 %collective-permute-start.13 = (bf16[768,128]{1,0:T(8,128)(2,1)S(1)}, bf16[768,128]{1,0:T(8,128)(2,1)S(1)}, u32[]{:S(2)}, u32[]{:S(2)}) collective-permute-start(bf16[768,128]{1,0:T(8,128)(2,1)S(1)} %slice.4.refs_0_), channel_id=1, source_target_pairs={{0,6},{2,0},{4,2},{6,4},{1,7},{3,1},{5,3},{7,5},{8,14},{10,8},{12,... | collective-permute-start | bytes 589832 | tf_op jit(solution)/shard_map/ppermute | solution.py:31
  100.0 15.8 %all-to-all-start.1 = ((bf16[4,768,128]{2,1,0:T(8,128)(2,1)}), bf16[4,768,128]{2,1,0:T(8,128)(2,1)S(1)}, u32[]{:S(2)}, u32[]{:S(2)}) async-start(bf16[4,768,128]{2,1,0:T(8,128)(2,1)} %bitcast.6), calls=%async_computation.1 | async-start | bytes 1572864 | tf_op jit(solution)/shard_map/all_to_all | solution.py:423
  108.6 0.9 copy-start.2
  109.6 0.9 copy-start.5
  117.8 28.0 %all-to-all-start.2 = ((bf16[32,8,1152]{2,1,0:T(8,128)(2,1)}), bf16[32,8,1152]{2,1,0:T(8,128)(2,1)S(1)}, u32[]{:S(2)}, u32[]{:S(2)}) async-start(bf16[32,8,1152]{2,1,0:T(8,128)(2,1)} %bitcast.9), calls=%async_computation.2 | async-start | bytes 1179648 | tf_op jit(solution)/shard_map/all_to_all | solution.py:448
  (6 other events, 4.6 us)
